TPU v7x, 32 devices: a whole 2x2x4 slice. The times are simulated.
32 devices in a mesh: blk: 8 (over y, x, core), fsdp: 4 (over z).
Axes of the slice: x: 2, y: 2, z: 4, core: 2. Of those that a mesh axis runs over, the one named last changes fastest.
Arguments:
- decoder_states: bfloat16 [2048, 4096], P('blk', 'fsdp'), may hold values from -10 to 10
- w_query: bfloat16 [4096, 4096], P('blk', 'fsdp'), may hold values from -0.09375 to 0.09375
- w_out_t: bfloat16 [4096, 4096], P('blk', 'fsdp'), may hold values from -0.1875 to 0.1875
- enc_keys: bfloat16 [2048, 4096], P('blk', 'fsdp'), may hold values from -80 to 80
- enc_values: bfloat16 [2048, 4096], P('blk', 'fsdp'), may hold values from -6 to 6
Outputs:
- attended: bfloat16 [2048, 4096], P(('blk', 'fsdp'))
All inputs are finite; a program needn't handle non-finite values.
Results may differ from a plain program's by a relative error of at most 0.0095.
Values may be sent and summed in bfloat16 or wider, within the bound.
No kernel may reach another device: no remote copies, remote signals or barrier semaphores. Data moves between devices by JAX's collectives and lax.ppermute only.
A program may use at most 128 MiB of HBM per device.

v0:
```python
import math

import jax
import jax.numpy as jnp
from jax import lax
from jax.sharding import PartitionSpec as P

HEAD_DIM = 64


def absorb(fold_state, query_heads, key_rows, value_rows):
    running_top, running_sum, weighted = fold_state
    local_heads = query_heads.shape[1]
    key_heads = key_rows.reshape(key_rows.shape[0], local_heads, HEAD_DIM)
    value_heads = value_rows.reshape(value_rows.shape[0], local_heads, HEAD_DIM)
    scores = jnp.einsum(
        "qhd,khd->hqk", query_heads, key_heads, preferred_element_type=jnp.float32
    ) * (1.0 / math.sqrt(HEAD_DIM))
    new_top = jnp.max(scores, axis=2)
    rescale = jnp.exp(running_top - new_top)
    probability = jnp.exp(scores - new_top[:, :, None])
    running_sum = running_sum * rescale + jnp.sum(probability, axis=2)
    weighted = weighted * rescale[:, :, None] + jnp.einsum(
        "hqk,khd->hqd",
        probability.astype(jnp.bfloat16),
        value_heads,
        preferred_element_type=jnp.float32,
    )
    return (new_top, running_sum, weighted)


def shards(decoder_states, w_query, w_out_t, enc_keys, enc_values):
    query_full = lax.all_gather(w_query, "blk", axis=0, tiled=True)
    row_count = decoder_states.shape[0]
    columns = query_full.shape[1]
    local_heads = columns // HEAD_DIM
    queries = jnp.dot(
        lax.all_gather(decoder_states, "fsdp", axis=1, tiled=True),
        query_full,
        preferred_element_type=jnp.float32,
    ).astype(jnp.bfloat16)
    start_state = (
        jnp.full((local_heads, row_count), -jnp.inf, jnp.float32),
        jnp.zeros((local_heads, row_count), jnp.float32),
        jnp.zeros((local_heads, row_count, HEAD_DIM), jnp.float32),
    )
    query_heads = queries.reshape(row_count, local_heads, HEAD_DIM)
    final_state = absorb(
        start_state,
        query_heads,
        lax.all_gather(enc_keys, "blk", axis=0, tiled=True),
        lax.all_gather(enc_values, "blk", axis=0, tiled=True),
    )
    context = final_state[2] / final_state[1][:, :, None]
    context = jnp.transpose(context, (1, 0, 2)).reshape(row_count, columns).astype(jnp.bfloat16)
    out_full = lax.all_gather(w_out_t, "blk", axis=0, tiled=True)
    return lax.psum_scatter(
        lax.dot_general(
            context, out_full, (((1,), (1,)), ((), ())), preferred_element_type=jnp.float32
        ),
        "fsdp",
        scatter_dimension=0,
        tiled=True,
    ).astype(jnp.bfloat16)


def solution(mesh):
    in_specs = (
        P("blk", "fsdp"),
        P("blk", "fsdp"),
        P("blk", "fsdp"),
        P("blk", "fsdp"),
        P("blk", "fsdp"),
    )
    out_specs = P(("blk", "fsdp"), None)
    return jax.shard_map(shards, mesh=mesh, in_specs=in_specs, out_specs=out_specs, check_vma=False)
```

profile of v0, /device:TPU:0, one launch (start us, length us, event | category | flops | bytes accessed | tf_op | source)
XLA Modules:
  0.0 339.5 jit_solution(10422449191895136661)
XLA Ops:
  6.5 0.0 all-gather.10.cloned.1.call-start
  6.5 0.7 all-gather.10.cloned.1.call-update
  7.3 0.0 all-gather.12.cloned.1.call-start
  7.3 0.7 all-gather.12.cloned.1.call-update
  8.0 0.0 all-gather.6.cloned.1.call-start
  8.1 0.7 all-gather.6.cloned.1.call-update
  8.7 0.0 all-gather.8.cloned.1.call-start
  8.8 0.5 all-gather.8.cloned.1.call-update
  9.3 0.0 all-gather.14.cloned.1.call-start
  9.4 0.5 all-gather.14.cloned.1.call-update
  9.9 0.0 reduce-scatter.2.cloned.1.call-start
  10.0 38.7 %all-gather.10.cloned.1.call-done = bf16[2048,1024]{1,0:T(8,128)(2,1)} async-done(((bf16[256,1024]{1,0:T(8,128)(2,1)}), bf16[2048,1024]{1,0:T(8,128)(2,1)}) %all-gather.10.cloned.1.call-update) | async-done | bytes 4194320 | tf_op jit(solution)/shard_map/all_gather | solution.py:51
  48.7 6.5 %copy.10 = bf16[2048,1024]{0,1:T(8,128)(2,1)} copy(bf16[2048,1024]{1,0:T(8,128)(2,1)} %all-gather.10.cloned.1.call-done) | data formatting | bytes 8388608 | tf_op jit(solution)/shard_map/all_gather | solution.py:51
  55.2 32.1 %all-gather.12.cloned.1.call-done = bf16[2048,1024]{1,0:T(8,128)(2,1)} async-done(((bf16[256,1024]{1,0:T(8,128)(2,1)}), bf16[2048,1024]{1,0:T(8,128)(2,1)}) %all-gather.12.cloned.1.call-update) | async-done | bytes 4194320 | tf_op jit(solution)/shard_map/all_gather | solution.py:52
  87.3 6.5 %copy.11 = bf16[2048,1024]{0,1:T(8,128)(2,1)} copy(bf16[2048,1024]{1,0:T(8,128)(2,1)} %all-gather.12.cloned.1.call-done) | data formatting | bytes 8388608 | tf_op jit(solution)/shard_map/all_gather | solution.py:52
  93.8 41.0 %all-gather.6.cloned.1.call-done = bf16[256,4096]{1,0:T(8,128)(2,1)} async-done(((bf16[256,1024]{1,0:T(8,128)(2,1)}), bf16[256,4096]{1,0:T(8,128)(2,1)}) %all-gather.6.cloned.1.call-update) | async-done | bytes 2097168 | tf_op jit(solution)/shard_map/all_gather | solution.py:38
  134.9 54.9 %all-gather.8.cloned.1.call-done = bf16[4096,1024]{1,0:T(8,128)(2,1)} async-done(((bf16[512,1024]{1,0:T(8,128)(2,1)}), bf16[4096,1024]{1,0:T(8,128)(2,1)}) %all-gather.8.cloned.1.call-update) | async-done | bytes 8388624 | tf_op jit(solution)/shard_map/all_gather | solution.py:33
  189.8 6.3 %convolution_convert_fusion = bf16[256,1024]{1,0:T(8,128)(2,1)S(1)} fusion(bf16[256,4096]{1,0:T(8,128)(2,1)} %all-gather.6.cloned.1.call-done, bf16[4096,1024]{1,0:T(8,128)(2,1)} %all-gather.8.cloned.1.call-done), kind=kOutput, calls=%fused_computation.7 | convolution fusion | flops 2147745792 | bytes 11010048 | tf_op jit(solution)/shard_map/dot_general | solution.py:37
  196.1 0.2 copy.9
  196.3 15.6 %multiply_reduce_fusion = (f32[16,256]{1,0:T(8,128)S(1)}, f32[16,256,2048]{2,1,0:T(8,128)}) fusion(bf16[256,16,64]{0,2,1:T(8,128)(2,1)S(1)} %bitcast.25, bf16[2048,16,64]{0,2,1:T(8,128)(2,1)} %bitcast.23), kind=kOutput, calls=%fused_computation.1 | convolution fusion | flops 1090514944 | bytes 38289408 | tf_op jit(solution)/shard_map/qhd,khd->hqk/dot_general | solution.py:16
  212.0 15.1 %fusion = f32[16,256]{1,0:T(8,128)S(1)} fusion(f32[16,256,2048]{2,1,0:T(8,128)} %get-tuple-element.6, f32[16,256]{1,0:T(8,128)S(1)} %get-tuple-element.5), kind=kLoop, calls=%fused_computation.2 | loop fusion | flops 25161728 | bytes 33587200 | tf_op jit(solution)/shard_map/reduce_sum | solution.py:22
  227.1 15.7 %divide_convert_fusion = bf16[256,16,64]{0,2,1:T(8,128)(2,1)S(1)} fusion(bf16[2048,16,64]{0,2,1:T(8,128)(2,1)} %bitcast.24, f32[16,256,2048]{2,1,0:T(8,128)} %get-tuple-element.6, f32[16,256]{1,0:T(8,128)S(1)} %get-tuple-element.5, f32[256,16]{0,1:T(8,128)S(1)} %bitcast_add_fusion, f32[256,16]{0,1:T(8,128)S(1)} %multiply_bitcast_fusion), kind=kOutput, calls=%fused_computation.8 | convolution fusion | flops 1099694080 | bytes 38322176 | tf_op jit(solution)/shard_map/hqk,khd->hqd/dot_general | solution.py:23
  242.8 3.1 all-gather.14.cloned.1.call-done
  245.9 7.7 %fusion.13 = f32[256,4096]{1,0:T(8,128)} fusion(bf16[256,1024]{0,1:T(8,128)(2,1)S(1)} %bitcast.26, bf16[4096,1024]{1,0:T(8,128)(2,1)} %all-gather.14.cloned.1.call-done), kind=kOutput, calls=%fused_computation.12 | convolution fusion | flops 2147483648 | bytes 13107200 | tf_op jit(solution)/shard_map/dot_general | solution.py:58
  253.6 0.0 reduce-scatter.2.cloned.1.call-update
  253.7 76.9 %reduce-scatter.2.cloned.1.call-done = f32[64,4096]{1,0:T(8,128)} async-done(((f32[256,4096]{1,0:T(8,128)}), f32[64,4096]{1,0:T(8,128)}) %reduce-scatter.2.cloned.1.call-update) | async-done | bytes 1048592 | tf_op jit(solution)/shard_map/reduce_scatter | solution.py:57
  330.6 2.1 convert_element_type.19
  (2 shorter events, 0.0 us)
Async XLA Ops:
  6.5 42.2 %all-gather.10.cloned.1.call-start = ((), (), s32[]{:S(2)}) async-start(), calls=%async_computation.3 | async-start | bytes 4718592 | tf_op jit(solution)/shard_map/all_gather | solution.py:51
  7.3 80.1 %all-gather.12.cloned.1.call-start = ((), (), s32[]{:S(2)}) async-start(), calls=%async_computation.4 | async-start | bytes 4718592 | tf_op jit(solution)/shard_map/all_gather | solution.py:52
  8.0 126.9 %all-gather.6.cloned.1.call-start = ((), (), s32[]{:S(2)}) async-start(), calls=%async_computation.1 | async-start | bytes 2621440 | tf_op jit(solution)/shard_map/all_gather | solution.py:38
  8.7 181.0 %all-gather.8.cloned.1.call-start = ((), (), s32[]{:S(2)}) async-start(), calls=%async_computation.2 | async-start | bytes 9437184 | tf_op jit(solution)/shard_map/all_gather | solution.py:33
  9.3 236.6 %all-gather.14.cloned.1.call-start = ((), (), s32[]{:S(2)}) async-start(), calls=%async_computation.5 | async-start | bytes 9437184 | tf_op jit(solution)/shard_map/all_gather | solution.py:56
  9.9 320.7 %reduce-scatter.2.cloned.1.call-start = ((), (), s32[]{:S(2)}) async-start(), calls=%async_computation.6 | async-start | bytes 5242880 | tf_op jit(solution)/shard_map/reduce_scatter | solution.py:57
Sparse Core Ops, SparseCore 0:
  9.2 39.4 all-gather.9
  50.6 36.7 all-gather.11
  88.9 45.9 all-gather.5
  136.6 53.0 all-gather.7
  191.5 54.3 all-gather.13
  253.8 76.7 reduce-scatter.1
where the time goes:
time: 340 us
  waiting for transfers between devices  250 us (74%)
  matrix products  45.4 us (13%)
  other arithmetic  17.2 us (5%)
  between operations  13.5 us (4%)
  local copies, waits for them, and re-layouts  13.2 us (4%)
    reduce_scatter x1, waiting for transfers between devices, shards(): lax.psum_scatter(lax.dot_general(context, out_full, (((1,), (1,)), ((), (...  76.9 us
    all_gather x1, waiting for transfers between devices, shards(): query_full = lax.all_gather(w_query, 'blk', axis=0, tiled=True)  54.9 us
    all_gather x1, waiting for transfers between devices, shards(): lax.all_gather(decoder_states, 'fsdp', axis=1, tiled=True)  41 us
    all_gather x1, waiting for transfers between devices, shards(): lax.all_gather(enc_keys, 'blk', axis=0, tiled=True)  38.7 us
    all_gather x1, waiting for transfers between devices, shards(): lax.all_gather(enc_values, 'blk', axis=0, tiled=True)  32.1 us
    dot_general x1, matrix products, absorb(): jnp.einsum('hqk,khd->hqd', probability.astype(jnp.bfloat16), value_heads,...  15.7 us
    dot_general x1, matrix products, absorb(): jnp.einsum('qhd,khd->hqk', query_heads, key_heads, preferred_element_type...  15.6 us
    reduce_sum x1, other arithmetic, absorb(): running_sum = running_sum * rescale + jnp.sum(probability, axis=2)  15.1 us
  transfers between devices with their start and end apart: 6, of which 6 were waited for; matrix products, arithmetic and copies ran while one was open for 19% of the time, Pallas kernels for 0%

commit v1 on v0

--- a/solution.py
+++ b/solution.py
@@ -3,9 +3,13 @@
 import jax
 import jax.numpy as jnp
 from jax import lax
+from jax.experimental import pallas as pl
+from jax.experimental.pallas import tpu as pltpu
 from jax.sharding import PartitionSpec as P
 
 HEAD_DIM = 64
+PAIR = 2 * HEAD_DIM
+VMEM = 60 * 1024 * 1024
 
 
 def absorb(fold_state, query_heads, key_rows, value_rows):
@@ -29,7 +33,7 @@
     return (new_top, running_sum, weighted)
 
 
-def shards(decoder_states, w_query, w_out_t, enc_keys, enc_values):
+def gathered_shards(decoder_states, w_query, w_out_t, enc_keys, enc_values):
     query_full = lax.all_gather(w_query, "blk", axis=0, tiled=True)
     row_count = decoder_states.shape[0]
     columns = query_full.shape[1]
@@ -64,6 +68,345 @@
     ).astype(jnp.bfloat16)
 
 
+CORE = [(b, b ^ 1) for b in range(8)]
+ALONG_X = [(b, b ^ 2) for b in range(8)]
+ALONG_Y = [(b, b ^ 4) for b in range(8)]
+
+
+def z_partner(step):
+    return [(z, z ^ step) for z in range(4)]
+
+
+def over_core(a):
+    return lax.ppermute(a, "blk", CORE)
+
+
+def over_x(a):
+    return lax.ppermute(a, "blk", ALONG_X)
+
+
+def over_y(a):
+    return lax.ppermute(a, "blk", ALONG_Y)
+
+
+def after(value, *earlier):
+    return lax.optimization_barrier((value,) + earlier)[0]
+
+
+def relay(from_x, from_y):
+    half = from_x.shape[0] // 2
+    return over_x(from_y[:half]), over_y(from_x[half:])
+
+
+def any_spec():
+    return pl.BlockSpec(memory_space=pl.ANY)
+
+
+def smem_spec():
+    return pl.BlockSpec(memory_space=pltpu.SMEM)
+
+
+def vmem_spec():
+    return pl.BlockSpec(memory_space=pltpu.VMEM)
+
+
+def project_queries(place, states, weights):
+    rows, depth = states[0].shape
+    columns = weights[0][3].shape[1]
+    shard = depth // 2
+    half = columns // 2
+    count = len(states) + len(weights)
+
+    def kernel(place_ref, *refs):
+        state_refs = refs[: len(states)]
+        weight_refs = refs[len(states) : count]
+        mine_ref, other_ref, state_s, weight_s, total, sems = refs[count:]
+        chip, core, plane = place_ref[0], place_ref[1], place_ref[2]
+        state_copies, weight_copies = [], {}
+        for step, ref in enumerate(state_refs):
+            copy = pltpu.make_async_copy(ref, state_s.at[plane ^ step], sems.at[step])
+            copy.start()
+            state_copies.append(copy)
+        for n, (ref, (chip_step, core_step, first, piece)) in enumerate(zip(weight_refs, weights)):
+            begin = pl.multiple_of((core ^ core_step) * shard + first, 16)
+            copy = pltpu.make_async_copy(
+                ref,
+                weight_s.at[chip ^ chip_step, pl.ds(begin, piece.shape[0])],
+                sems.at[len(states) + n],
+            )
+            copy.start()
+            weight_copies.setdefault(chip_step, []).append(copy)
+        for copy in state_copies:
+            copy.wait()
+        for chip_step in range(4):
+            for copy in weight_copies[chip_step]:
+                copy.wait()
+            part = jnp.dot(
+                state_s[chip ^ chip_step],
+                weight_s[chip ^ chip_step],
+                preferred_element_type=jnp.float32,
+            )
+            total[...] = part if chip_step == 0 else total[...] + part
+        factor = 1.0 / math.sqrt(HEAD_DIM)
+        for ref, which in ((mine_ref, core), (other_ref, 1 - core)):
+            begin = pl.multiple_of(which * half, half)
+            queries = total[:, pl.ds(begin, half)].astype(jnp.bfloat16)
+            ref[...] = (queries.astype(jnp.float32) * factor).astype(jnp.bfloat16)
+
+    shape = jax.ShapeDtypeStruct((rows, half), jnp.bfloat16)
+    return pl.pallas_call(
+        kernel,
+        out_shape=(shape, shape),
+        in_specs=[smem_spec()] + [any_spec()] * count,
+        out_specs=(vmem_spec(), vmem_spec()),
+        scratch_shapes=[
+            pltpu.VMEM((4, rows, depth), jnp.bfloat16),
+            pltpu.VMEM((4, depth, columns), jnp.bfloat16),
+            pltpu.VMEM((rows, columns), jnp.float32),
+            pltpu.SemaphoreType.DMA((count,)),
+        ],
+        compiler_params=pltpu.CompilerParams(vmem_limit_bytes=VMEM),
+        cost_estimate=pl.CostEstimate(
+            flops=2 * rows * 4 * depth * columns,
+            bytes_accessed=2 * 4 * depth * (rows + columns),
+            transcendentals=0,
+        ),
+        name="project_queries",
+    )(place, *states, *[w[3] for w in weights])
+
+
+def pair_part(queries, keys, values):
+    rows = queries.shape[0]
+    first = lax.broadcasted_iota(jnp.int32, (rows, PAIR), 1) < HEAD_DIM
+    found = []
+    for head in range(2):
+        masked = jnp.where(first if head == 0 else jnp.logical_not(first), queries, 0)
+        scores = [
+            lax.dot_general(
+                masked, k, (((1,), (1,)), ((), ())), preferred_element_type=jnp.float32
+            )
+            for k in keys
+        ]
+        top = scores[0].max(axis=1, keepdims=True)
+        for s in scores[1:]:
+            top = jnp.maximum(top, s.max(axis=1, keepdims=True))
+        both = None
+        for s, v in zip(scores, values):
+            probability = jnp.exp(s - top).astype(jnp.bfloat16)
+            part = jnp.dot(probability, v, preferred_element_type=jnp.float32)
+            both = part if both is None else both + part
+        found.append((both[:, :PAIR], both[:, PAIR:], jnp.broadcast_to(top, (rows, PAIR))))
+    return [jnp.where(first, a, b) for a, b in zip(*found)]
+
+
+def attend(query_blocks, keys, values, before=None):
+    rows, columns = query_blocks[0].shape
+    pairs = columns // PAIR
+    blocks = len(query_blocks)
+    last = before is not None
+    held = [] if before is None else [a for block in before for a in block]
+    outs = blocks if last else 3 * blocks
+
+    def kernel(*refs):
+        refs = list(refs)
+        q_refs = [refs.pop(0) for _ in range(blocks)]
+        k_refs = [refs.pop(0) for _ in keys]
+        v_refs = [refs.pop(0) for _ in values]
+        held_refs = [refs.pop(0) for _ in held]
+        out_refs = [refs.pop(0) for _ in range(outs)]
+        ks = [r[...] for r in k_refs]
+        vs = [
+            jnp.concatenate([r[...], jnp.ones(r.shape, jnp.bfloat16)], axis=1) for r in v_refs
+        ]
+        for n in range(blocks):
+            weighted, sums, tops = pair_part(q_refs[n][...], ks, vs)
+            if last:
+                weighted_0, sums_0, tops_0 = (r[...] for r in held_refs[3 * n : 3 * n + 3])
+                top = jnp.maximum(tops, tops_0)
+                now, then = jnp.exp(tops - top), jnp.exp(tops_0 - top)
+                weighted = weighted * now + weighted_0 * then
+                sums = sums * now + sums_0 * then
+                out_refs[n][...] = (weighted / sums).astype(jnp.bfloat16)
+            else:
+                for ref, a in zip(out_refs[3 * n : 3 * n + 3], (weighted, sums, tops)):
+                    ref[...] = a
+
+    def spec(a):
+        return pl.BlockSpec((a.shape[0], PAIR), lambda p: (0, p))
+
+    args = list(query_blocks) + list(keys) + list(values) + held
+    out_shape = [
+        jax.ShapeDtypeStruct((rows, columns), jnp.bfloat16 if last else jnp.float32)
+    ] * outs
+    total_keys = sum(k.shape[0] for k in keys)
+    found = pl.pallas_call(
+        kernel,
+        grid=(pairs,),
+        out_shape=out_shape,
+        in_specs=[spec(a) for a in args],
+        out_specs=[spec(a) for a in out_shape],
+        compiler_params=pltpu.CompilerParams(vmem_limit_bytes=VMEM),
+        cost_estimate=pl.CostEstimate(
+            flops=2 * 2 * blocks * rows * total_keys * columns * 4,
+            bytes_accessed=sum(a.size * a.dtype.itemsize for a in args),
+            transcendentals=blocks * rows * total_keys * (columns // HEAD_DIM),
+        ),
+        name="attend_last" if last else "attend_first",
+    )(*args)
+    if last:
+        return found
+    return [found[3 * n : 3 * n + 3] for n in range(blocks)]
+
+
+def project_out(place, mine, other, weights):
+    rows, half = mine.shape
+    quarter = rows // 4
+    width = sum(w.shape[0] for w in weights)
+
+    def kernel(place_ref, mine_ref, other_ref, *refs):
+        weight_refs = refs[: len(weights)]
+        outs = refs[len(weights) : len(weights) + 4]
+        context = refs[-1]
+        core, plane = place_ref[1], place_ref[2]
+        for step in range(4):
+            begin = pl.multiple_of((plane ^ step) * quarter, quarter)
+            here = slice(step * quarter, (step + 1) * quarter)
+            for ref, which in ((mine_ref, core), (other_ref, 1 - core)):
+                lanes = pl.ds(pl.multiple_of(which * half, half), half)
+                context[here, lanes] = ref[pl.ds(begin, quarter), :]
+        at = 0
+        for ref in weight_refs:
+            part = lax.dot_general(
+                context[...],
+                ref[...],
+                (((1,), (1,)), ((), ())),
+                preferred_element_type=jnp.float32,
+            )
+            for step in range(4):
+                outs[step][:, at : at + ref.shape[0]] = part[
+                    step * quarter : (step + 1) * quarter
+                ].astype(outs[step].dtype)
+            at += ref.shape[0]
+
+    return pl.pallas_call(
+        kernel,
+        out_shape=[
+            jax.ShapeDtypeStruct((quarter, width), jnp.float32 if step == 0 else jnp.bfloat16)
+            for step in range(4)
+        ],
+        in_specs=[smem_spec()] + [vmem_spec()] * (2 + len(weights)),
+        out_specs=[vmem_spec()] * 4,
+        scratch_shapes=[pltpu.VMEM((rows, 2 * half), jnp.bfloat16)],
+        compiler_params=pltpu.CompilerParams(vmem_limit_bytes=VMEM),
+        cost_estimate=pl.CostEstimate(
+            flops=2 * rows * 2 * half * width,
+            bytes_accessed=2 * width * 2 * half,
+            transcendentals=0,
+        ),
+        name="project_out",
+    )(place, mine, other, *weights)
+
+
+def add_up(place, groups, shard):
+    rows = groups[0][1].shape[0]
+
+    def kernel(place_ref, *refs):
+        out_ref = refs[-1]
+        chip, core = place_ref[0], place_ref[1]
+        for n, (spots, *_) in enumerate(groups):
+            own, *received = refs[4 * n : 4 * n + 4]
+            at = 0
+            for chip_step, core_step, first, size in spots:
+                total = own[:, at : at + size]
+                for ref in received:
+                    total = total + ref[:, at : at + size].astype(jnp.float32)
+                begin = ((chip ^ chip_step) * 2 + (core ^ core_step)) * shard + first
+                out_ref[:, pl.ds(pl.multiple_of(begin, 128), size)] = total.astype(jnp.bfloat16)
+                at += size
+
+    args = [a for group in groups for a in group[1:]]
+    return pl.pallas_call(
+        kernel,
+        out_shape=jax.ShapeDtypeStruct((rows, 8 * shard), jnp.bfloat16),
+        in_specs=[smem_spec()] + [vmem_spec()] * len(args),
+        out_specs=vmem_spec(),
+        compiler_params=pltpu.CompilerParams(vmem_limit_bytes=VMEM),
+        cost_estimate=pl.CostEstimate(
+            flops=4 * rows * 8 * shard, bytes_accessed=12 * rows * 8 * shard, transcendentals=0
+        ),
+        name="add_up",
+    )(place, *args)
+
+
+def plane_shards(decoder_states, w_query, w_out_t, enc_keys, enc_values):
+    block, plane = lax.axis_index("blk"), lax.axis_index("fsdp")
+    chip, core = block // 2, block % 2
+    place = jnp.stack([chip, core, plane]).astype(jnp.int32)
+    shard = w_query.shape[0]
+    half_shard = shard // 2
+    half = enc_keys.shape[1] // 2
+
+    states = [decoder_states] + [
+        lax.ppermute(decoder_states, "fsdp", z_partner(step)) for step in (1, 2, 3)
+    ]
+    query_x, query_y = over_x(w_query), over_y(w_query)
+
+    def columns(a, which):
+        return lax.dynamic_slice_in_dim(a, which * half, half, 1)
+
+    swapped = over_core(
+        jnp.concatenate([columns(enc_keys, 1 - core), columns(enc_values, 1 - core)], axis=0)
+    )
+    row_count = enc_keys.shape[0]
+    keys = jnp.concatenate([columns(enc_keys, core), swapped[:row_count]], axis=0)
+    values = jnp.concatenate([columns(enc_values, core), swapped[row_count:]], axis=0)
+    keys_x, keys_y = over_x(keys), over_y(keys)
+
+    query_top, query_bottom = relay(query_x, query_y)
+    values = after(values, query_x, query_y)
+    values_x, values_y = over_x(values), over_y(values)
+    keys_top, keys_bottom = relay(keys_x, keys_y)
+    values_top, values_bottom = relay(values_x, values_y)
+
+    out_own = after(w_out_t, keys_x, keys_y)
+    out_x, out_y = over_x(out_own), over_y(out_own)
+    out_top, out_bottom = relay(out_x, out_y)
+
+    def with_sibling(chip_step, first, piece):
+        return [(chip_step, 0, first, piece), (chip_step, 1, first, over_core(piece))]
+
+    query_pieces = (
+        with_sibling(0, 0, w_query)
+        + with_sibling(1, 0, query_x)
+        + with_sibling(2, 0, query_y)
+        + with_sibling(3, 0, query_top)
+        + with_sibling(3, half_shard, query_bottom)
+    )
+    out_groups = [
+        with_sibling(0, 0, w_out_t),
+        with_sibling(1, 0, out_x) + with_sibling(2, 0, out_y),
+        with_sibling(3, 0, out_top) + with_sibling(3, half_shard, out_bottom),
+    ]
+
+    queries, queries_other = project_queries(place, states, query_pieces)
+    query_blocks = [queries, over_core(queries_other)]
+    before = attend(query_blocks, [keys, keys_x, keys_y], [values, values_x, values_y])
+    context, context_other = attend(
+        query_blocks, [keys_top, keys_bottom], [values_top, values_bottom], before
+    )
+    context_back = over_core(context_other)
+
+    sums = []
+    for group in out_groups:
+        own, *sent = project_out(place, context, context_back, [piece for *_, piece in group])
+        received = [
+            lax.ppermute(part, "fsdp", z_partner(step + 1)) for step, part in enumerate(sent)
+        ]
+        spots = [(a, b, first, piece.shape[0]) for a, b, first, piece in group]
+        sums.append((spots, own, *received))
+    return add_up(place, sums, shard)
+
+
 def solution(mesh):
     in_specs = (
         P("blk", "fsdp"),
@@ -73,4 +416,11 @@
         P("blk", "fsdp"),
     )
     out_specs = P(("blk", "fsdp"), None)
-    return jax.shard_map(shards, mesh=mesh, in_specs=in_specs, out_specs=out_specs, check_vma=False)
+    by_planes = mesh.shape["blk"] == 8 and mesh.shape["fsdp"] == 4
+    return jax.shard_map(
+        plane_shards if by_planes else gathered_shards,
+        mesh=mesh,
+        in_specs=in_specs,
+        out_specs=out_specs,
+        check_vma=False,
+    )

time: 340 us -> 208 us (0.61)
  waiting for transfers between devices: 250 us -> 113 us
  matrix products: 45.4 us -> 0 us
  starting transfers between devices: 0.19 us -> 43.1 us
  Pallas kernels: 0 us -> 38.8 us
  other arithmetic: 17.2 us -> 0.76 us
  between operations: 13.5 us -> 0.38 us
    all_gather x5 -> x0, waiting for transfers between devices: 170 us -> none  [the longest x1 54.9 us: shards(): query_full = lax.all_gather(w_query, 'blk', axis=0, tiled=True)]
    ppermute x0 -> x41, waiting for transfers between devices: none -> 113 us  [the longest x8 48.5 us: over_x(): return lax.ppermute(a, 'blk', ALONG_X)]
    reduce_scatter x1 -> x0, waiting for transfers between devices: 76.9 us -> none  [shards(): lax.psum_scatter(lax.dot_general(context, out_full, (((1,), (1,)), ((), (...]
    dot_general x4 -> x0, matrix products: 45.4 us -> none  [the longest x1 15.7 us: absorb(): jnp.einsum('hqk,khd->hqd', probability.astype(jnp.bfloat16), value_heads,...]
    ppermute x0 -> x41, starting transfers between devices: none -> 43.1 us  [the longest x9 14.5 us: plane_shards(): lax.ppermute(part, 'fsdp', z_partner(step + 1))]
    pallas_call x0 -> x7, Pallas kernels: none -> 38.8 us  [the longest x2 18.4 us: attend(): pl.pallas_call(kernel, grid=(pairs,), out_shape=out_shape, in_specs=[spec...]
    reduce_sum x1 -> x0, other arithmetic: 15.1 us -> none  [absorb(): running_sum = running_sum * rescale + jnp.sum(probability, axis=2)]
    all_gather x2 -> x0, local copies, waits for them, and re-layouts: 13 us -> none  [the longest x1 6.53 us: shards(): lax.all_gather(enc_keys, 'blk', axis=0, tiled=True)]
  transfers between devices with their start and end apart: 6 -> 41, of which waited for: 6 -> 13; matrix products, arithmetic and copies ran while one was open for 19% -> 3% of each run, Pallas kernels for 0% -> 17%
where the time goes in v1:
time: 208 us; the launch traced here: 206 us
  waiting for transfers between devices  113 us (54%)
  starting transfers between devices  43.1 us (21%)
  Pallas kernels  38.8 us (19%)
  local copies, waits for them, and re-layouts  9.93 us (5%)
    ppermute x8, waiting for transfers between devices, over_x(): return lax.ppermute(a, 'blk', ALONG_X)  48.5 us
    ppermute x9, waiting for transfers between devices, plane_shards(): lax.ppermute(part, 'fsdp', z_partner(step + 1))  29 us
    ppermute x3, waiting for transfers between devices, plane_shards(): lax.ppermute(decoder_states, 'fsdp', z_partner(step))  25.7 us
    pallas_call x2, Pallas kernels, attend(): pl.pallas_call(kernel, grid=(pairs,), out_shape=out_shape, in_specs=[spec...  18.4 us
    ppermute x9, starting transfers between devices, plane_shards(): lax.ppermute(part, 'fsdp', z_partner(step + 1))  14.5 us
    ppermute x8, starting transfers between devices, over_y(): return lax.ppermute(a, 'blk', ALONG_Y)  11.9 us
    pallas_call x3, Pallas kernels, project_out(): pl.pallas_call(kernel, out_shape=[jax.ShapeDtypeStruct((quarter, width),...  11.2 us
    ppermute x8, starting transfers between devices, over_x(): return lax.ppermute(a, 'blk', ALONG_X)  8.97 us
  transfers between devices with their start and end apart: 41, of which 13 were waited for; matrix products, arithmetic and copies ran while one was open for 3% of the time, Pallas kernels for 17%

profile of v1, /device:TPU:0, one launch (start us, length us, event | category | flops | bytes accessed | tf_op | source)
XLA Modules:
  0.0 206.2 jit_solution(2138766300593060586)
XLA Ops:
  0.0 2.9 %collective-permute-start.4 = (bf16[512,1024]{1,0:T(8,128)(2,1)}, bf16[512,1024]{1,0:T(8,128)(2,1)S(1)}, u32[]{:S(2)}, u32[]{:S(2)}) collective-permute-start(bf16[512,1024]{1,0:T(8,128)(2,1)} %refs_4_.1), channel_id=1, source_target_pairs={{0,8},{4,12},{8,0},{12,4},{16,24},{20,28},{24,16},{28,20},{1,9},{5... | collective-permute-start | bytes 3145736 | tf_op jit(solution)/shard_map/ppermute | solution.py:85
  2.9 1.6 collective-permute-start
  4.5 1.3 constant_dynamic-slice_fusion
  6.0 1.1 copy-done.5
  7.1 1.5 collective-permute-start.6
  8.6 7.9 %collective-permute-done.refs_1_ = bf16[256,1024]{1,0:T(8,128)(2,1)S(1)} collective-permute-done((bf16[256,1024]{1,0:T(8,128)(2,1)}, bf16[256,1024]{1,0:T(8,128)(2,1)S(1)}, u32[]{:S(2)}, u32[]{:S(2)}) %collective-permute-start) | collective-permute-done | bytes 524320 | tf_op jit(solution)/shard_map/ppermute | solution.py:350
  16.5 2.6 %collective-permute-start.1 = (bf16[256,1024]{1,0:T(8,128)(2,1)S(1)}, bf16[256,1024]{1,0:T(8,128)(2,1)S(1)}, u32[]{:S(2)}, u32[]{:S(2)}) collective-permute-start(bf16[256,1024]{1,0:T(8,128)(2,1)S(1)} %copy-done.9), channel_id=1, source_target_pairs={{0,2},{1,3},{2,0},{3,1},{4,6},{5,7},{6,4},{7,5},{8,10},{9,11},{10,... | collective-permute-start | bytes 1572872 | tf_op jit(solution)/shard_map/ppermute | solution.py:350
  19.1 1.3 collective-permute-start.2
  20.6 5.7 %collective-permute-done.4.refs_6_ = bf16[512,1024]{1,0:T(8,128)(2,1)S(1)} collective-permute-done((bf16[512,1024]{1,0:T(8,128)(2,1)}, bf16[512,1024]{1,0:T(8,128)(2,1)S(1)}, u32[]{:S(2)}, u32[]{:S(2)}) %collective-permute-start.4) | collective-permute-done | bytes 1048608 | tf_op jit(solution)/shard_map/ppermute | solution.py:85
  26.3 1.8 collective-permute-start.14
  28.1 5.2 %collective-permute-done.6.refs_8_ = bf16[512,1024]{1,0:T(8,128)(2,1)} collective-permute-done((bf16[512,1024]{1,0:T(8,128)(2,1)S(1)}, bf16[512,1024]{1,0:T(8,128)(2,1)}, u32[]{:S(2)}, u32[]{:S(2)}) %collective-permute-start.6) | collective-permute-done | bytes 1048608 | tf_op jit(solution)/shard_map/ppermute | solution.py:89
  33.3 1.5 collective-permute-start.10
  34.8 1.1 slice.40
  35.9 17.8 %collective-permute-done.1.refs_2_ = bf16[256,1024]{1,0:T(8,128)(2,1)S(1)} collective-permute-done((bf16[256,1024]{1,0:T(8,128)(2,1)S(1)}, bf16[256,1024]{1,0:T(8,128)(2,1)S(1)}, u32[]{:S(2)}, u32[]{:S(2)}) %collective-permute-start.1) | collective-permute-done | bytes 524320 | tf_op jit(solution)/shard_map/ppermute | solution.py:350
  54.2 1.5 collective-permute-start.8
  55.8 1.6 collective-permute-start.18
  57.4 0.8 collective-permute-start.20
  58.2 10.3 %collective-permute-done.16.refs_3_ = bf16[512,512]{1,0:T(8,128)(2,1)S(1)} collective-permute-done((bf16[512,512]{1,0:T(8,128)(2,1)S(1)}, bf16[512,512]{1,0:T(8,128)(2,1)S(1)}, u32[]{:S(2)}, u32[]{:S(2)}) %collective-permute-start.16) | collective-permute-done | bytes 524320 | tf_op jit(solution)/shard_map/ppermute | solution.py:85
  68.5 11.3 %collective-permute-done.8.refs_10_ = bf16[256,1024]{1,0:T(8,128)(2,1)} collective-permute-done((bf16[256,1024]{1,0:T(8,128)(2,1)S(1)}, bf16[256,1024]{1,0:T(8,128)(2,1)}, u32[]{:S(2)}, u32[]{:S(2)}) %collective-permute-start.8) | collective-permute-done | bytes 524320 | tf_op jit(solution)/shard_map/ppermute | solution.py:85
  79.9 1.6 collective-permute-start.29
  81.5 6.5 %collective-permute-done.20.refs_6_ = bf16[512,512]{1,0:T(8,128)(2,1)S(1)} collective-permute-done((bf16[512,512]{1,0:T(8,128)(2,1)S(1)}, bf16[512,512]{1,0:T(8,128)(2,1)S(1)}, u32[]{:S(2)}, u32[]{:S(2)}) %collective-permute-start.20) | collective-permute-done | bytes 524320 | tf_op jit(solution)/shard_map/ppermute | solution.py:85
  88.8 0.8 copy-done.14
  89.7 1.1 slice.43
  90.7 1.2 collective-permute-done.9.refs_11_
  91.9 1.2 collective-permute-start.15
  95.3 1.6 collective-permute-start.17
  96.8 0.8 collective-permute-start.19
  97.6 6.4 %project_queries.1 = (bf16[256,512]{1,0:T(8,128)(2,1)}, bf16[256,512]{1,0:T(8,128)(2,1)}) custom-call(s32[3]{0:T(128)} %pad_add_fusion.place_ref, bf16[256,1024]{1,0:T(8,128)(2,1)} %refs_0_.2, bf16[256,1024]{1,0:T(8,128)(2,1)} %copy-done.10, bf16[256,1024]{1,0:T(8,128)(2,1)} %copy-done.11, bf16[256,1024]{1,0:T(8,128)(2,1)} %copy-done.12, ...), custom_call_target="tpu_custom_call" | custom-call | flops 2147483648 | bytes 10485760 | tf_op jit(solution)/shard_map/project_queries/pallas_call | solution.py:157
  104.0 14.6 %collective-permute-done.15.refs_2_ = bf16[256,512]{1,0:T(8,128)(2,1)S(1)} collective-permute-done((bf16[256,512]{1,0:T(8,128)(2,1)S(1)}, bf16[256,512]{1,0:T(8,128)(2,1)S(1)}, u32[]{:S(2)}, u32[]{:S(2)}) %collective-permute-start.15) | collective-permute-done | bytes 262176 | tf_op jit(solution)/shard_map/ppermute | solution.py:85
  118.6 1.5 collective-permute-start.21
  120.7 0.9 slice.48
  122.3 0.8 collective-permute-start.36
  123.1 2.2 %collective-permute-done.21.refs_5_ = bf16[256,512]{1,0:T(8,128)(2,1)} collective-permute-done((bf16[256,512]{1,0:T(8,128)(2,1)S(1)}, bf16[256,512]{1,0:T(8,128)(2,1)}, u32[]{:S(2)}, u32[]{:S(2)}) %collective-permute-start.21) | collective-permute-done | bytes 262176 | tf_op jit(solution)/shard_map/ppermute | solution.py:89
  126.0 11.9 %attend_first.1 = (f32[256,512]{1,0:T(8,128)}, f32[256,512]{1,0:T(8,128)}, f32[256,512]{1,0:T(8,128)}, f32[256,512]{1,0:T(8,128)}, f32[256,512]{1,0:T(8,128)}, /*index=5*/f32[256,512]{1,0:T(8,128)}) custom-call(bf16[256,512]{1,0:T(8,128)(2,1)} %get-tuple-element.29.refs_0_, bf16[256,512]{1,0:T(8,128)(2,1)} %copy-done.34, bf16[512,512]{1,0:T(8,128)(2,1)} %copy-done.7, ...), custom_call_target="tpu_custom_call" | custom-call | flops 6442450944 | bytes 3670016 | tf_op jit(solution)/shard_map/attend_first/pallas_call | solution.py:242
  138.6 6.5 %attend_last.1 = (bf16[256,512]{1,0:T(8,128)(2,1)}, bf16[256,512]{1,0:T(8,128)(2,1)}) custom-call(bf16[256,512]{1,0:T(8,128)(2,1)} %get-tuple-element.29.refs_0_, bf16[256,512]{1,0:T(8,128)(2,1)} %copy-done.34, bf16[256,512]{1,0:T(8,128)(2,1)} %copy-done.31, bf16[256,512]{1,0:T(8,128)(2,1)} %copy-done.32, bf16[256,512]{1,0:T(8,128)(2,1)} %copy-done.33, ...), custom_call_target="tpu_custom_call" | custom-call | flops 2147483648 | bytes 4718592 | tf_op jit(solution)/shard_map/attend_last/pallas_call | solution.py:242
  145.6 1.4 collective-permute-done.22.other_ref
  147.7 3.3 %project_out.3 = (f32[64,1024]{1,0:T(8,128)}, bf16[64,1024]{1,0:T(8,128)(2,1)}, bf16[64,1024]{1,0:T(8,128)(2,1)}, bf16[64,1024]{1,0:T(8,128)(2,1)}) custom-call(s32[3]{0:T(128)} %pad_add_fusion.place_ref, bf16[256,512]{1,0:T(8,128)(2,1)} %get-tuple-element.38.mine_ref, bf16[256,512]{1,0:T(8,128)(2,1)} %copy-done.2, bf16[512,1024]{1,0:T(8,128)(2,1)} %refs_0_.3, ...), custom_call_target="tpu_custom_call" | custom-call | flops 536870912 | bytes 2097152 | tf_op jit(solution)/shard_map/project_out/pallas_call | solution.py:291
  151.0 2.8 %collective-permute-start.24 = (bf16[64,1024]{1,0:T(8,128)(2,1)}, bf16[64,1024]{1,0:T(8,128)(2,1)S(1)}, u32[]{:S(2)}, u32[]{:S(2)}) collective-permute-start(bf16[64,1024]{1,0:T(8,128)(2,1)} %get-tuple-element.41), channel_id=1, source_target_pairs={{0,1},{1,0},{2,3},{3,2},{4,5},{5,4},{6,7},{7,6},{8,9},{9,8},{10,11... | collective-permute-start | bytes 393224 | tf_op jit(solution)/shard_map/ppermute | solution.py:403
  153.8 3.4 %collective-permute-start.25 = (bf16[64,1024]{1,0:T(8,128)(2,1)}, bf16[64,1024]{1,0:T(8,128)(2,1)S(1)}, u32[]{:S(2)}, u32[]{:S(2)}) collective-permute-start(bf16[64,1024]{1,0:T(8,128)(2,1)} %get-tuple-element.42), channel_id=1, source_target_pairs={{0,2},{1,3},{2,0},{3,1},{4,6},{5,7},{6,4},{7,5},{8,10},{9,11},{10,... | collective-permute-start | bytes 393224 | tf_op jit(solution)/shard_map/ppermute | solution.py:403
  157.2 4.7 %project_out.4 = (f32[64,2048]{1,0:T(8,128)}, bf16[64,2048]{1,0:T(8,128)(2,1)}, bf16[64,2048]{1,0:T(8,128)(2,1)}, bf16[64,2048]{1,0:T(8,128)(2,1)}) custom-call(s32[3]{0:T(128)} %pad_add_fusion.place_ref, bf16[256,512]{1,0:T(8,128)(2,1)} %get-tuple-element.38.mine_ref, bf16[256,512]{1,0:T(8,128)(2,1)} %copy-done.2, bf16[512,1024]{1,0:T(8,128)(2,1)} %copy-done.1, ...), custom_call_target="tpu_custom_call" | custom-call | flops 1073741824 | bytes 4194304 | tf_op jit(solution)/shard_map/project_out/pallas_call | solution.py:291
  162.6 3.3 %project_out.5 = (f32[64,1024]{1,0:T(8,128)}, bf16[64,1024]{1,0:T(8,128)(2,1)}, bf16[64,1024]{1,0:T(8,128)(2,1)}, bf16[64,1024]{1,0:T(8,128)(2,1)}) custom-call(s32[3]{0:T(128)} %pad_add_fusion.place_ref, bf16[256,512]{1,0:T(8,128)(2,1)} %get-tuple-element.38.mine_ref, bf16[256,512]{1,0:T(8,128)(2,1)} %copy-done.2, ...), custom_call_target="tpu_custom_call" | custom-call | flops 536870912 | bytes 2097152 | tf_op jit(solution)/shard_map/project_out/pallas_call | solution.py:291
  165.9 1.4 collective-permute-start.38
  167.3 2.4 %collective-permute-start.32 = (bf16[64,2048]{1,0:T(8,128)(2,1)S(1)}, bf16[64,2048]{1,0:T(8,128)(2,1)S(1)}, u32[]{:S(2)}, u32[]{:S(2)}) collective-permute-start(bf16[64,2048]{1,0:T(8,128)(2,1)S(1)} %copy-done.36), channel_id=1, source_target_pairs={{0,2},{1,3},{2,0},{3,1},{4,6},{5,7},{6,4},{7,5},{8,10},{9,11},{10,... | collective-permute-start | bytes 786440 | tf_op jit(solution)/shard_map/ppermute | solution.py:403
  169.8 1.5 collective-permute-start.33
  171.3 2.0 collective-permute-start.39
  173.2 6.7 %collective-permute-done.38.refs_9_ = bf16[64,1024]{1,0:T(8,128)(2,1)S(1)} collective-permute-done((bf16[64,1024]{1,0:T(8,128)(2,1)}, bf16[64,1024]{1,0:T(8,128)(2,1)S(1)}, u32[]{:S(2)}, u32[]{:S(2)}) %collective-permute-start.38) | collective-permute-done | bytes 131104 | tf_op jit(solution)/shard_map/ppermute | solution.py:403
  180.2 22.3 %collective-permute-done.39.refs_10_ = bf16[64,1024]{1,0:T(8,128)(2,1)S(1)} collective-permute-done((bf16[64,1024]{1,0:T(8,128)(2,1)}, bf16[64,1024]{1,0:T(8,128)(2,1)S(1)}, u32[]{:S(2)}, u32[]{:S(2)}) %collective-permute-start.39) | collective-permute-done | bytes 131104 | tf_op jit(solution)/shard_map/ppermute | solution.py:403
  203.5 2.7 %add_up.1 = bf16[64,4096]{1,0:T(8,128)(2,1)} custom-call(s32[3]{0:T(128)} %pad_add_fusion.place_ref, f32[64,1024]{1,0:T(8,128)} %get-tuple-element.40.refs_0_, bf16[64,1024]{1,0:T(8,128)(2,1)} %copy-done.25, bf16[64,1024]{1,0:T(8,128)(2,1)} %copy-done.26, bf16[64,1024]{1,0:T(8,128)(2,1)} %copy-done.27, f32[64,2048]{1,0:T(8,128)} %get-tuple-element.45.refs_4_, ...), custom_call_target="tpu_custom_call" | custom-call | flops 1048576 | bytes 3145728 | tf_op jit(solution)/shard_map/add_up/pallas_call | solution.py:328
  (129 shorter events, 9.4 us)
Async XLA Ops:
  0.0 26.3 %collective-permute-start.4 = (bf16[512,1024]{1,0:T(8,128)(2,1)}, bf16[512,1024]{1,0:T(8,128)(2,1)S(1)}, u32[]{:S(2)}, u32[]{:S(2)}) collective-permute-start(bf16[512,1024]{1,0:T(8,128)(2,1)} %refs_4_.1), channel_id=1, source_target_pairs={{0,8},{4,12},{8,0},{12,4},{16,24},{20,28},{24,16},{28,20},{1,9},{5... | collective-permute-start | bytes 3145736 | tf_op jit(solution)/shard_map/ppermute | solution.py:85
  2.9 13.6 %collective-permute-start = (bf16[256,1024]{1,0:T(8,128)(2,1)}, bf16[256,1024]{1,0:T(8,128)(2,1)S(1)}, u32[]{:S(2)}, u32[]{:S(2)}) collective-permute-start(bf16[256,1024]{1,0:T(8,128)(2,1)} %refs_0_.2), channel_id=1, source_target_pairs={{0,1},{1,0},{2,3},{3,2},{4,5},{5,4},{6,7},{7,6},{8,9},{9,8},{10,11... | collective-permute-start | bytes 1572872 | tf_op jit(solution)/shard_map/ppermute | solution.py:350
  5.9 13.2 %collective-permute-start.13 = (bf16[512,512]{1,0:T(8,128)(2,1)S(1)}, bf16[512,512]{1,0:T(8,128)(2,1)S(1)}, u32[]{:S(2)}, u32[]{:S(2)}) collective-permute-start(bf16[512,512]{1,0:T(8,128)(2,1)S(1)} %pad_maximum_fusion), channel_id=1, source_target_pairs={{0,4},{4,0},{8,12},{12,8},{16,20},{20,16},{24,28},{28,24},{1,5},{5... | collective-permute-start | bytes 1572872 | tf_op jit(solution)/shard_map/ppermute | solution.py:81
  7.1 26.2 %collective-permute-start.6 = (bf16[512,1024]{1,0:T(8,128)(2,1)S(1)}, bf16[512,1024]{1,0:T(8,128)(2,1)}, u32[]{:S(2)}, u32[]{:S(2)}) collective-permute-start(bf16[512,1024]{1,0:T(8,128)(2,1)S(1)} %copy-done.5), channel_id=1, source_target_pairs={{0,16},{4,20},{8,24},{12,28},{16,0},{20,4},{24,8},{28,12},{1,17},{... | collective-permute-start | bytes 3145736 | tf_op jit(solution)/shard_map/ppermute | solution.py:89
  8.6 47.2 %collective-permute-start.3 = (bf16[512,1024]{1,0:T(8,128)(2,1)S(1)}, bf16[512,1024]{1,0:T(8,128)(2,1)S(1)}, u32[]{:S(2)}, u32[]{:S(2)}) collective-permute-start(bf16[512,1024]{1,0:T(8,128)(2,1)S(1)} %copy-done.5), channel_id=1, source_target_pairs={{0,4},{4,0},{8,12},{12,8},{16,20},{20,16},{24,28},{28,24},{1,5},{5... | collective-permute-start | bytes 3145736 | tf_op jit(solution)/shard_map/ppermute | solution.py:81
  16.5 37.1 %collective-permute-start.1 = (bf16[256,1024]{1,0:T(8,128)(2,1)S(1)}, bf16[256,1024]{1,0:T(8,128)(2,1)S(1)}, u32[]{:S(2)}, u32[]{:S(2)}) collective-permute-start(bf16[256,1024]{1,0:T(8,128)(2,1)S(1)} %copy-done.9), channel_id=1, source_target_pairs={{0,2},{1,3},{2,0},{3,1},{4,6},{5,7},{6,4},{7,5},{8,10},{9,11},{10,... | collective-permute-start | bytes 1572872 | tf_op jit(solution)/shard_map/ppermute | solution.py:350
  19.1 35.1 %collective-permute-start.2 = (bf16[256,1024]{1,0:T(8,128)(2,1)S(1)}, bf16[256,1024]{1,0:T(8,128)(2,1)S(1)}, u32[]{:S(2)}, u32[]{:S(2)}) collective-permute-start(bf16[256,1024]{1,0:T(8,128)(2,1)S(1)} %copy-done.9), channel_id=1, source_target_pairs={{0,3},{1,2},{2,1},{3,0},{4,7},{5,6},{6,5},{7,4},{8,11},{9,10},{10,... | collective-permute-start | bytes 1572872 | tf_op jit(solution)/shard_map/ppermute | solution.py:350
  20.6 33.1 %copy-start.7 = (bf16[512,512]{1,0:T(8,128)(2,1)}, bf16[512,512]{1,0:T(8,128)(2,1)S(1)}, u32[]{:S(2)}) copy-start(bf16[512,512]{1,0:T(8,128)(2,1)S(1)} %pad_maximum_fusion.1.refs_2_) | copy-start | bytes 1572868
  26.3 42.2 %copy-start.3 = (bf16[512,1024]{1,0:T(8,128)(2,1)}, bf16[512,1024]{1,0:T(8,128)(2,1)S(1)}, u32[]{:S(2)}) copy-start(bf16[512,1024]{1,0:T(8,128)(2,1)S(1)} %collective-permute-done.4.refs_6_) | copy-start | bytes 3145732
  26.3 31.1 %collective-permute-start.14 = (bf16[512,512]{1,0:T(8,128)(2,1)S(1)}, bf16[512,512]{1,0:T(8,128)(2,1)S(1)}, u32[]{:S(2)}, u32[]{:S(2)}) collective-permute-start(bf16[512,512]{1,0:T(8,128)(2,1)S(1)} %pad_maximum_fusion.1.refs_2_), channel_id=1, source_target_pairs={{0,16},{4,20},{8,24},{12,28},{16,0},{20,4},{24,8},{28,12},{1,17},{... | collective-permute-start | bytes 1572872 | tf_op jit(solution)/shard_map/ppermute | solution.py:89
  33.3 24.9 %collective-permute-start.10 = (bf16[256,1024]{1,0:T(8,128)(2,1)S(1)}, bf16[256,1024]{1,0:T(8,128)(2,1)S(1)}, u32[]{:S(2)}, u32[]{:S(2)}) collective-permute-start(bf16[256,1024]{1,0:T(8,128)(2,1)S(1)} %slice.41), channel_id=1, source_target_pairs={{0,16},{4,20},{8,24},{12,28},{16,0},{20,4},{24,8},{28,12},{1,17},{... | collective-permute-start | bytes 1572872 | tf_op jit(solution)/shard_map/ppermute | solution.py:89
  53.7 14.9 %collective-permute-start.16 = (bf16[512,512]{1,0:T(8,128)(2,1)S(1)}, bf16[512,512]{1,0:T(8,128)(2,1)S(1)}, u32[]{:S(2)}, u32[]{:S(2)}) collective-permute-start(bf16[512,512]{1,0:T(8,128)(2,1)S(1)} %pad_maximum_fusion.1.refs_2_), channel_id=1, source_target_pairs={{0,8},{4,12},{8,0},{12,4},{16,24},{20,28},{24,16},{28,20},{1,9},{5... | collective-permute-start | bytes 1572872 | tf_op jit(solution)/shard_map/ppermute | solution.py:85
  54.2 25.7 %collective-permute-start.8 = (bf16[256,1024]{1,0:T(8,128)(2,1)S(1)}, bf16[256,1024]{1,0:T(8,128)(2,1)}, u32[]{:S(2)}, u32[]{:S(2)}) collective-permute-start(bf16[256,1024]{1,0:T(8,128)(2,1)S(1)} %slice.40), channel_id=1, source_target_pairs={{0,8},{4,12},{8,0},{12,4},{16,24},{20,28},{24,16},{28,20},{1,9},{5... | collective-permute-start | bytes 1572872 | tf_op jit(solution)/shard_map/ppermute | solution.py:85
  55.8 24.1 %collective-permute-start.18 = (bf16[512,512]{1,0:T(8,128)(2,1)S(1)}, bf16[512,512]{1,0:T(8,128)(2,1)S(1)}, u32[]{:S(2)}, u32[]{:S(2)}) collective-permute-start(bf16[512,512]{1,0:T(8,128)(2,1)S(1)} %pad_maximum_fusion.2.refs_5_), channel_id=1, source_target_pairs={{0,16},{4,20},{8,24},{12,28},{16,0},{20,4},{24,8},{28,12},{1,17},{... | collective-permute-start | bytes 1572872 | tf_op jit(solution)/shard_map/ppermute | solution.py:89
  57.4 31.2 %copy-start.18 = (bf16[512,512]{1,0:T(8,128)(2,1)}, bf16[512,512]{1,0:T(8,128)(2,1)S(1)}, u32[]{:S(2)}) copy-start(bf16[512,512]{1,0:T(8,128)(2,1)S(1)} %collective-permute-done.14.refs_4_) | copy-start | bytes 1572868
  57.4 30.6 %collective-permute-start.20 = (bf16[512,512]{1,0:T(8,128)(2,1)S(1)}, bf16[512,512]{1,0:T(8,128)(2,1)S(1)}, u32[]{:S(2)}, u32[]{:S(2)}) collective-permute-start(bf16[512,512]{1,0:T(8,128)(2,1)S(1)} %pad_maximum_fusion.2.refs_5_), channel_id=1, source_target_pairs={{0,8},{4,12},{8,0},{12,4},{16,24},{20,28},{24,16},{28,20},{1,9},{5... | collective-permute-start | bytes 1572872 | tf_op jit(solution)/shard_map/ppermute | solution.py:85
  58.2 29.8 %copy-start.13 = (bf16[256,1024]{1,0:T(8,128)(2,1)}, bf16[256,1024]{1,0:T(8,128)(2,1)S(1)}, u32[]{:S(2)}) copy-start(bf16[256,1024]{1,0:T(8,128)(2,1)S(1)} %collective-permute-done.10.refs_12_) | copy-start | bytes 1572868
  58.2 30.4 %collective-permute-start.11 = (bf16[256,1024]{1,0:T(8,128)(2,1)S(1)}, bf16[256,1024]{1,0:T(8,128)(2,1)S(1)}, u32[]{:S(2)}, u32[]{:S(2)}) collective-permute-start(bf16[256,1024]{1,0:T(8,128)(2,1)S(1)} %collective-permute-done.10.refs_12_), channel_id=1, source_target_pairs={{0,4},{4,0},{8,12},{12,8},{16,20},{20,16},{24,28},{28,24},{1,5},{5... | collective-permute-start | bytes 1572872 | tf_op jit(solution)/shard_map/ppermute | solution.py:81
  68.5 26.7 %collective-permute-start.5 = (bf16[512,1024]{1,0:T(8,128)(2,1)S(1)}, bf16[512,1024]{1,0:T(8,128)(2,1)}, u32[]{:S(2)}, u32[]{:S(2)}) collective-permute-start(bf16[512,1024]{1,0:T(8,128)(2,1)S(1)} %collective-permute-done.4.refs_6_), channel_id=1, source_target_pairs={{0,4},{4,0},{8,12},{12,8},{16,20},{20,16},{24,28},{28,24},{1,5},{5... | collective-permute-start | bytes 3145736 | tf_op jit(solution)/shard_map/ppermute | solution.py:81
  79.9 17.0 %collective-permute-start.7 = (bf16[512,1024]{1,0:T(8,128)(2,1)}, bf16[512,1024]{1,0:T(8,128)(2,1)}, u32[]{:S(2)}, u32[]{:S(2)}) collective-permute-start(bf16[512,1024]{1,0:T(8,128)(2,1)} %collective-permute-done.6.refs_8_), channel_id=1, source_target_pairs={{0,4},{4,0},{8,12},{12,8},{16,20},{20,16},{24,28},{28,24},{1,5},{5... | collective-permute-start | bytes 3145736 | tf_op jit(solution)/shard_map/ppermute | solution.py:81
  79.9 40.3 %collective-permute-start.29 = (bf16[512,1024]{1,0:T(8,128)(2,1)}, bf16[512,1024]{1,0:T(8,128)(2,1)S(1)}, u32[]{:S(2)}, u32[]{:S(2)}) collective-permute-start(bf16[512,1024]{1,0:T(8,128)(2,1)} %refs_0_.3), channel_id=1, source_target_pairs={{0,16},{4,20},{8,24},{12,28},{16,0},{20,4},{24,8},{28,12},{1,17},{... | collective-permute-start | bytes 3145736 | tf_op jit(solution)/shard_map/ppermute | solution.py:89
  88.0 32.1 %collective-permute-start.27 = (bf16[512,1024]{1,0:T(8,128)(2,1)}, bf16[512,1024]{1,0:T(8,128)(2,1)S(1)}, u32[]{:S(2)}, u32[]{:S(2)}) collective-permute-start(bf16[512,1024]{1,0:T(8,128)(2,1)} %refs_0_.3), channel_id=1, source_target_pairs={{0,8},{4,12},{8,0},{12,4},{16,24},{20,28},{24,16},{28,20},{1,9},{5... | collective-permute-start | bytes 3145736 | tf_op jit(solution)/shard_map/ppermute | solution.py:85
  89.6 2.3 %collective-permute-start.9 = (bf16[256,1024]{1,0:T(8,128)(2,1)}, bf16[256,1024]{1,0:T(8,128)(2,1)}, u32[]{:S(2)}, u32[]{:S(2)}) collective-permute-start(bf16[256,1024]{1,0:T(8,128)(2,1)} %collective-permute-done.8.refs_10_), channel_id=1, source_target_pairs={{0,4},{4,0},{8,12},{12,8},{16,20},{20,16},{24,28},{28,24},{1,5},{5... | collective-permute-start | bytes 1572872 | tf_op jit(solution)/shard_map/ppermute | solution.py:81
  91.9 26.7 %collective-permute-start.15 = (bf16[256,512]{1,0:T(8,128)(2,1)S(1)}, bf16[256,512]{1,0:T(8,128)(2,1)S(1)}, u32[]{:S(2)}, u32[]{:S(2)}) collective-permute-start(bf16[256,512]{1,0:T(8,128)(2,1)S(1)} %slice.43), channel_id=1, source_target_pairs={{0,8},{4,12},{8,0},{12,4},{16,24},{20,28},{24,16},{28,20},{1,9},{5... | collective-permute-start | bytes 786440 | tf_op jit(solution)/shard_map/ppermute | solution.py:85
  95.3 26.4 %collective-permute-start.17 = (bf16[256,512]{1,0:T(8,128)(2,1)}, bf16[256,512]{1,0:T(8,128)(2,1)S(1)}, u32[]{:S(2)}, u32[]{:S(2)}) collective-permute-start(bf16[256,512]{1,0:T(8,128)(2,1)} %slice.44), channel_id=1, source_target_pairs={{0,16},{4,20},{8,24},{12,28},{16,0},{20,4},{24,8},{28,12},{1,17},{... | collective-permute-start | bytes 786440 | tf_op jit(solution)/shard_map/ppermute | solution.py:89
  96.8 25.4 %collective-permute-start.19 = (bf16[256,512]{1,0:T(8,128)(2,1)}, bf16[256,512]{1,0:T(8,128)(2,1)S(1)}, u32[]{:S(2)}, u32[]{:S(2)}) collective-permute-start(bf16[256,512]{1,0:T(8,128)(2,1)} %slice.46), channel_id=1, source_target_pairs={{0,8},{4,12},{8,0},{12,4},{16,24},{20,28},{24,16},{28,20},{1,9},{5... | collective-permute-start | bytes 786440 | tf_op jit(solution)/shard_map/ppermute | solution.py:85
  118.6 6.7 %collective-permute-start.21 = (bf16[256,512]{1,0:T(8,128)(2,1)S(1)}, bf16[256,512]{1,0:T(8,128)(2,1)}, u32[]{:S(2)}, u32[]{:S(2)}) collective-permute-start(bf16[256,512]{1,0:T(8,128)(2,1)S(1)} %slice.47), channel_id=1, source_target_pairs={{0,16},{4,20},{8,24},{12,28},{16,0},{20,4},{24,8},{28,12},{1,17},{... | collective-permute-start | bytes 786440 | tf_op jit(solution)/shard_map/ppermute | solution.py:89
  120.2 5.2 %collective-permute-start.12 = (bf16[256,512]{1,0:T(8,128)(2,1)}, bf16[256,512]{1,0:T(8,128)(2,1)S(1)}, u32[]{:S(2)}, u32[]{:S(2)}) collective-permute-start(bf16[256,512]{1,0:T(8,128)(2,1)} %get-tuple-element.30), channel_id=1, source_target_pairs={{0,4},{4,0},{8,12},{12,8},{16,20},{20,16},{24,28},{28,24},{1,5},{5... | collective-permute-start | bytes 786440 | tf_op jit(solution)/shard_map/ppermute | solution.py:81
  120.2 24.9 %collective-permute-start.23 = (bf16[512,1024]{1,0:T(8,128)(2,1)}, bf16[512,1024]{1,0:T(8,128)(2,1)}, u32[]{:S(2)}, u32[]{:S(2)}) collective-permute-start(bf16[512,1024]{1,0:T(8,128)(2,1)} %refs_0_.3), channel_id=1, source_target_pairs={{0,4},{4,0},{8,12},{12,8},{16,20},{20,16},{24,28},{28,24},{1,5},{5... | collective-permute-start | bytes 3145736 | tf_op jit(solution)/shard_map/ppermute | solution.py:81
  121.7 16.2 %collective-permute-start.34 = (bf16[256,1024]{1,0:T(8,128)(2,1)}, bf16[256,1024]{1,0:T(8,128)(2,1)}, u32[]{:S(2)}, u32[]{:S(2)}) collective-permute-start(bf16[256,1024]{1,0:T(8,128)(2,1)} %slice.48), channel_id=1, source_target_pairs={{0,8},{4,12},{8,0},{12,4},{16,24},{20,28},{24,16},{28,20},{1,9},{5... | collective-permute-start | bytes 1572872 | tf_op jit(solution)/shard_map/ppermute | solution.py:85
  122.3 16.2 %collective-permute-start.36 = (bf16[256,1024]{1,0:T(8,128)(2,1)S(1)}, bf16[256,1024]{1,0:T(8,128)(2,1)}, u32[]{:S(2)}, u32[]{:S(2)}) collective-permute-start(bf16[256,1024]{1,0:T(8,128)(2,1)S(1)} %slice.49), channel_id=1, source_target_pairs={{0,16},{4,20},{8,24},{12,28},{16,0},{20,4},{24,8},{28,12},{1,17},{... | collective-permute-start | bytes 1572872 | tf_op jit(solution)/shard_map/ppermute | solution.py:89
  125.3 28.5 %collective-permute-start.28 = (bf16[512,1024]{1,0:T(8,128)(2,1)S(1)}, bf16[512,1024]{1,0:T(8,128)(2,1)S(1)}, u32[]{:S(2)}, u32[]{:S(2)}) collective-permute-start(bf16[512,1024]{1,0:T(8,128)(2,1)S(1)} %collective-permute-done.27.refs_0_), channel_id=1, source_target_pairs={{0,4},{4,0},{8,12},{12,8},{16,20},{20,16},{24,28},{28,24},{1,5},{5... | collective-permute-start | bytes 3145736 | tf_op jit(solution)/shard_map/ppermute | solution.py:81
  125.4 31.8 %collective-permute-start.30 = (bf16[512,1024]{1,0:T(8,128)(2,1)S(1)}, bf16[512,1024]{1,0:T(8,128)(2,1)}, u32[]{:S(2)}, u32[]{:S(2)}) collective-permute-start(bf16[512,1024]{1,0:T(8,128)(2,1)S(1)} %collective-permute-done.29.refs_2_), channel_id=1, source_target_pairs={{0,4},{4,0},{8,12},{12,8},{16,20},{20,16},{24,28},{28,24},{1,5},{5... | collective-permute-start | bytes 3145736 | tf_op jit(solution)/shard_map/ppermute | solution.py:81
  137.9 24.0 %collective-permute-start.35 = (bf16[256,1024]{1,0:T(8,128)(2,1)}, bf16[256,1024]{1,0:T(8,128)(2,1)}, u32[]{:S(2)}, u32[]{:S(2)}) collective-permute-start(bf16[256,1024]{1,0:T(8,128)(2,1)} %collective-permute-done.34.refs_0_), channel_id=1, source_target_pairs={{0,4},{4,0},{8,12},{12,8},{16,20},{20,16},{24,28},{28,24},{1,5},{5... | collective-permute-start | bytes 1572872 | tf_op jit(solution)/shard_map/ppermute | solution.py:81
  138.5 24.1 %collective-permute-start.37 = (bf16[256,1024]{1,0:T(8,128)(2,1)}, bf16[256,1024]{1,0:T(8,128)(2,1)}, u32[]{:S(2)}, u32[]{:S(2)}) collective-permute-start(bf16[256,1024]{1,0:T(8,128)(2,1)} %collective-permute-done.36.refs_2_), channel_id=1, source_target_pairs={{0,4},{4,0},{8,12},{12,8},{16,20},{20,16},{24,28},{28,24},{1,5},{5... | collective-permute-start | bytes 1572872 | tf_op jit(solution)/shard_map/ppermute | solution.py:81
  145.1 1.9 collective-permute-start.22
  151.0 16.3 %collective-permute-start.24 = (bf16[64,1024]{1,0:T(8,128)(2,1)}, bf16[64,1024]{1,0:T(8,128)(2,1)S(1)}, u32[]{:S(2)}, u32[]{:S(2)}) collective-permute-start(bf16[64,1024]{1,0:T(8,128)(2,1)} %get-tuple-element.41), channel_id=1, source_target_pairs={{0,1},{1,0},{2,3},{3,2},{4,5},{5,4},{6,7},{7,6},{8,9},{9,8},{10,11... | collective-permute-start | bytes 393224 | tf_op jit(solution)/shard_map/ppermute | solution.py:403
  153.8 16.0 %collective-permute-start.25 = (bf16[64,1024]{1,0:T(8,128)(2,1)}, bf16[64,1024]{1,0:T(8,128)(2,1)S(1)}, u32[]{:S(2)}, u32[]{:S(2)}) collective-permute-start(bf16[64,1024]{1,0:T(8,128)(2,1)} %get-tuple-element.42), channel_id=1, source_target_pairs={{0,2},{1,3},{2,0},{3,1},{4,6},{5,7},{6,4},{7,5},{8,10},{9,11},{10,... | collective-permute-start | bytes 393224 | tf_op jit(solution)/shard_map/ppermute | solution.py:403
  157.2 14.1 %collective-permute-start.26 = (bf16[64,1024]{1,0:T(8,128)(2,1)}, bf16[64,1024]{1,0:T(8,128)(2,1)S(1)}, u32[]{:S(2)}, u32[]{:S(2)}) collective-permute-start(bf16[64,1024]{1,0:T(8,128)(2,1)} %get-tuple-element.43), channel_id=1, source_target_pairs={{0,3},{1,2},{2,1},{3,0},{4,7},{5,6},{6,5},{7,4},{8,11},{9,10},{10,... | collective-permute-start | bytes 393224 | tf_op jit(solution)/shard_map/ppermute | solution.py:403
  161.9 40.5 %collective-permute-start.31 = (bf16[64,2048]{1,0:T(8,128)(2,1)}, bf16[64,2048]{1,0:T(8,128)(2,1)S(1)}, u32[]{:S(2)}, u32[]{:S(2)}) collective-permute-start(bf16[64,2048]{1,0:T(8,128)(2,1)} %get-tuple-element.46), channel_id=1, source_target_pairs={{0,1},{1,0},{2,3},{3,2},{4,5},{5,4},{6,7},{7,6},{8,9},{9,8},{10,11... | collective-permute-start | bytes 786440 | tf_op jit(solution)/shard_map/ppermute | solution.py:403
  165.9 14.1 %collective-permute-start.38 = (bf16[64,1024]{1,0:T(8,128)(2,1)}, bf16[64,1024]{1,0:T(8,128)(2,1)S(1)}, u32[]{:S(2)}, u32[]{:S(2)}) collective-permute-start(bf16[64,1024]{1,0:T(8,128)(2,1)} %get-tuple-element.50), channel_id=1, source_target_pairs={{0,1},{1,0},{2,3},{3,2},{4,5},{5,4},{6,7},{7,6},{8,9},{9,8},{10,11... | collective-permute-start | bytes 393224 | tf_op jit(solution)/shard_map/ppermute | solution.py:403
  167.3 35.2 %copy-start.25 = (bf16[64,1024]{1,0:T(8,128)(2,1)}, bf16[64,1024]{1,0:T(8,128)(2,1)S(1)}, u32[]{:S(2)}) copy-start(bf16[64,1024]{1,0:T(8,128)(2,1)S(1)} %collective-permute-done.24.refs_1_) | copy-start | bytes 393220
  167.3 35.2 %collective-permute-start.32 = (bf16[64,2048]{1,0:T(8,128)(2,1)S(1)}, bf16[64,2048]{1,0:T(8,128)(2,1)S(1)}, u32[]{:S(2)}, u32[]{:S(2)}) collective-permute-start(bf16[64,2048]{1,0:T(8,128)(2,1)S(1)} %copy-done.36), channel_id=1, source_target_pairs={{0,2},{1,3},{2,0},{3,1},{4,6},{5,7},{6,4},{7,5},{8,10},{9,11},{10,... | collective-permute-start | bytes 786440 | tf_op jit(solution)/shard_map/ppermute | solution.py:403
  169.8 32.8 %copy-start.26 = (bf16[64,1024]{1,0:T(8,128)(2,1)}, bf16[64,1024]{1,0:T(8,128)(2,1)S(1)}, u32[]{:S(2)}) copy-start(bf16[64,1024]{1,0:T(8,128)(2,1)S(1)} %collective-permute-done.25.refs_2_) | copy-start | bytes 393220
  169.8 32.8 %collective-permute-start.33 = (bf16[64,2048]{1,0:T(8,128)(2,1)S(1)}, bf16[64,2048]{1,0:T(8,128)(2,1)S(1)}, u32[]{:S(2)}, u32[]{:S(2)}) collective-permute-start(bf16[64,2048]{1,0:T(8,128)(2,1)S(1)} %copy-done.35), channel_id=1, source_target_pairs={{0,3},{1,2},{2,1},{3,0},{4,7},{5,6},{6,5},{7,4},{8,11},{9,10},{10,... | collective-permute-start | bytes 786440 | tf_op jit(solution)/shard_map/ppermute | solution.py:403
  171.3 31.3 %copy-start.27 = (bf16[64,1024]{1,0:T(8,128)(2,1)}, bf16[64,1024]{1,0:T(8,128)(2,1)S(1)}, u32[]{:S(2)}) copy-start(bf16[64,1024]{1,0:T(8,128)(2,1)S(1)} %collective-permute-done.26.refs_3_) | copy-start | bytes 393220
  171.3 31.2 %collective-permute-start.39 = (bf16[64,1024]{1,0:T(8,128)(2,1)}, bf16[64,1024]{1,0:T(8,128)(2,1)S(1)}, u32[]{:S(2)}, u32[]{:S(2)}) collective-permute-start(bf16[64,1024]{1,0:T(8,128)(2,1)} %get-tuple-element.51), channel_id=1, source_target_pairs={{0,2},{1,3},{2,0},{3,1},{4,6},{5,7},{6,4},{7,5},{8,10},{9,11},{10,... | collective-permute-start | bytes 393224 | tf_op jit(solution)/shard_map/ppermute | solution.py:403
  180.0 22.5 %collective-permute-start.40 = (bf16[64,1024]{1,0:T(8,128)(2,1)}, bf16[64,1024]{1,0:T(8,128)(2,1)S(1)}, u32[]{:S(2)}, u32[]{:S(2)}) collective-permute-start(bf16[64,1024]{1,0:T(8,128)(2,1)} %get-tuple-element.52), channel_id=1, source_target_pairs={{0,3},{1,2},{2,1},{3,0},{4,7},{5,6},{6,5},{7,4},{8,11},{9,10},{10,... | collective-permute-start | bytes 393224 | tf_op jit(solution)/shard_map/ppermute | solution.py:403
  (30 other events, 173.4 us)

commit v2 on v1

v2 whole, which is shorter than its diff:
```python
import math

import jax
import jax.numpy as jnp
from jax import lax
from jax.experimental import pallas as pl
from jax.experimental.pallas import tpu as pltpu
from jax.sharding import PartitionSpec as P

HEAD_DIM = 64
PAIR = 2 * HEAD_DIM
VMEM = 60 * 1024 * 1024


def absorb(fold_state, query_heads, key_rows, value_rows):
    running_top, running_sum, weighted = fold_state
    local_heads = query_heads.shape[1]
    key_heads = key_rows.reshape(key_rows.shape[0], local_heads, HEAD_DIM)
    value_heads = value_rows.reshape(value_rows.shape[0], local_heads, HEAD_DIM)
    scores = jnp.einsum(
        "qhd,khd->hqk", query_heads, key_heads, preferred_element_type=jnp.float32
    ) * (1.0 / math.sqrt(HEAD_DIM))
    new_top = jnp.max(scores, axis=2)
    rescale = jnp.exp(running_top - new_top)
    probability = jnp.exp(scores - new_top[:, :, None])
    running_sum = running_sum * rescale + jnp.sum(probability, axis=2)
    weighted = weighted * rescale[:, :, None] + jnp.einsum(
        "hqk,khd->hqd",
        probability.astype(jnp.bfloat16),
        value_heads,
        preferred_element_type=jnp.float32,
    )
    return (new_top, running_sum, weighted)


def gathered_shards(decoder_states, w_query, w_out_t, enc_keys, enc_values):
    query_full = lax.all_gather(w_query, "blk", axis=0, tiled=True)
    row_count = decoder_states.shape[0]
    columns = query_full.shape[1]
    local_heads = columns // HEAD_DIM
    queries = jnp.dot(
        lax.all_gather(decoder_states, "fsdp", axis=1, tiled=True),
        query_full,
        preferred_element_type=jnp.float32,
    ).astype(jnp.bfloat16)
    start_state = (
        jnp.full((local_heads, row_count), -jnp.inf, jnp.float32),
        jnp.zeros((local_heads, row_count), jnp.float32),
        jnp.zeros((local_heads, row_count, HEAD_DIM), jnp.float32),
    )
    query_heads = queries.reshape(row_count, local_heads, HEAD_DIM)
    final_state = absorb(
        start_state,
        query_heads,
        lax.all_gather(enc_keys, "blk", axis=0, tiled=True),
        lax.all_gather(enc_values, "blk", axis=0, tiled=True),
    )
    context = final_state[2] / final_state[1][:, :, None]
    context = jnp.transpose(context, (1, 0, 2)).reshape(row_count, columns).astype(jnp.bfloat16)
    out_full = lax.all_gather(w_out_t, "blk", axis=0, tiled=True)
    return lax.psum_scatter(
        lax.dot_general(
            context, out_full, (((1,), (1,)), ((), ())), preferred_element_type=jnp.float32
        ),
        "fsdp",
        scatter_dimension=0,
        tiled=True,
    ).astype(jnp.bfloat16)


CORE = [(b, b ^ 1) for b in range(8)]
CROSS = [(b, b ^ (2 if b % 2 == 0 else 4)) for b in range(8)]
CROSS_BACK = [(b, b ^ (4 if b % 2 == 0 else 2)) for b in range(8)]

def over_core(a):
    return lax.ppermute(a, "blk", CORE)


def cross(a):
    return lax.ppermute(a, "blk", CROSS)


def cross_back(a):
    return lax.ppermute(a, "blk", CROSS_BACK)


def over_z(a, step):
    return lax.ppermute(a, "fsdp", [(z, z ^ step) for z in range(4)])


def after(value, *earlier):
    return lax.optimization_barrier((value,) + earlier)[0]


OWN, OWN_SWAPPED = (0, 0, 0), (0, 0, 1)
NEAR, NEAR_SWAPPED = (1, 2, 0), (2, 1, 1)
SIDE, SIDE_SWAPPED = (2, 1, 0), (1, 2, 1)
FAR, FAR_SWAPPED = (3, 3, 0), (3, 3, 1)


def owner(place_ref, whose):
    chip, core = place_ref[0], place_ref[1]
    even, odd, core_step = whose
    return chip ^ (even + core * (odd - even)), core ^ core_step


def any_spec():
    return pl.BlockSpec(memory_space=pl.ANY)


def smem_spec():
    return pl.BlockSpec(memory_space=pltpu.SMEM)


def vmem_spec():
    return pl.BlockSpec(memory_space=pltpu.VMEM)


def project_queries(place, states, weights):
    rows, depth = states[0].shape
    shard, columns = weights[0][1].shape
    half = columns // 2
    count = len(states) + len(weights)

    def kernel(place_ref, *refs):
        state_refs = refs[: len(states)]
        weight_refs = refs[len(states) : count]
        mine_ref, other_ref, state_s, weight_s, total, sems = refs[count:]
        core, plane = place_ref[1], place_ref[2]
        state_copies, weight_copies = [], []
        for n, ref in enumerate(state_refs):
            copy = pltpu.make_async_copy(ref, state_s.at[plane ^ n], sems.at[n])
            copy.start()
            state_copies.append(copy)
        for n, (ref, (whose, _)) in enumerate(zip(weight_refs, weights)):
            chip_at, core_at = owner(place_ref, whose)
            begin = pl.multiple_of(core_at * shard, shard)
            copy = pltpu.make_async_copy(
                ref, weight_s.at[chip_at, pl.ds(begin, shard)], sems.at[len(states) + n]
            )
            copy.start()
            weight_copies.append(copy)
        for copy in state_copies:
            copy.wait()
        for n, (whose, _) in enumerate(weights):
            weight_copies[n].wait()
            chip_at, core_at = owner(place_ref, whose)
            begin = pl.multiple_of(core_at * shard, shard)
            part = jnp.dot(
                state_s[chip_at, :, pl.ds(begin, shard)],
                weight_s[chip_at, pl.ds(begin, shard)],
                preferred_element_type=jnp.float32,
            )
            total[...] = part if n == 0 else total[...] + part
        factor = 1.0 / math.sqrt(HEAD_DIM)
        for ref, which in ((mine_ref, core), (other_ref, 1 - core)):
            begin = pl.multiple_of(which * half, half)
            queries = total[:, pl.ds(begin, half)].astype(jnp.bfloat16)
            ref[...] = (queries.astype(jnp.float32) * factor).astype(jnp.bfloat16)

    shape = jax.ShapeDtypeStruct((rows, half), jnp.bfloat16)
    return pl.pallas_call(
        kernel,
        out_shape=(shape, shape),
        in_specs=[smem_spec()] + [any_spec()] * count,
        out_specs=(vmem_spec(), vmem_spec()),
        scratch_shapes=[
            pltpu.VMEM((4, rows, depth), jnp.bfloat16),
            pltpu.VMEM((4, depth, columns), jnp.bfloat16),
            pltpu.VMEM((rows, columns), jnp.float32),
            pltpu.SemaphoreType.DMA((count,)),
        ],
        compiler_params=pltpu.CompilerParams(vmem_limit_bytes=VMEM),
        cost_estimate=pl.CostEstimate(
            flops=2 * rows * 4 * depth * columns,
            bytes_accessed=2 * 4 * depth * (rows + columns),
            transcendentals=0,
        ),
        name="project_queries",
    )(place, *states, *[w[1] for w in weights])


def pair_part(queries, keys, values):
    rows = queries.shape[0]
    first = lax.broadcasted_iota(jnp.int32, (rows, PAIR), 1) < HEAD_DIM
    found = []
    for head in range(2):
        masked = jnp.where(first if head == 0 else jnp.logical_not(first), queries, 0)
        scores = [
            lax.dot_general(
                masked, k, (((1,), (1,)), ((), ())), preferred_element_type=jnp.float32
            )
            for k in keys
        ]
        top = scores[0].max(axis=1, keepdims=True)
        for s in scores[1:]:
            top = jnp.maximum(top, s.max(axis=1, keepdims=True))
        both = None
        for s, v in zip(scores, values):
            probability = jnp.exp(s - top).astype(jnp.bfloat16)
            part = jnp.dot(probability, v, preferred_element_type=jnp.float32)
            both = part if both is None else both + part
        found.append((both[:, :PAIR], both[:, PAIR:], jnp.broadcast_to(top, (rows, PAIR))))
    return [jnp.where(first, a, b) for a, b in zip(*found)]


def attend(query_blocks, pieces, before=None):
    rows, columns = query_blocks[0].shape
    pairs = columns // PAIR
    blocks = len(query_blocks)
    last = before is not None
    held = [] if before is None else [a for block in before for a in block]
    outs = blocks if last else 3 * blocks

    def kernel(*refs):
        refs = list(refs)
        q_refs = [refs.pop(0) for _ in range(blocks)]
        k_refs = [refs.pop(0) for _ in pieces]
        v_refs = [refs.pop(0) for _ in pieces]
        held_refs = [refs.pop(0) for _ in held]
        out_refs = [refs.pop(0) for _ in range(outs)]
        ks = [r[...] for r in k_refs]
        vs = [
            jnp.concatenate([r[...], jnp.ones(r.shape, jnp.bfloat16)], axis=1) for r in v_refs
        ]
        for n in range(blocks):
            weighted, sums, tops = pair_part(q_refs[n][...], ks, vs)
            if last:
                weighted_0, sums_0, tops_0 = (r[...] for r in held_refs[3 * n : 3 * n + 3])
                top = jnp.maximum(tops, tops_0)
                now, then = jnp.exp(tops - top), jnp.exp(tops_0 - top)
                weighted = weighted * now + weighted_0 * then
                sums = sums * now + sums_0 * then
                out_refs[n][...] = (weighted / sums).astype(jnp.bfloat16)
            else:
                for ref, a in zip(out_refs[3 * n : 3 * n + 3], (weighted, sums, tops)):
                    ref[...] = a

    def spec(a, skip=0):
        return pl.BlockSpec((a.shape[0], PAIR), lambda p: (0, p + skip))

    args = list(query_blocks) + list(pieces) + list(pieces) + held
    in_specs = (
        [spec(a) for a in query_blocks]
        + [spec(a) for a in pieces]
        + [spec(a, pairs) for a in pieces]
        + [spec(a) for a in held]
    )
    out_shape = [
        jax.ShapeDtypeStruct((rows, columns), jnp.bfloat16 if last else jnp.float32)
    ] * outs
    total_keys = sum(a.shape[0] for a in pieces)
    found = pl.pallas_call(
        kernel,
        grid=(pairs,),
        out_shape=out_shape,
        in_specs=in_specs,
        out_specs=[spec(a) for a in out_shape],
        compiler_params=pltpu.CompilerParams(vmem_limit_bytes=VMEM),
        cost_estimate=pl.CostEstimate(
            flops=2 * 2 * blocks * rows * total_keys * columns * 4,
            bytes_accessed=sum(a.size * a.dtype.itemsize for a in args),
            transcendentals=blocks * rows * total_keys * (columns // HEAD_DIM),
        ),
        name="attend_last" if last else "attend_first",
    )(*args)
    if last:
        return found
    return [found[3 * n : 3 * n + 3] for n in range(blocks)]


def project_out(place, mine, other, weights, tiles=2):
    rows, half = mine.shape
    quarter = rows // 4
    tile = weights[0].shape[0] // tiles
    width = tile * len(weights)

    def kernel(place_ref, mine_ref, other_ref, *refs):
        weight_refs = refs[: len(weights)]
        kept_ref, sent_ref, context = refs[len(weights) :]
        core, plane = place_ref[1], place_ref[2]

        @pl.when(pl.program_id(0) == 0)
        def _():
            for n, step in enumerate((0, 2, 1, 3)):
                begin = pl.multiple_of((plane ^ step) * quarter, quarter)
                here = slice(n * quarter, (n + 1) * quarter)
                for ref, which in ((mine_ref, core), (other_ref, 1 - core)):
                    lanes = pl.ds(pl.multiple_of(which * half, half), half)
                    context[here, lanes] = ref[pl.ds(begin, quarter), :]

        for n, ref in enumerate(weight_refs):
            part = lax.dot_general(
                context[...],
                ref[...],
                (((1,), (1,)), ((), ())),
                preferred_element_type=jnp.float32,
            )
            here = slice(n * tile, (n + 1) * tile)
            kept_ref[:, here] = part[: 2 * quarter]
            sent_ref[:, here] = part[2 * quarter :].astype(jnp.bfloat16)

    def whole(a):
        return pl.BlockSpec(a.shape, lambda t: (0, 0))

    return pl.pallas_call(
        kernel,
        grid=(tiles,),
        out_shape=[
            jax.ShapeDtypeStruct((2 * quarter, tiles * width), kind)
            for kind in (jnp.float32, jnp.bfloat16)
        ],
        in_specs=[smem_spec(), whole(mine), whole(other)]
        + [pl.BlockSpec((tile, 2 * half), lambda t: (t, 0))] * len(weights),
        out_specs=[pl.BlockSpec((2 * quarter, width), lambda t: (0, t))] * 2,
        scratch_shapes=[pltpu.VMEM((rows, 2 * half), jnp.bfloat16)],
        compiler_params=pltpu.CompilerParams(vmem_limit_bytes=VMEM),
        cost_estimate=pl.CostEstimate(
            flops=2 * rows * 2 * half * width * tiles,
            bytes_accessed=2 * width * tiles * 2 * half,
            transcendentals=0,
        ),
        name="project_out",
    )(place, mine, other, *weights)


def add_up(place, groups, shard, tiles=2):
    rows, width = groups[0][3].shape
    tile = shard // tiles

    def kernel(place_ref, *refs):
        out_ref = refs[-1]
        for n, (owners, *_) in enumerate(groups):
            kept_ref, first_ref, second_ref = refs[3 * n : 3 * n + 3]
            total = kept_ref[...] + first_ref[...].astype(jnp.float32)
            total = total + second_ref[...].astype(jnp.float32)
            for i, whose in enumerate(owners):
                chip_at, core_at = owner(place_ref, whose)
                for t in range(tiles):
                    begin = (chip_at * 2 + core_at) * shard + t * tile
                    at = (t * len(owners) + i) * tile
                    out_ref[:, pl.ds(pl.multiple_of(begin, tile), tile)] = total[
                        :, at : at + tile
                    ].astype(jnp.bfloat16)

    args = [a for group in groups for a in group[1:]]
    return pl.pallas_call(
        kernel,
        out_shape=jax.ShapeDtypeStruct((rows, 8 * shard), jnp.bfloat16),
        grid=(1,),
        in_specs=[smem_spec()] + [pl.BlockSpec((rows, width), lambda t: (0, 0))] * len(args),
        out_specs=pl.BlockSpec((rows, 8 * shard), lambda t: (0, 0)),
        compiler_params=pltpu.CompilerParams(vmem_limit_bytes=VMEM),
        cost_estimate=pl.CostEstimate(
            flops=2 * rows * 8 * shard, bytes_accessed=8 * rows * 8 * shard, transcendentals=0
        ),
        name="add_up",
    )(place, *args)


def plane_shards(decoder_states, w_query, w_out_t, enc_keys, enc_values):
    block, plane = lax.axis_index("blk"), lax.axis_index("fsdp")
    chip, core = block // 2, block % 2
    place = jnp.stack([chip, core, plane]).astype(jnp.int32)
    shard = w_query.shape[0]
    half = enc_keys.shape[1] // 2

    states_2 = over_z(decoder_states, 2)
    states_1 = over_z(decoder_states, 1)
    states_3 = over_z(states_2, 1)

    near, side = cross(w_query), cross_back(w_query)
    far = cross(after(side, near, states_1, states_2))
    query_pieces = [
        (OWN, w_query),
        (OWN_SWAPPED, over_core(w_query)),
        (NEAR, near),
        (NEAR_SWAPPED, over_core(near)),
        (SIDE, side),
        (SIDE_SWAPPED, over_core(side)),
        (FAR, far),
        (FAR_SWAPPED, over_core(far)),
    ]

    def columns(a, which):
        return lax.dynamic_slice_in_dim(a, which * half, half, 1)

    def side_by_side(which):
        return jnp.concatenate([columns(enc_keys, which), columns(enc_values, which)], axis=1)

    swapped = over_core(side_by_side(1 - core))
    encoded = jnp.concatenate([side_by_side(core), swapped], axis=0)
    encoded_near = cross(after(encoded, near, side, states_1, states_2))

    queries, queries_other = project_queries(
        place,
        [decoder_states, states_1, states_2, states_3],
        query_pieces,
    )
    encoded_passed = cross(after(over_core(encoded), far, states_3))
    encoded_far = cross_back(after(encoded_near, queries))
    query_blocks = [queries, over_core(queries_other)]
    before = attend(query_blocks, [encoded, encoded_near])
    encoded_side = over_core(after(encoded_passed, before[0][0]))
    context, context_other = attend(query_blocks, [encoded_side, encoded_far], before)
    context_back = over_core(context_other)

    out_own = after(w_out_t, encoded_passed, before[0][0])
    out_near = cross_back(out_own)
    out_side = cross(after(w_out_t, encoded_far))
    sums = []

    def add_group(*group):
        pieces = [piece for _, piece in group]
        kept, sent = project_out(place, context, context_back, pieces)
        first = over_z(sent, 1)
        rows = kept.shape[0] // 2
        passed = (kept[rows:] + first[rows:].astype(jnp.float32)).astype(jnp.bfloat16)
        second = over_z(passed, 2)
        sums.append(([whose for whose, _ in group], kept, first, second))
        return sent, passed, second

    sent, passed, second = add_group((OWN, w_out_t), (OWN_SWAPPED, over_core(out_own)))
    sent, passed_next, _ = add_group((SIDE, out_near), (SIDE_SWAPPED, over_core(after(out_near, context))))
    out_far = cross(after(out_near, sent))
    out_side = after(out_side, passed)
    add_group((NEAR, out_side), (NEAR_SWAPPED, over_core(out_side)))
    out_far = after(out_far, passed_next, second)
    add_group((FAR, out_far), (FAR_SWAPPED, over_core(out_far)))
    return add_up(place, sums, shard)


def solution(mesh):
    in_specs = (
        P("blk", "fsdp"),
        P("blk", "fsdp"),
        P("blk", "fsdp"),
        P("blk", "fsdp"),
        P("blk", "fsdp"),
    )
    out_specs = P(("blk", "fsdp"), None)
    by_planes = mesh.shape["blk"] == 8 and mesh.shape["fsdp"] == 4
    return jax.shard_map(
        plane_shards if by_planes else gathered_shards,
        mesh=mesh,
        in_specs=in_specs,
        out_specs=out_specs,
        check_vma=False,
    )
```

time: 208 us -> 163 us (0.78)
  waiting for transfers between devices: 113 us -> 87.1 us
  starting transfers between devices: 43.1 us -> 24 us
  other arithmetic: 0.76 us -> 3.7 us
  local copies, waits for them, and re-layouts: 9.93 us -> 7.81 us
    ppermute x28 -> x20, waiting for transfers between devices: 111 us -> 83.7 us  [the longest x11 66.4 us: over_z(): return lax.ppermute(a, 'fsdp', [(z, z ^ step) for z in range(4)])]
    ppermute x28 -> x20, starting transfers between devices: 40.8 us -> 22 us  [the longest x11 11.3 us: over_z(): return lax.ppermute(a, 'fsdp', [(z, z ^ step) for z in range(4)])]
    slice x9 -> x0, local copies, waits for them, and re-layouts: 4.62 us -> none  [the longest x8 4.59 us: relay(): return (over_x(from_y[:half]), over_y(from_x[half:]))]
    convert_element_type x0 -> x4, other arithmetic: none -> 2.91 us  [add_group(): (kept[rows:] + first[rows:].astype(jnp.float32)).astype(jnp.bfloat16)]
    unnamed x74 -> x52, local copies, waits for them, and re-layouts: 4 us -> 6.56 us
    pallas_call x5 -> x6, Pallas kernels: 29.7 us -> 30.8 us  [the longest x2 18.1 us: attend(): pl.pallas_call(kernel, grid=(pairs,), out_shape=out_shape, in_specs=in_sp...]
  transfers between devices with their start and end apart: 41 -> 33, of which waited for: 13 -> 17; matrix products, arithmetic and copies ran while one was open for 3% -> 3% of each run, Pallas kernels for 17% -> 23%
where the time goes in v2:
time: 163 us; the launch traced here: 162 us
  waiting for transfers between devices  87.1 us (53%)
  Pallas kernels  39.6 us (24%)
  starting transfers between devices  24 us (15%)
  local copies, waits for them, and re-layouts  7.81 us (5%)
  other arithmetic  3.7 us (2%)
    ppermute x11, waiting for transfers between devices, over_z(): return lax.ppermute(a, 'fsdp', [(z, z ^ step) for z in range(4)])  66.4 us
    pallas_call x2, Pallas kernels, attend(): pl.pallas_call(kernel, grid=(pairs,), out_shape=out_shape, in_specs=in_sp...  18.1 us
    ppermute x6, waiting for transfers between devices, cross(): return lax.ppermute(a, 'blk', CROSS)  14.5 us
    pallas_call x4, Pallas kernels, project_out(): pl.pallas_call(kernel, grid=(tiles,), out_shape=[jax.ShapeDtypeStruct((2...  12.8 us
    ppermute x11, starting transfers between devices, over_z(): return lax.ppermute(a, 'fsdp', [(z, z ^ step) for z in range(4)])  11.3 us
    ppermute x6, starting transfers between devices, cross(): return lax.ppermute(a, 'blk', CROSS)  8.24 us
    unnamed x52, local copies, waits for them, and re-layouts  6.56 us
    pallas_call x1, Pallas kernels, project_queries(): pl.pallas_call(kernel, out_shape=(shape, shape), in_specs=[smem_spec()] +...  6.27 us
  transfers between devices with their start and end apart: 33, of which 17 were waited for; matrix products, arithmetic and copies ran while one was open for 3% of the time, Pallas kernels for 23%

profile of v2, /device:TPU:0, one launch (start us, length us, event | category | flops | bytes accessed | tf_op | source)
XLA Modules:
  0.0 162.5 jit_solution(8696140361043304079)
XLA Ops:
  0.0 2.9 %collective-permute-start.4 = (bf16[512,1024]{1,0:T(8,128)(2,1)}, bf16[512,1024]{1,0:T(8,128)(2,1)}, u32[]{:S(2)}, u32[]{:S(2)}) collective-permute-start(bf16[512,1024]{1,0:T(8,128)(2,1)} %refs_4_.1), channel_id=1, source_target_pairs={{0,8},{4,20},{8,0},{12,28},{16,24},{20,4},{24,16},{28,12},{1,9},{5... | collective-permute-start | bytes 3145736 | tf_op jit(solution)/shard_map/ppermute | solution.py:80
  2.9 1.5 collective-permute-start.6
  4.5 1.6 collective-permute-start
  6.0 2.6 %collective-permute-start.1 = (bf16[256,1024]{1,0:T(8,128)(2,1)}, bf16[256,1024]{1,0:T(8,128)(2,1)S(1)}, u32[]{:S(2)}, u32[]{:S(2)}) collective-permute-start(bf16[256,1024]{1,0:T(8,128)(2,1)} %refs_0_.2), channel_id=1, source_target_pairs={{0,2},{1,3},{2,0},{3,1},{4,6},{5,7},{6,4},{7,5},{8,10},{9,11},{10,... | collective-permute-start | bytes 1572872 | tf_op jit(solution)/shard_map/ppermute | solution.py:88
  8.6 1.3 constant_dynamic-slice_fusion.2
  10.0 18.8 %collective-permute-done.refs_1_ = bf16[256,1024]{1,0:T(8,128)(2,1)S(1)} collective-permute-done((bf16[256,1024]{1,0:T(8,128)(2,1)}, bf16[256,1024]{1,0:T(8,128)(2,1)S(1)}, u32[]{:S(2)}, u32[]{:S(2)}) %collective-permute-start) | collective-permute-done | bytes 524320 | tf_op jit(solution)/shard_map/ppermute | solution.py:88
  28.9 2.4 %collective-permute-done.1.refs_2_ = bf16[256,1024]{1,0:T(8,128)(2,1)S(1)} collective-permute-done((bf16[256,1024]{1,0:T(8,128)(2,1)}, bf16[256,1024]{1,0:T(8,128)(2,1)S(1)}, u32[]{:S(2)}, u32[]{:S(2)}) %collective-permute-start.1) | collective-permute-done | bytes 524320 | tf_op jit(solution)/shard_map/ppermute | solution.py:88
  32.3 0.9 copy-done.17
  34.3 12.2 %collective-permute-done.2.refs_3_ = bf16[256,1024]{1,0:T(8,128)(2,1)S(1)} collective-permute-done((bf16[256,1024]{1,0:T(8,128)(2,1)S(1)}, bf16[256,1024]{1,0:T(8,128)(2,1)S(1)}, u32[]{:S(2)}, u32[]{:S(2)}) %collective-permute-start.2) | collective-permute-done | bytes 524320 | tf_op jit(solution)/shard_map/ppermute | solution.py:88
  47.1 1.3 collective-permute-start.14
  48.4 1.0 copy-done.10
  49.4 0.7 collective-permute-start.13
  50.1 0.6 pad_add_fusion.place_ref
  51.1 6.3 %project_queries.1 = (bf16[256,512]{1,0:T(8,128)(2,1)}, bf16[256,512]{1,0:T(8,128)(2,1)}) custom-call(s32[3]{0:T(128)} %pad_add_fusion.place_ref, bf16[256,1024]{1,0:T(8,128)(2,1)} %refs_0_.2, bf16[256,1024]{1,0:T(8,128)(2,1)} %copy-done.15, bf16[256,1024]{1,0:T(8,128)(2,1)} %copy-done.16, bf16[256,1024]{1,0:T(8,128)(2,1)} %copy-done.18, ...), custom_call_target="tpu_custom_call" | custom-call | flops 2147483648 | bytes 10485760 | tf_op jit(solution)/shard_map/project_queries/pallas_call | solution.py:162
  57.6 4.4 %collective-permute-done.14.refs_3_.refs_5_ = bf16[512,1024]{1,0:T(8,128)(2,1)} collective-permute-done((bf16[512,1024]{1,0:T(8,128)(2,1)S(1)}, bf16[512,1024]{1,0:T(8,128)(2,1)}, u32[]{:S(2)}, u32[]{:S(2)}) %collective-permute-start.14) | collective-permute-done | bytes 1048608 | tf_op jit(solution)/shard_map/ppermute | solution.py:80
  62.5 0.7 copy-done.25
  63.3 8.9 %attend_first.1 = (f32[256,512]{1,0:T(8,128)}, f32[256,512]{1,0:T(8,128)}, f32[256,512]{1,0:T(8,128)}, f32[256,512]{1,0:T(8,128)}, f32[256,512]{1,0:T(8,128)}, /*index=5*/f32[256,512]{1,0:T(8,128)}) custom-call(bf16[256,512]{1,0:T(8,128)(2,1)} %get-tuple-element.35.refs_0_, bf16[256,512]{1,0:T(8,128)(2,1)} %copy-done.25, bf16[512,1024]{1,0:T(8,128)(2,1)} %copy-done.4, ...), custom_call_target="tpu_custom_call" | custom-call | flops 4294967296 | bytes 4718592 | tf_op jit(solution)/shard_map/attend_first/pallas_call | solution.py:253
  72.2 10.0 %collective-permute-done.13 = bf16[512,1024]{1,0:T(8,128)(2,1)S(1)} collective-permute-done((bf16[512,1024]{1,0:T(8,128)(2,1)}, bf16[512,1024]{1,0:T(8,128)(2,1)S(1)}, u32[]{:S(2)}, u32[]{:S(2)}) %collective-permute-start.13) | collective-permute-done | bytes 1048608 | tf_op jit(solution)/shard_map/ppermute | solution.py:80
  82.7 0.9 collective-permute-done.16.refs_3_.refs_5_
  83.6 1.3 collective-permute-done.15.refs_2_.refs_4_
  84.8 1.0 copy-done.24
  85.9 9.2 %attend_last.1 = (bf16[256,512]{1,0:T(8,128)(2,1)}, bf16[256,512]{1,0:T(8,128)(2,1)}) custom-call(bf16[256,512]{1,0:T(8,128)(2,1)} %get-tuple-element.35.refs_0_, bf16[256,512]{1,0:T(8,128)(2,1)} %copy-done.25, bf16[512,1024]{1,0:T(8,128)(2,1)} %copy-done.24, bf16[512,1024]{1,0:T(8,128)(2,1)} %collective-permute-done.16.refs_3_.refs_5_, ...), custom_call_target="tpu_custom_call" | custom-call | flops 4294967296 | bytes 7864320 | tf_op jit(solution)/shard_map/attend_last/pallas_call | solution.py:253
  95.0 2.0 %collective-permute-done.21.refs_0_ = bf16[512,1024]{1,0:T(8,128)(2,1)S(1)} collective-permute-done((bf16[512,1024]{1,0:T(8,128)(2,1)S(1)}, bf16[512,1024]{1,0:T(8,128)(2,1)S(1)}, u32[]{:S(2)}, u32[]{:S(2)}) %collective-permute-start.21) | collective-permute-done | bytes 1048608 | tf_op jit(solution)/shard_map/ppermute | solution.py:84
  97.5 1.3 collective-permute-start.25
  98.8 1.8 %collective-permute-done.17.other_ref = bf16[256,512]{1,0:T(8,128)(2,1)S(1)} collective-permute-done((bf16[256,512]{1,0:T(8,128)(2,1)}, bf16[256,512]{1,0:T(8,128)(2,1)S(1)}, u32[]{:S(2)}, u32[]{:S(2)}) %collective-permute-start.17) | collective-permute-done | bytes 262176 | tf_op jit(solution)/shard_map/ppermute | solution.py:76
  100.6 0.7 copy-done
  101.3 3.2 %project_out.5 = (f32[128,1024]{1,0:T(8,128)}, bf16[128,1024]{1,0:T(8,128)(2,1)}) custom-call(s32[3]{0:T(128)} %pad_add_fusion.place_ref, bf16[256,512]{1,0:T(8,128)(2,1)} %get-tuple-element.47.mine_ref, bf16[256,512]{1,0:T(8,128)(2,1)} %copy-done, bf16[512,1024]{1,0:T(8,128)(2,1)} %copy-done.5, bf16[512,1024]{1,0:T(8,128)(2,1)} %collective-permute-done.22.refs_1_), custom_call_target="tpu_custom_call" | custom-call | flops 536870912 | bytes 2097152 | tf_op jit(solution)/shard_map/project_out/pallas_call | solution.py:306
  104.5 1.4 collective-permute-start.29
  105.9 3.2 %project_out.4 = (f32[128,1024]{1,0:T(8,128)}, bf16[128,1024]{1,0:T(8,128)(2,1)}) custom-call(s32[3]{0:T(128)} %pad_add_fusion.place_ref, bf16[256,512]{1,0:T(8,128)(2,1)} %get-tuple-element.47.mine_ref, bf16[256,512]{1,0:T(8,128)(2,1)} %copy-done, bf16[512,1024]{1,0:T(8,128)(2,1)} %refs_0_.3, bf16[512,1024]{1,0:T(8,128)(2,1)} %collective-permute-done.18.refs_1_), custom_call_target="tpu_custom_call" | custom-call | flops 536870912 | bytes 2097152 | tf_op jit(solution)/shard_map/project_out/pallas_call | solution.py:306
  109.5 1.6 collective-permute-start.23
  111.0 7.4 %collective-permute-done.19.refs_1_ = bf16[128,1024]{1,0:T(8,128)(2,1)S(1)} collective-permute-done((bf16[128,1024]{1,0:T(8,128)(2,1)}, bf16[128,1024]{1,0:T(8,128)(2,1)S(1)}, u32[]{:S(2)}, u32[]{:S(2)}) %collective-permute-start.19) | collective-permute-done | bytes 262176 | tf_op jit(solution)/shard_map/ppermute | solution.py:88
  118.5 1.1 add_convert_fusion.3
  119.6 1.3 collective-permute-start.20
  120.9 2.6 %collective-permute-done.23.refs_4_ = bf16[128,1024]{1,0:T(8,128)(2,1)S(1)} collective-permute-done((bf16[128,1024]{1,0:T(8,128)(2,1)}, bf16[128,1024]{1,0:T(8,128)(2,1)S(1)}, u32[]{:S(2)}, u32[]{:S(2)}) %collective-permute-start.23) | collective-permute-done | bytes 262176 | tf_op jit(solution)/shard_map/ppermute | solution.py:88
  123.5 0.7 add_convert_fusion.2
  124.3 2.6 %collective-permute-done.20.refs_2_ = bf16[64,1024]{1,0:T(8,128)(2,1)S(1)} collective-permute-done((bf16[64,1024]{1,0:T(8,128)(2,1)S(1)}, bf16[64,1024]{1,0:T(8,128)(2,1)S(1)}, u32[]{:S(2)}, u32[]{:S(2)}) %collective-permute-start.20) | collective-permute-done | bytes 131104 | tf_op jit(solution)/shard_map/ppermute | solution.py:88
  127.0 1.1 copy-done.8
  128.1 3.1 %project_out.6 = (f32[128,1024]{1,0:T(8,128)}, bf16[128,1024]{1,0:T(8,128)(2,1)}) custom-call(s32[3]{0:T(128)} %pad_add_fusion.place_ref, bf16[256,512]{1,0:T(8,128)(2,1)} %get-tuple-element.47.mine_ref, bf16[256,512]{1,0:T(8,128)(2,1)} %copy-done, bf16[512,1024]{1,0:T(8,128)(2,1)} %copy-done.6, bf16[512,1024]{1,0:T(8,128)(2,1)} %copy-done.8), custom_call_target="tpu_custom_call" | custom-call | flops 536870912 | bytes 2097152 | tf_op jit(solution)/shard_map/project_out/pallas_call | solution.py:306
  131.4 3.3 %project_out.7 = (f32[128,1024]{1,0:T(8,128)}, bf16[128,1024]{1,0:T(8,128)(2,1)}) custom-call(s32[3]{0:T(128)} %pad_add_fusion.place_ref, bf16[256,512]{1,0:T(8,128)(2,1)} %get-tuple-element.47.mine_ref, bf16[256,512]{1,0:T(8,128)(2,1)} %copy-done, bf16[512,1024]{1,0:T(8,128)(2,1)} %copy-done.7, bf16[512,1024]{1,0:T(8,128)(2,1)} %collective-permute-done.30.refs_1_), custom_call_target="tpu_custom_call" | custom-call | flops 536870912 | bytes 2097152 | tf_op jit(solution)/shard_map/project_out/pallas_call | solution.py:306
  134.7 1.9 %collective-permute-start.31 = (bf16[128,1024]{1,0:T(8,128)(2,1)}, bf16[128,1024]{1,0:T(8,128)(2,1)S(1)}, u32[]{:S(2)}, u32[]{:S(2)}) collective-permute-start(bf16[128,1024]{1,0:T(8,128)(2,1)} %get-tuple-element.62), channel_id=1, source_target_pairs={{0,1},{1,0},{2,3},{3,2},{4,5},{5,4},{6,7},{7,6},{8,9},{9,8},{10,11... | collective-permute-start | bytes 786440 | tf_op jit(solution)/shard_map/ppermute | solution.py:88
  136.6 0.8 collective-permute-start.24
  137.4 7.5 %collective-permute-done.27.refs_7_ = bf16[128,1024]{1,0:T(8,128)(2,1)S(1)} collective-permute-done((bf16[128,1024]{1,0:T(8,128)(2,1)}, bf16[128,1024]{1,0:T(8,128)(2,1)S(1)}, u32[]{:S(2)}, u32[]{:S(2)}) %collective-permute-start.27) | collective-permute-done | bytes 262176 | tf_op jit(solution)/shard_map/ppermute | solution.py:88
  145.0 5.0 %collective-permute-done.31.refs_10_ = bf16[128,1024]{1,0:T(8,128)(2,1)S(1)} collective-permute-done((bf16[128,1024]{1,0:T(8,128)(2,1)}, bf16[128,1024]{1,0:T(8,128)(2,1)S(1)}, u32[]{:S(2)}, u32[]{:S(2)}) %collective-permute-start.31) | collective-permute-done | bytes 262176 | tf_op jit(solution)/shard_map/ppermute | solution.py:88
  150.0 1.1 add_convert_fusion
  151.5 1.7 %collective-permute-done.28.refs_8_ = bf16[64,1024]{1,0:T(8,128)(2,1)S(1)} collective-permute-done((bf16[64,1024]{1,0:T(8,128)(2,1)S(1)}, bf16[64,1024]{1,0:T(8,128)(2,1)S(1)}, u32[]{:S(2)}, u32[]{:S(2)}) %collective-permute-start.28) | collective-permute-done | bytes 131104 | tf_op jit(solution)/shard_map/ppermute | solution.py:88
  153.2 6.1 %collective-permute-done.32.refs_11_ = bf16[64,1024]{1,0:T(8,128)(2,1)S(1)} collective-permute-done((bf16[64,1024]{1,0:T(8,128)(2,1)S(1)}, bf16[64,1024]{1,0:T(8,128)(2,1)S(1)}, u32[]{:S(2)}, u32[]{:S(2)}) %collective-permute-start.32) | collective-permute-done | bytes 131104 | tf_op jit(solution)/shard_map/ppermute | solution.py:88
  159.3 0.6 copy-done.22
  160.0 2.5 %add_up.1 = bf16[64,4096]{1,0:T(8,128)(2,1)} custom-call(s32[3]{0:T(128)} %pad_add_fusion.place_ref, f32[128,1024]{1,0:T(8,128)} %get-tuple-element.50.refs_0_, bf16[128,1024]{1,0:T(8,128)(2,1)} %copy-done.11, bf16[64,1024]{1,0:T(8,128)(2,1)} %copy-done.19, f32[128,1024]{1,0:T(8,128)} %get-tuple-element.53.refs_3_, bf16[128,1024]{1,0:T(8,128)(2,1)} %copy-done.12, ...), custom_call_target="tpu_custom_call" | custom-call | flops 524288 | bytes 2097152 | tf_op jit(solution)/shard_map/add_up/pallas_call | solution.py:347
  (86 shorter events, 6.0 us)
Async XLA Ops:
  0.0 31.3 %collective-permute-start.4 = (bf16[512,1024]{1,0:T(8,128)(2,1)}, bf16[512,1024]{1,0:T(8,128)(2,1)}, u32[]{:S(2)}, u32[]{:S(2)}) collective-permute-start(bf16[512,1024]{1,0:T(8,128)(2,1)} %refs_4_.1), channel_id=1, source_target_pairs={{0,8},{4,20},{8,0},{12,28},{16,24},{20,4},{24,16},{28,12},{1,9},{5... | collective-permute-start | bytes 3145736 | tf_op jit(solution)/shard_map/ppermute | solution.py:80
  2.9 28.3 %collective-permute-start.6 = (bf16[512,1024]{1,0:T(8,128)(2,1)}, bf16[512,1024]{1,0:T(8,128)(2,1)}, u32[]{:S(2)}, u32[]{:S(2)}) collective-permute-start(bf16[512,1024]{1,0:T(8,128)(2,1)} %refs_4_.1), channel_id=1, source_target_pairs={{0,16},{4,12},{8,24},{12,4},{16,0},{20,28},{24,8},{28,20},{1,17},{... | collective-permute-start | bytes 3145736 | tf_op jit(solution)/shard_map/ppermute | solution.py:84
  4.5 24.4 %collective-permute-start = (bf16[256,1024]{1,0:T(8,128)(2,1)}, bf16[256,1024]{1,0:T(8,128)(2,1)S(1)}, u32[]{:S(2)}, u32[]{:S(2)}) collective-permute-start(bf16[256,1024]{1,0:T(8,128)(2,1)} %refs_0_.2), channel_id=1, source_target_pairs={{0,1},{1,0},{2,3},{3,2},{4,5},{5,4},{6,7},{7,6},{8,9},{9,8},{10,11... | collective-permute-start | bytes 1572872 | tf_op jit(solution)/shard_map/ppermute | solution.py:88
  6.0 25.2 %collective-permute-start.1 = (bf16[256,1024]{1,0:T(8,128)(2,1)}, bf16[256,1024]{1,0:T(8,128)(2,1)S(1)}, u32[]{:S(2)}, u32[]{:S(2)}) collective-permute-start(bf16[256,1024]{1,0:T(8,128)(2,1)} %refs_0_.2), channel_id=1, source_target_pairs={{0,2},{1,3},{2,0},{3,1},{4,6},{5,7},{6,4},{7,5},{8,10},{9,11},{10,... | collective-permute-start | bytes 1572872 | tf_op jit(solution)/shard_map/ppermute | solution.py:88
  9.9 21.9 %collective-permute-start.11 = (bf16[256,1024]{1,0:T(8,128)(2,1)S(1)}, bf16[256,1024]{1,0:T(8,128)(2,1)S(1)}, u32[]{:S(2)}, u32[]{:S(2)}) collective-permute-start(bf16[256,1024]{1,0:T(8,128)(2,1)S(1)} %pad_maximum_fusion.1), channel_id=1, source_target_pairs={{0,4},{4,0},{8,12},{12,8},{16,20},{20,16},{24,28},{28,24},{1,5},{5... | collective-permute-start | bytes 1572872 | tf_op jit(solution)/shard_map/ppermute | solution.py:76
  31.3 15.3 %collective-permute-start.8 = (bf16[512,1024]{1,0:T(8,128)(2,1)}, bf16[512,1024]{1,0:T(8,128)(2,1)}, u32[]{:S(2)}, u32[]{:S(2)}) collective-permute-start(bf16[512,1024]{1,0:T(8,128)(2,1)} %collective-permute-done.6.refs_8_), channel_id=1, source_target_pairs={{0,8},{4,20},{8,0},{12,28},{16,24},{20,4},{24,16},{28,12},{1,9},{5... | collective-permute-start | bytes 3145736 | tf_op jit(solution)/shard_map/ppermute | solution.py:80
  32.2 25.2 %copy-start.4 = (bf16[512,1024]{1,0:T(8,128)(2,1)}, bf16[512,1024]{1,0:T(8,128)(2,1)S(1)}, u32[]{:S(2)}) copy-start(bf16[512,1024]{1,0:T(8,128)(2,1)S(1)} %pad_maximum_fusion.refs_2_.refs_4_) | copy-start | bytes 3145732
  32.2 14.9 %collective-permute-start.12 = (bf16[512,1024]{1,0:T(8,128)(2,1)S(1)}, bf16[512,1024]{1,0:T(8,128)(2,1)}, u32[]{:S(2)}, u32[]{:S(2)}) collective-permute-start(bf16[512,1024]{1,0:T(8,128)(2,1)S(1)} %pad_maximum_fusion.refs_2_.refs_4_), channel_id=1, source_target_pairs={{0,4},{4,0},{8,12},{12,8},{16,20},{20,16},{24,28},{28,24},{1,5},{5... | collective-permute-start | bytes 3145736 | tf_op jit(solution)/shard_map/ppermute | solution.py:76
  33.2 13.4 %collective-permute-start.2 = (bf16[256,1024]{1,0:T(8,128)(2,1)S(1)}, bf16[256,1024]{1,0:T(8,128)(2,1)S(1)}, u32[]{:S(2)}, u32[]{:S(2)}) collective-permute-start(bf16[256,1024]{1,0:T(8,128)(2,1)S(1)} %copy-done.17), channel_id=1, source_target_pairs={{0,1},{1,0},{2,3},{3,2},{4,5},{5,4},{6,7},{7,6},{8,9},{9,8},{10,11... | collective-permute-start | bytes 1572872 | tf_op jit(solution)/shard_map/ppermute | solution.py:88
  33.8 14.6 %collective-permute-start.3 = (bf16[512,1024]{1,0:T(8,128)(2,1)S(1)}, bf16[512,1024]{1,0:T(8,128)(2,1)S(1)}, u32[]{:S(2)}, u32[]{:S(2)}) collective-permute-start(bf16[512,1024]{1,0:T(8,128)(2,1)S(1)} %copy-done.9), channel_id=1, source_target_pairs={{0,4},{4,0},{8,12},{12,8},{16,20},{20,16},{24,28},{28,24},{1,5},{5... | collective-permute-start | bytes 3145736 | tf_op jit(solution)/shard_map/ppermute | solution.py:76
  33.8 16.9 %collective-permute-start.5 = (bf16[512,1024]{1,0:T(8,128)(2,1)}, bf16[512,1024]{1,0:T(8,128)(2,1)}, u32[]{:S(2)}, u32[]{:S(2)}) collective-permute-start(bf16[512,1024]{1,0:T(8,128)(2,1)} %collective-permute-done.4.refs_6_), channel_id=1, source_target_pairs={{0,4},{4,0},{8,12},{12,8},{16,20},{20,16},{24,28},{28,24},{1,5},{5... | collective-permute-start | bytes 3145736 | tf_op jit(solution)/shard_map/ppermute | solution.py:76
  46.6 4.5 %copy-start.18 = (bf16[256,1024]{1,0:T(8,128)(2,1)}, bf16[256,1024]{1,0:T(8,128)(2,1)S(1)}, u32[]{:S(2)}) copy-start(bf16[256,1024]{1,0:T(8,128)(2,1)S(1)} %collective-permute-done.2.refs_3_) | copy-start | bytes 1572868
  46.6 4.2 %collective-permute-start.7 = (bf16[512,1024]{1,0:T(8,128)(2,1)}, bf16[512,1024]{1,0:T(8,128)(2,1)}, u32[]{:S(2)}, u32[]{:S(2)}) collective-permute-start(bf16[512,1024]{1,0:T(8,128)(2,1)} %collective-permute-done.6.refs_8_), channel_id=1, source_target_pairs={{0,4},{4,0},{8,12},{12,8},{16,20},{20,16},{24,28},{28,24},{1,5},{5... | collective-permute-start | bytes 3145736 | tf_op jit(solution)/shard_map/ppermute | solution.py:76
  46.6 4.5 %collective-permute-start.9 = (bf16[512,1024]{1,0:T(8,128)(2,1)}, bf16[512,1024]{1,0:T(8,128)(2,1)}, u32[]{:S(2)}, u32[]{:S(2)}) collective-permute-start(bf16[512,1024]{1,0:T(8,128)(2,1)} %collective-permute-done.8.refs_10_), channel_id=1, source_target_pairs={{0,4},{4,0},{8,12},{12,8},{16,20},{20,16},{24,28},{28,24},{1,5},{5... | collective-permute-start | bytes 3145736 | tf_op jit(solution)/shard_map/ppermute | solution.py:76
  47.1 14.9 %collective-permute-start.14 = (bf16[512,1024]{1,0:T(8,128)(2,1)S(1)}, bf16[512,1024]{1,0:T(8,128)(2,1)}, u32[]{:S(2)}, u32[]{:S(2)}) collective-permute-start(bf16[512,1024]{1,0:T(8,128)(2,1)S(1)} %pad_maximum_fusion.refs_2_.refs_4_), channel_id=1, source_target_pairs={{0,8},{4,20},{8,0},{12,28},{16,24},{20,4},{24,16},{28,12},{1,9},{5... | collective-permute-start | bytes 3145736 | tf_op jit(solution)/shard_map/ppermute | solution.py:80
  49.4 32.8 %collective-permute-start.13 = (bf16[512,1024]{1,0:T(8,128)(2,1)}, bf16[512,1024]{1,0:T(8,128)(2,1)S(1)}, u32[]{:S(2)}, u32[]{:S(2)}) collective-permute-start(bf16[512,1024]{1,0:T(8,128)(2,1)} %collective-permute-done.12), channel_id=1, source_target_pairs={{0,8},{4,20},{8,0},{12,28},{16,24},{20,4},{24,16},{28,12},{1,9},{5... | collective-permute-start | bytes 3145736 | tf_op jit(solution)/shard_map/ppermute | solution.py:80
  57.4 5.1 %collective-permute-start.10 = (bf16[256,512]{1,0:T(8,128)(2,1)}, bf16[256,512]{1,0:T(8,128)(2,1)S(1)}, u32[]{:S(2)}, u32[]{:S(2)}) collective-permute-start(bf16[256,512]{1,0:T(8,128)(2,1)} %get-tuple-element.36), channel_id=1, source_target_pairs={{0,4},{4,0},{8,12},{12,8},{16,20},{20,16},{24,28},{28,24},{1,5},{5... | collective-permute-start | bytes 786440 | tf_op jit(solution)/shard_map/ppermute | solution.py:76
  62.0 20.2 %copy-start.3 = (bf16[512,1024]{1,0:T(8,128)(2,1)S(1)}, bf16[512,1024]{1,0:T(8,128)(2,1)}, u32[]{:S(2)}) copy-start(bf16[512,1024]{1,0:T(8,128)(2,1)} %refs_0_.3) | copy-start | bytes 3145732
  62.0 21.6 %collective-permute-start.16 = (bf16[512,1024]{1,0:T(8,128)(2,1)}, bf16[512,1024]{1,0:T(8,128)(2,1)}, u32[]{:S(2)}, u32[]{:S(2)}) collective-permute-start(bf16[512,1024]{1,0:T(8,128)(2,1)} %collective-permute-done.14.refs_3_.refs_5_), channel_id=1, source_target_pairs={{0,16},{4,12},{8,24},{12,4},{16,0},{20,28},{24,8},{28,20},{1,17},{... | collective-permute-start | bytes 3145736 | tf_op jit(solution)/shard_map/ppermute | solution.py:84
  82.2 2.7 %collective-permute-start.15 = (bf16[512,1024]{1,0:T(8,128)(2,1)S(1)}, bf16[512,1024]{1,0:T(8,128)(2,1)S(1)}, u32[]{:S(2)}, u32[]{:S(2)}) collective-permute-start(bf16[512,1024]{1,0:T(8,128)(2,1)S(1)} %collective-permute-done.13), channel_id=1, source_target_pairs={{0,4},{4,0},{8,12},{12,8},{16,20},{20,16},{24,28},{28,24},{1,5},{5... | collective-permute-start | bytes 3145736 | tf_op jit(solution)/shard_map/ppermute | solution.py:76
  82.2 14.8 %collective-permute-start.21 = (bf16[512,1024]{1,0:T(8,128)(2,1)S(1)}, bf16[512,1024]{1,0:T(8,128)(2,1)S(1)}, u32[]{:S(2)}, u32[]{:S(2)}) collective-permute-start(bf16[512,1024]{1,0:T(8,128)(2,1)S(1)} %copy-done.3), channel_id=1, source_target_pairs={{0,16},{4,12},{8,24},{12,4},{16,0},{20,28},{24,8},{28,20},{1,17},{... | collective-permute-start | bytes 3145736 | tf_op jit(solution)/shard_map/ppermute | solution.py:84
  97.0 3.6 %copy-start.5 = (bf16[512,1024]{1,0:T(8,128)(2,1)}, bf16[512,1024]{1,0:T(8,128)(2,1)S(1)}, u32[]{:S(2)}) copy-start(bf16[512,1024]{1,0:T(8,128)(2,1)S(1)} %collective-permute-done.21.refs_0_) | copy-start | bytes 3145732
  97.0 3.6 %collective-permute-start.22 = (bf16[512,1024]{1,0:T(8,128)(2,1)S(1)}, bf16[512,1024]{1,0:T(8,128)(2,1)}, u32[]{:S(2)}, u32[]{:S(2)}) collective-permute-start(bf16[512,1024]{1,0:T(8,128)(2,1)S(1)} %collective-permute-done.21.refs_0_), channel_id=1, source_target_pairs={{0,4},{4,0},{8,12},{12,8},{16,20},{20,16},{24,28},{28,24},{1,5},{5... | collective-permute-start | bytes 3145736 | tf_op jit(solution)/shard_map/ppermute | solution.py:76
  97.0 8.9 %collective-permute-start.18 = (bf16[512,1024]{1,0:T(8,128)(2,1)S(1)}, bf16[512,1024]{1,0:T(8,128)(2,1)}, u32[]{:S(2)}, u32[]{:S(2)}) collective-permute-start(bf16[512,1024]{1,0:T(8,128)(2,1)S(1)} %copy-done.3), channel_id=1, source_target_pairs={{0,4},{4,0},{8,12},{12,8},{16,20},{20,16},{24,28},{28,24},{1,5},{5... | collective-permute-start | bytes 3145736 | tf_op jit(solution)/shard_map/ppermute | solution.py:76
  97.5 3.1 %collective-permute-start.17 = (bf16[256,512]{1,0:T(8,128)(2,1)}, bf16[256,512]{1,0:T(8,128)(2,1)S(1)}, u32[]{:S(2)}, u32[]{:S(2)}) collective-permute-start(bf16[256,512]{1,0:T(8,128)(2,1)} %get-tuple-element.48), channel_id=1, source_target_pairs={{0,4},{4,0},{8,12},{12,8},{16,20},{20,16},{24,28},{28,24},{1,5},{5... | collective-permute-start | bytes 786440 | tf_op jit(solution)/shard_map/ppermute | solution.py:76
  97.5 23.4 %collective-permute-start.25 = (bf16[512,1024]{1,0:T(8,128)(2,1)S(1)}, bf16[512,1024]{1,0:T(8,128)(2,1)S(1)}, u32[]{:S(2)}, u32[]{:S(2)}) collective-permute-start(bf16[512,1024]{1,0:T(8,128)(2,1)S(1)} %copy-done.3), channel_id=1, source_target_pairs={{0,8},{4,20},{8,0},{12,28},{16,24},{20,4},{24,16},{28,12},{1,9},{5... | collective-permute-start | bytes 3145736 | tf_op jit(solution)/shard_map/ppermute | solution.py:80
  104.5 19.0 %copy-start.1 = (f32[128,1024]{1,0:T(8,128)S(1)}, f32[128,1024]{1,0:T(8,128)}, u32[]{:S(2)}) copy-start(f32[128,1024]{1,0:T(8,128)} %get-tuple-element.53.refs_3_) | copy-start | bytes 1572868
  104.5 22.4 %collective-permute-start.29 = (bf16[512,1024]{1,0:T(8,128)(2,1)}, bf16[512,1024]{1,0:T(8,128)(2,1)S(1)}, u32[]{:S(2)}, u32[]{:S(2)}) collective-permute-start(bf16[512,1024]{1,0:T(8,128)(2,1)} %copy-done.5), channel_id=1, source_target_pairs={{0,8},{4,20},{8,0},{12,28},{16,24},{20,4},{24,16},{28,12},{1,9},{5... | collective-permute-start | bytes 3145736 | tf_op jit(solution)/shard_map/ppermute | solution.py:80
  109.0 9.5 %collective-permute-start.19 = (bf16[128,1024]{1,0:T(8,128)(2,1)}, bf16[128,1024]{1,0:T(8,128)(2,1)S(1)}, u32[]{:S(2)}, u32[]{:S(2)}) collective-permute-start(bf16[128,1024]{1,0:T(8,128)(2,1)} %get-tuple-element.51), channel_id=1, source_target_pairs={{0,1},{1,0},{2,3},{3,2},{4,5},{5,4},{6,7},{7,6},{8,9},{9,8},{10,11... | collective-permute-start | bytes 786440 | tf_op jit(solution)/shard_map/ppermute | solution.py:88
  109.5 14.0 %collective-permute-start.23 = (bf16[128,1024]{1,0:T(8,128)(2,1)}, bf16[128,1024]{1,0:T(8,128)(2,1)S(1)}, u32[]{:S(2)}, u32[]{:S(2)}) collective-permute-start(bf16[128,1024]{1,0:T(8,128)(2,1)} %get-tuple-element.54), channel_id=1, source_target_pairs={{0,1},{1,0},{2,3},{3,2},{4,5},{5,4},{6,7},{7,6},{8,9},{9,8},{10,11... | collective-permute-start | bytes 786440 | tf_op jit(solution)/shard_map/ppermute | solution.py:88
  118.5 12.8 %copy-start.11 = (bf16[128,1024]{1,0:T(8,128)(2,1)}, bf16[128,1024]{1,0:T(8,128)(2,1)S(1)}, u32[]{:S(2)}) copy-start(bf16[128,1024]{1,0:T(8,128)(2,1)S(1)} %collective-permute-done.19.refs_1_) | copy-start | bytes 786436
  119.6 7.3 %collective-permute-start.20 = (bf16[64,1024]{1,0:T(8,128)(2,1)S(1)}, bf16[64,1024]{1,0:T(8,128)(2,1)S(1)}, u32[]{:S(2)}, u32[]{:S(2)}) collective-permute-start(bf16[64,1024]{1,0:T(8,128)(2,1)S(1)} %add_convert_fusion.3), channel_id=1, source_target_pairs={{0,2},{1,3},{2,0},{3,1},{4,6},{5,7},{6,4},{7,5},{8,10},{9,11},{10,... | collective-permute-start | bytes 393224 | tf_op jit(solution)/shard_map/ppermute | solution.py:88
  120.9 6.1 %copy-start.6 = (bf16[512,1024]{1,0:T(8,128)(2,1)}, bf16[512,1024]{1,0:T(8,128)(2,1)S(1)}, u32[]{:S(2)}) copy-start(bf16[512,1024]{1,0:T(8,128)(2,1)S(1)} %collective-permute-done.25.refs_0_) | copy-start | bytes 3145732
  120.9 6.1 %collective-permute-start.26 = (bf16[512,1024]{1,0:T(8,128)(2,1)S(1)}, bf16[512,1024]{1,0:T(8,128)(2,1)S(1)}, u32[]{:S(2)}, u32[]{:S(2)}) collective-permute-start(bf16[512,1024]{1,0:T(8,128)(2,1)S(1)} %collective-permute-done.25.refs_0_), channel_id=1, source_target_pairs={{0,4},{4,0},{8,12},{12,8},{16,20},{20,16},{24,28},{28,24},{1,5},{5... | collective-permute-start | bytes 3145736 | tf_op jit(solution)/shard_map/ppermute | solution.py:76
  126.9 24.2 %copy-start.19 = (bf16[64,1024]{1,0:T(8,128)(2,1)}, bf16[64,1024]{1,0:T(8,128)(2,1)S(1)}, u32[]{:S(2)}) copy-start(bf16[64,1024]{1,0:T(8,128)(2,1)S(1)} %collective-permute-done.20.refs_2_) | copy-start | bytes 393220
  126.9 4.4 %copy-start.7 = (bf16[512,1024]{1,0:T(8,128)(2,1)}, bf16[512,1024]{1,0:T(8,128)(2,1)S(1)}, u32[]{:S(2)}) copy-start(bf16[512,1024]{1,0:T(8,128)(2,1)S(1)} %collective-permute-done.29.refs_0_) | copy-start | bytes 3145732
  126.9 4.5 %collective-permute-start.30 = (bf16[512,1024]{1,0:T(8,128)(2,1)S(1)}, bf16[512,1024]{1,0:T(8,128)(2,1)}, u32[]{:S(2)}, u32[]{:S(2)}) collective-permute-start(bf16[512,1024]{1,0:T(8,128)(2,1)S(1)} %collective-permute-done.29.refs_0_), channel_id=1, source_target_pairs={{0,4},{4,0},{8,12},{12,8},{16,20},{20,16},{24,28},{28,24},{1,5},{5... | collective-permute-start | bytes 3145736 | tf_op jit(solution)/shard_map/ppermute | solution.py:76
  131.3 5.3 %copy-start.23 = (bf16[64,1024]{1,0:T(8,128)(2,1)S(1)}, bf16[64,1024]{1,0:T(8,128)(2,1)}, u32[]{:S(2)}) copy-start(bf16[64,1024]{1,0:T(8,128)(2,1)} %add_convert_fusion.2) | copy-start | bytes 393220
  131.3 13.6 %copy-start.2 = (f32[128,1024]{1,0:T(8,128)S(1)}, f32[128,1024]{1,0:T(8,128)}, u32[]{:S(2)}) copy-start(f32[128,1024]{1,0:T(8,128)} %get-tuple-element.57.refs_6_) | copy-start | bytes 1572868
  131.3 13.6 %collective-permute-start.27 = (bf16[128,1024]{1,0:T(8,128)(2,1)}, bf16[128,1024]{1,0:T(8,128)(2,1)S(1)}, u32[]{:S(2)}, u32[]{:S(2)}) collective-permute-start(bf16[128,1024]{1,0:T(8,128)(2,1)} %get-tuple-element.58), channel_id=1, source_target_pairs={{0,1},{1,0},{2,3},{3,2},{4,5},{5,4},{6,7},{7,6},{8,9},{9,8},{10,11... | collective-permute-start | bytes 786440 | tf_op jit(solution)/shard_map/ppermute | solution.py:88
  134.7 15.3 %collective-permute-start.31 = (bf16[128,1024]{1,0:T(8,128)(2,1)}, bf16[128,1024]{1,0:T(8,128)(2,1)S(1)}, u32[]{:S(2)}, u32[]{:S(2)}) collective-permute-start(bf16[128,1024]{1,0:T(8,128)(2,1)} %get-tuple-element.62), channel_id=1, source_target_pairs={{0,1},{1,0},{2,3},{3,2},{4,5},{5,4},{6,7},{7,6},{8,9},{9,8},{10,11... | collective-permute-start | bytes 786440 | tf_op jit(solution)/shard_map/ppermute | solution.py:88
  136.6 14.9 %collective-permute-start.24 = (bf16[64,1024]{1,0:T(8,128)(2,1)S(1)}, bf16[64,1024]{1,0:T(8,128)(2,1)S(1)}, u32[]{:S(2)}, u32[]{:S(2)}) collective-permute-start(bf16[64,1024]{1,0:T(8,128)(2,1)S(1)} %copy-done.23), channel_id=1, source_target_pairs={{0,2},{1,3},{2,0},{3,1},{4,6},{5,7},{6,4},{7,5},{8,10},{9,11},{10,... | collective-permute-start | bytes 393224 | tf_op jit(solution)/shard_map/ppermute | solution.py:88
  144.9 14.4 %copy-start.13 = (bf16[128,1024]{1,0:T(8,128)(2,1)}, bf16[128,1024]{1,0:T(8,128)(2,1)S(1)}, u32[]{:S(2)}) copy-start(bf16[128,1024]{1,0:T(8,128)(2,1)S(1)} %collective-permute-done.27.refs_7_) | copy-start | bytes 786436
  144.9 8.2 %collective-permute-start.28 = (bf16[64,1024]{1,0:T(8,128)(2,1)S(1)}, bf16[64,1024]{1,0:T(8,128)(2,1)S(1)}, u32[]{:S(2)}, u32[]{:S(2)}) collective-permute-start(bf16[64,1024]{1,0:T(8,128)(2,1)S(1)} %add_convert_fusion.1), channel_id=1, source_target_pairs={{0,2},{1,3},{2,0},{3,1},{4,6},{5,7},{6,4},{7,5},{8,10},{9,11},{10,... | collective-permute-start | bytes 393224 | tf_op jit(solution)/shard_map/ppermute | solution.py:88
  150.0 9.3 %copy-start.14 = (bf16[128,1024]{1,0:T(8,128)(2,1)}, bf16[128,1024]{1,0:T(8,128)(2,1)S(1)}, u32[]{:S(2)}) copy-start(bf16[128,1024]{1,0:T(8,128)(2,1)S(1)} %collective-permute-done.31.refs_10_) | copy-start | bytes 786436
  151.1 8.2 %collective-permute-start.32 = (bf16[64,1024]{1,0:T(8,128)(2,1)S(1)}, bf16[64,1024]{1,0:T(8,128)(2,1)S(1)}, u32[]{:S(2)}, u32[]{:S(2)}) collective-permute-start(bf16[64,1024]{1,0:T(8,128)(2,1)S(1)} %add_convert_fusion), channel_id=1, source_target_pairs={{0,2},{1,3},{2,0},{3,1},{4,6},{5,7},{6,4},{7,5},{8,10},{9,11},{10,... | collective-permute-start | bytes 393224 | tf_op jit(solution)/shard_map/ppermute | solution.py:88
  151.5 7.8 %copy-start.20 = (bf16[64,1024]{1,0:T(8,128)(2,1)}, bf16[64,1024]{1,0:T(8,128)(2,1)S(1)}, u32[]{:S(2)}) copy-start(bf16[64,1024]{1,0:T(8,128)(2,1)S(1)} %collective-permute-done.24.refs_5_) | copy-start | bytes 393220
  153.2 6.1 %copy-start.21 = (bf16[64,1024]{1,0:T(8,128)(2,1)}, bf16[64,1024]{1,0:T(8,128)(2,1)S(1)}, u32[]{:S(2)}) copy-start(bf16[64,1024]{1,0:T(8,128)(2,1)S(1)} %collective-permute-done.28.refs_8_) | copy-start | bytes 393220
  (11 other events, 15.6 us)

commit v3 on v0

--- a/solution.py
+++ b/solution.py
@@ -3,9 +3,14 @@
 import jax
 import jax.numpy as jnp
 from jax import lax
+from jax.experimental import pallas as pl
+from jax.experimental.pallas import tpu as pltpu
 from jax.sharding import PartitionSpec as P
 
 HEAD_DIM = 64
+PAIR = 2 * HEAD_DIM
+PAIRS_AT_ONCE = 2
+VMEM = 60 * 1024 * 1024
 
 
 def absorb(fold_state, query_heads, key_rows, value_rows):
@@ -29,7 +34,7 @@
     return (new_top, running_sum, weighted)
 
 
-def shards(decoder_states, w_query, w_out_t, enc_keys, enc_values):
+def gathered_shards(decoder_states, w_query, w_out_t, enc_keys, enc_values):
     query_full = lax.all_gather(w_query, "blk", axis=0, tiled=True)
     row_count = decoder_states.shape[0]
     columns = query_full.shape[1]
@@ -64,6 +69,401 @@
     ).astype(jnp.bfloat16)
 
 
+CORE = [(b, b ^ 1) for b in range(8)]
+CROSS = [(b, b ^ (2 if b % 2 == 0 else 4)) for b in range(8)]
+CROSS_BACK = [(b, b ^ (4 if b % 2 == 0 else 2)) for b in range(8)]
+
+def over_core(a):
+    return lax.ppermute(a, "blk", CORE)
+
+
+def cross(a):
+    return lax.ppermute(a, "blk", CROSS)
+
+
+def cross_back(a):
+    return lax.ppermute(a, "blk", CROSS_BACK)
+
+
+def over_z(a, step):
+    return lax.ppermute(a, "fsdp", [(z, z ^ step) for z in range(4)])
+
+
+def over_core_and_z(a, step):
+    pairs = [(b * 4 + z, (b ^ 1) * 4 + (z ^ step)) for b in range(8) for z in range(4)]
+    return lax.ppermute(a, ("blk", "fsdp"), pairs)
+
+
+def after(value, *earlier):
+    return lax.optimization_barrier((value,) + earlier)[0]
+
+
+OWN, NEAR, SIDE, FAR = (0, 0), (1, 2), (2, 1), (3, 3)
+
+
+def chip_of(place_ref, whose, core_step=0):
+    chip, core = place_ref[0], place_ref[1] ^ core_step
+    even, odd = whose
+    return chip ^ (even + core * (odd - even))
+
+
+def any_spec():
+    return pl.BlockSpec(memory_space=pl.ANY)
+
+
+def smem_spec():
+    return pl.BlockSpec(memory_space=pltpu.SMEM)
+
+
+def vmem_spec():
+    return pl.BlockSpec(memory_space=pltpu.VMEM)
+
+
+def project_queries(place, states, weights):
+    rows, depth = states[0].shape
+    columns = weights[0][1].shape[1]
+    shard = depth // 2
+
+    def kernel(place_ref, *refs):
+        state_refs = refs[: len(states)]
+        weight_refs = refs[len(states) : len(states) + len(weights)]
+        mine_ref, other_ref, state_s, weight_s, total, sems = refs[len(states) + len(weights) :]
+        core, plane = place_ref[1], place_ref[2]
+        chips = [chip_of(place_ref, whose) for whose, _ in weights]
+
+        def copy_states(which, n):
+            here = pl.ds(n // 4 * rows, rows)
+            sem = sems.at[n // 4, plane ^ (n % 4)] if which is None else sems.at[n // 4, which]
+            at = plane ^ (n % 4) if which is None else which
+            return pltpu.make_async_copy(state_refs[n], state_s.at[at, here], sem)
+
+        def copy_weights(n, part):
+            begin = pl.multiple_of((core ^ part) * shard, shard)
+            return pltpu.make_async_copy(
+                weight_refs[n].at[pl.ds(part * shard, shard)],
+                weight_s.at[chips[n], pl.ds(begin, shard)],
+                sems.at[2 + part, n],
+            )
+
+        for n in range(4):
+            copy_states(None, n).start()
+            copy_states(None, n + 4).start()
+            copy_weights(n, 0).start()
+            copy_weights(n, 1).start()
+        for n, chip_at in enumerate(chips):
+            copy_states(chip_at, 0).wait()
+            copy_states(chip_at, 4).wait()
+            copy_weights(n, 0).wait()
+            copy_weights(n, 1).wait()
+            part = jnp.dot(state_s[chip_at], weight_s[chip_at], preferred_element_type=jnp.float32)
+            total[...] = part if n == 0 else total[...] + part
+        factor = 1.0 / math.sqrt(HEAD_DIM)
+        for ref, first in ((mine_ref, 0), (other_ref, rows)):
+            queries = total[first : first + rows].astype(jnp.bfloat16)
+            ref[...] = (queries.astype(jnp.float32) * factor).astype(jnp.bfloat16)
+
+    shape = jax.ShapeDtypeStruct((rows, columns), jnp.bfloat16)
+    return pl.pallas_call(
+        kernel,
+        out_shape=(shape, shape),
+        in_specs=[smem_spec()] + [any_spec()] * (len(states) + len(weights)),
+        out_specs=(vmem_spec(), vmem_spec()),
+        scratch_shapes=[
+            pltpu.VMEM((4, 2 * rows, depth), jnp.bfloat16),
+            pltpu.VMEM((4, depth, columns), jnp.bfloat16),
+            pltpu.VMEM((2 * rows, columns), jnp.float32),
+            pltpu.SemaphoreType.DMA((4, 4)),
+        ],
+        compiler_params=pltpu.CompilerParams(vmem_limit_bytes=VMEM),
+        cost_estimate=pl.CostEstimate(
+            flops=4 * rows * 4 * depth * columns,
+            bytes_accessed=2 * 4 * depth * (2 * rows + columns),
+            transcendentals=0,
+        ),
+        name="project_queries",
+    )(place, *states, *[w[1] for w in weights])
+
+
+def pair_part(queries, keys, values):
+    rows = queries.shape[0]
+    first = lax.broadcasted_iota(jnp.int32, (rows, PAIR), 1) < HEAD_DIM
+    found = []
+    for head in range(2):
+        masked = jnp.where(first if head == 0 else jnp.logical_not(first), queries, 0)
+        scores = [
+            lax.dot_general(
+                masked, k, (((1,), (1,)), ((), ())), preferred_element_type=jnp.float32
+            )
+            for k in keys
+        ]
+        top = scores[0].max(axis=1, keepdims=True)
+        for s in scores[1:]:
+            top = jnp.maximum(top, s.max(axis=1, keepdims=True))
+        both = None
+        for s, v in zip(scores, values):
+            probability = jnp.exp(s - top).astype(jnp.bfloat16)
+            part = jnp.dot(probability, v, preferred_element_type=jnp.float32)
+            both = part if both is None else both + part
+        found.append((both[:, :PAIR], both[:, PAIR:], jnp.broadcast_to(top, (rows, PAIR))))
+    return [jnp.where(first, a, b) for a, b in zip(*found)]
+
+
+def attend(query_blocks, pieces, before=None):
+    rows, columns = query_blocks[0].shape
+    width = PAIRS_AT_ONCE * PAIR
+    steps = columns // width
+    blocks = len(query_blocks)
+    last = before is not None
+    held = [] if before is None else [a for block in before for a in block]
+    outs = 1 if last else 3 * blocks
+
+    def kernel(*refs):
+        refs = list(refs)
+        q_refs = [refs.pop(0) for _ in range(blocks)]
+        k_refs = [refs.pop(0) for _ in pieces]
+        v_refs = [refs.pop(0) for _ in pieces]
+        held_refs = [refs.pop(0) for _ in held]
+        out_refs = [refs.pop(0) for _ in range(outs)]
+        for pair in range(PAIRS_AT_ONCE):
+            at = slice(pair * PAIR, (pair + 1) * PAIR)
+            ks = [r[:, at] for r in k_refs]
+            ones = [jnp.ones((r.shape[0], PAIR), jnp.bfloat16) for r in v_refs]
+            vs = [jnp.concatenate([r[:, at], one], axis=1) for r, one in zip(v_refs, ones)]
+            for n in range(blocks):
+                weighted, sums, tops = pair_part(q_refs[n][:, at], ks, vs)
+                if last:
+                    weighted_0, sums_0, tops_0 = (r[:, at] for r in held_refs[3 * n : 3 * n + 3])
+                    top = jnp.maximum(tops, tops_0)
+                    now, then = jnp.exp(tops - top), jnp.exp(tops_0 - top)
+                    weighted = weighted * now + weighted_0 * then
+                    sums = sums * now + sums_0 * then
+                    out_refs[0][n, :, at] = (weighted / sums).astype(jnp.bfloat16)
+                else:
+                    for ref, a in zip(out_refs[3 * n : 3 * n + 3], (weighted, sums, tops)):
+                        ref[:, at] = a
+
+    def spec(a, skip=0):
+        return pl.BlockSpec((a.shape[0], width), lambda p: (0, p + skip))
+
+    args = list(query_blocks) + list(pieces) + list(pieces) + held
+    in_specs = (
+        [spec(a) for a in query_blocks]
+        + [spec(a) for a in pieces]
+        + [spec(a, steps) for a in pieces]
+        + [spec(a) for a in held]
+    )
+    out_shape = [jax.ShapeDtypeStruct((rows, columns), jnp.float32)] * outs
+    out_specs = [spec(a) for a in out_shape]
+    if last:
+        out_shape = [jax.ShapeDtypeStruct((blocks, rows, columns), jnp.bfloat16)]
+        out_specs = [pl.BlockSpec((blocks, rows, width), lambda p: (0, 0, p))]
+    total_keys = sum(a.shape[0] for a in pieces)
+    found = pl.pallas_call(
+        kernel,
+        grid=(steps,),
+        out_shape=out_shape,
+        in_specs=in_specs,
+        out_specs=out_specs,
+        compiler_params=pltpu.CompilerParams(vmem_limit_bytes=VMEM),
+        cost_estimate=pl.CostEstimate(
+            flops=2 * 2 * blocks * rows * total_keys * columns * 4,
+            bytes_accessed=sum(a.size * a.dtype.itemsize for a in args),
+            transcendentals=blocks * rows * total_keys * (columns // HEAD_DIM),
+        ),
+        name="attend_last" if last else "attend_first",
+    )(*args)
+    if last:
+        return found[0]
+    return [found[3 * n : 3 * n + 3] for n in range(blocks)]
+
+
+def project_out(place, mine, got, weights, tiles=2):
+    blocks, rows, half = mine.shape
+    quarter = rows // 4
+    tile = weights.shape[0] // tiles
+    held = blocks * rows // 2
+
+    def kernel(place_ref, mine_ref, got_ref, weight_ref, kept_ref, sent_ref, context):
+        core, plane = place_ref[1], place_ref[2]
+
+        @pl.when(pl.program_id(0) == 0)
+        def _():
+            for n, step in enumerate((0, 2, 1, 3)):
+                begin = pl.ds(pl.multiple_of((plane ^ step) * quarter, quarter), quarter)
+                for i in range(blocks):
+                    here = pl.ds((n * blocks + i) * quarter, quarter)
+                    lanes = pl.ds(pl.multiple_of(core * half, half), half)
+                    context[here, lanes] = mine_ref[i, begin]
+                    lanes = pl.ds(pl.multiple_of((1 - core) * half, half), half)
+                    context[here, lanes] = got_ref[1 - i, begin]
+
+        part = lax.dot_general(
+            context[...],
+            weight_ref[...],
+            (((1,), (1,)), ((), ())),
+            preferred_element_type=jnp.float32,
+        )
+        kept_ref[...] = part[:held]
+        sent_ref[...] = part[held:].astype(jnp.bfloat16)
+
+    def whole(a):
+        return pl.BlockSpec(a.shape, lambda t: (0, 0, 0))
+
+    return pl.pallas_call(
+        kernel,
+        grid=(tiles,),
+        out_shape=[
+            jax.ShapeDtypeStruct((held, tiles * tile), kind) for kind in (jnp.float32, jnp.bfloat16)
+        ],
+        in_specs=[
+            smem_spec(),
+            whole(mine),
+            whole(got),
+            pl.BlockSpec((tile, 2 * half), lambda t: (t, 0)),
+        ],
+        out_specs=[pl.BlockSpec((held, tile), lambda t: (0, t))] * 2,
+        scratch_shapes=[pltpu.VMEM((2 * held, 2 * half), jnp.bfloat16)],
+        compiler_params=pltpu.CompilerParams(vmem_limit_bytes=VMEM),
+        cost_estimate=pl.CostEstimate(
+            flops=2 * 2 * held * 2 * half * tile * tiles,
+            bytes_accessed=2 * tile * tiles * 2 * half,
+            transcendentals=0,
+        ),
+        name="project_out",
+    )(place, mine, got, weights)
+
+
+def add_up(groups):
+    rows, width = groups[0][2].shape
+    rows //= 2
+
+    def kernel(*refs):
+        own_ref, other_ref = refs[-2:]
+        for n in range(len(groups)):
+            kept_ref, first_ref, second_ref = refs[3 * n : 3 * n + 3]
+            total = kept_ref[...] + first_ref[...].astype(jnp.float32)
+            total = (total + second_ref[...].astype(jnp.float32)).astype(jnp.bfloat16)
+            here = slice(n * width, (n + 1) * width)
+            own_ref[:, here] = total[:rows]
+            other_ref[:, here] = total[rows:]
+
+    args = [a for group in groups for a in group]
+    shape = jax.ShapeDtypeStruct((rows, len(groups) * width), jnp.bfloat16)
+    return pl.pallas_call(
+        kernel,
+        grid=(1,),
+        out_shape=(shape, shape),
+        in_specs=[pl.BlockSpec((2 * rows, width), lambda t: (0, 0))] * len(args),
+        out_specs=[pl.BlockSpec(shape.shape, lambda t: (0, 0))] * 2,
+        compiler_params=pltpu.CompilerParams(vmem_limit_bytes=VMEM),
+        cost_estimate=pl.CostEstimate(
+            flops=4 * rows * shape.shape[1],
+            bytes_accessed=20 * rows * shape.shape[1],
+            transcendentals=0,
+        ),
+        name="add_up",
+    )(*args)
+
+
+def put_in_place(place, chips, mine, got, last):
+    rows = mine.shape[0]
+    shard = mine.shape[1] // (len(chips) - 1)
+
+    def kernel(place_ref, *refs):
+        out_ref = refs[-1]
+        for n, whose in enumerate(chips):
+            for core_step in range(2):
+                if n < len(chips) - 1:
+                    value = refs[core_step][:, n * shard : (n + 1) * shard]
+                else:
+                    near_ref, away_ref = refs[2 + 2 * core_step : 4 + 2 * core_step]
+                    value = near_ref[...] + away_ref[...].astype(jnp.float32)
+                at = chip_of(place_ref, whose, core_step) * 2 + (place_ref[1] ^ core_step)
+                begin = pl.multiple_of(at * shard, shard)
+                out_ref[:, pl.ds(begin, shard)] = value.astype(jnp.bfloat16)
+
+    args = [mine, got, *last]
+    return pl.pallas_call(
+        kernel,
+        out_shape=jax.ShapeDtypeStruct((rows, 8 * shard), jnp.bfloat16),
+        in_specs=[smem_spec()] + [vmem_spec()] * len(args),
+        out_specs=vmem_spec(),
+        compiler_params=pltpu.CompilerParams(vmem_limit_bytes=VMEM),
+        cost_estimate=pl.CostEstimate(
+            flops=0, bytes_accessed=4 * rows * 8 * shard, transcendentals=0
+        ),
+        name="put_in_place",
+    )(place, *args)
+
+
+def plane_shards(decoder_states, w_query, w_out_t, enc_keys, enc_values):
+    block, plane = lax.axis_index("blk"), lax.axis_index("fsdp")
+    core = block % 2
+    place = jnp.stack([block // 2, core, plane]).astype(jnp.int32)
+    shard, rows = w_query.shape[0], enc_keys.shape[0]
+
+    def half_of(a, which):
+        width = a.shape[1] // 2
+        return lax.dynamic_slice_in_dim(a, which * width, width, 1)
+
+    def whole_rows(a, got):
+        return jnp.concatenate([half_of(a, core), got])
+
+    def add_passed(sums, first):
+        begin = sums[0].shape[0] // 2
+        return (sums[0][begin:] + first[begin:].astype(jnp.float32)).astype(jnp.bfloat16)
+
+    def totals(sums, first):
+        own, other, same, crossed = jnp.split(sums[0] + first.astype(jnp.float32), 4)
+        return own, other, same.astype(jnp.bfloat16), crossed.astype(jnp.bfloat16)
+
+    states_1 = over_z(decoder_states, 1)
+    states_2 = over_z(decoder_states, 2)
+    states_3 = over_z(states_2, 1)
+    others = over_core(decoder_states)
+    others_1 = over_core(after(states_1, others))
+    others_2 = over_core(after(states_2, others_1))
+    others_3 = over_core(after(states_3, others_2))
+    to_swap = jnp.concatenate([half_of(a, 1 - core) for a in (w_query, enc_keys, enc_values)])
+    swapped = over_core(to_swap)
+    weights = jnp.concatenate([half_of(w_query, core), swapped[:shard]])
+    near_weights = cross(weights)
+    side_weights = cross_back(weights)
+    far_weights = cross_back(after(near_weights, near_weights, side_weights, states_1, states_2))
+    queries = project_queries(place, [decoder_states, states_1, states_2, states_3, others, others_1, others_2, others_3], [(OWN, weights), (NEAR, near_weights), (SIDE, side_weights), (FAR, far_weights)])
+    encoded = jnp.concatenate([whole_rows(enc_keys, swapped[shard:-rows]), whole_rows(enc_values, swapped[-rows:])], axis=1)
+    near_encoded = cross(after(encoded, states_1))
+    before = attend(queries, [encoded, near_encoded])
+    side_encoded = cross_back(after(encoded, states_1, states_2, others_1))
+    far_encoded = cross_back(near_encoded)
+    context = attend(queries, [side_encoded, far_encoded], before)
+    context_got = over_core(context)
+    sums_0 = project_out(place, context, context_got, w_out_t)
+    first_0 = over_z(sums_0[1], 1)
+    near_out = cross(after(w_out_t, context))
+    passed_0 = add_passed(after(sums_0, context_got, near_out), first_0)
+    side_out = cross_back(after(w_out_t, before))
+    sums_1 = project_out(place, after(context, sums_0), context_got, side_out)
+    first_1 = over_z(sums_1[1], 1)
+    second_0 = over_z(after(passed_0, first_1), 2)
+    passed_1 = add_passed(sums_1, first_1)
+    second_1 = over_z(passed_1, 2)
+    sums_2 = project_out(place, after(context, sums_1), context_got, near_out)
+    first_2 = over_z(sums_2[1], 1)
+    far_out = cross(side_out)
+    passed_2 = add_passed(after(sums_2, far_out), first_2)
+    second_2 = over_z(passed_2, 2)
+    most_added = add_up([(sums_0[0], first_0, second_0), (sums_1[0], first_1, second_1), (sums_2[0], first_2, second_2)])
+    most_got = over_core(most_added[1])
+    sums_3 = project_out(place, after(context, sums_2), context_got, far_out)
+    first_3 = over_z(sums_3[1], 1)
+    passed_3 = totals(sums_3, first_3)
+    second_3 = over_z(passed_3[2], 2)
+    last_got = over_core(passed_3[1])
+    third_3 = over_core_and_z(after(passed_3, first_2)[3], 2)
+    return put_in_place(place, (OWN, SIDE, NEAR, FAR), most_added[0], most_got, (passed_3[0], second_3, last_got, third_3))
+
+
 def solution(mesh):
     in_specs = (
         P("blk", "fsdp"),
@@ -73,4 +473,11 @@
         P("blk", "fsdp"),
     )
     out_specs = P(("blk", "fsdp"), None)
-    return jax.shard_map(shards, mesh=mesh, in_specs=in_specs, out_specs=out_specs, check_vma=False)
+    by_planes = mesh.shape["blk"] == 8 and mesh.shape["fsdp"] == 4
+    return jax.shard_map(
+        plane_shards if by_planes else gathered_shards,
+        mesh=mesh,
+        in_specs=in_specs,
+        out_specs=out_specs,
+        check_vma=False,
+    )

time: 340 us -> 144 us (0.42)
  waiting for transfers between devices: 250 us -> 59.5 us
  matrix products: 45.4 us -> 0 us
  Pallas kernels: 0 us -> 39.3 us
  starting transfers between devices: 0.19 us -> 35.4 us
  other arithmetic: 17.2 us -> 2.22 us
  between operations: 13.5 us -> 0.26 us
  local copies, waits for them, and re-layouts: 13.2 us -> 6.87 us
    all_gather x5 -> x0, waiting for transfers between devices: 170 us -> none  [the longest x1 54.9 us: shards(): query_full = lax.all_gather(w_query, 'blk', axis=0, tiled=True)]
    reduce_scatter x1 -> x0, waiting for transfers between devices: 76.9 us -> none  [shards(): lax.psum_scatter(lax.dot_general(context, out_full, (((1,), (1,)), ((), (...]
    ppermute x0 -> x29, waiting for transfers between devices: none -> 59.5 us  [the longest x11 45 us: over_z(): return lax.ppermute(a, 'fsdp', [(z, z ^ step) for z in range(4)])]
    dot_general x4 -> x0, matrix products: 45.4 us -> none  [the longest x1 15.7 us: absorb(): jnp.einsum('hqk,khd->hqd', probability.astype(jnp.bfloat16), value_heads,...]
    pallas_call x0 -> x9, Pallas kernels: none -> 39.3 us  [the longest x2 16.8 us: attend(): pl.pallas_call(kernel, grid=(steps,), out_shape=out_shape, in_specs=in_sp...]
    ppermute x0 -> x29, starting transfers between devices: none -> 35.4 us  [the longest x11 18.9 us: over_z(): return lax.ppermute(a, 'fsdp', [(z, z ^ step) for z in range(4)])]
    reduce_sum x1 -> x0, other arithmetic: 15.1 us -> none  [absorb(): running_sum = running_sum * rescale + jnp.sum(probability, axis=2)]
    all_gather x2 -> x0, local copies, waits for them, and re-layouts: 13 us -> none  [the longest x1 6.53 us: shards(): lax.all_gather(enc_keys, 'blk', axis=0, tiled=True)]
  transfers between devices with their start and end apart: 6 -> 29, of which waited for: 6 -> 14; matrix products, arithmetic and copies ran while one was open for 19% -> 2% of each run, Pallas kernels for 0% -> 26%
where the time goes in v3:
time: 144 us; the launch traced here: 143 us
  waiting for transfers between devices  59.5 us (41%)
  Pallas kernels  39.3 us (27%)
  starting transfers between devices  35.4 us (25%)
  local copies, waits for them, and re-layouts  6.87 us (5%)
  other arithmetic  2.22 us (2%)
    ppermute x11, waiting for transfers between devices, over_z(): return lax.ppermute(a, 'fsdp', [(z, z ^ step) for z in range(4)])  45 us
    ppermute x11, starting transfers between devices, over_z(): return lax.ppermute(a, 'fsdp', [(z, z ^ step) for z in range(4)])  18.9 us
    pallas_call x2, Pallas kernels, attend(): pl.pallas_call(kernel, grid=(steps,), out_shape=out_shape, in_specs=in_sp...  16.8 us
    pallas_call x4, Pallas kernels, project_out(): pl.pallas_call(kernel, grid=(tiles,), out_shape=[jax.ShapeDtypeStruct((he...  12.6 us
    ppermute x4, starting transfers between devices, cross(): return lax.ppermute(a, 'blk', CROSS)  7.95 us
    ppermute x5, waiting for transfers between devices, cross_back(): return lax.ppermute(a, 'blk', CROSS_BACK)  7.86 us
    ppermute x5, starting transfers between devices, cross_back(): return lax.ppermute(a, 'blk', CROSS_BACK)  7.33 us
    pallas_call x1, Pallas kernels, project_queries(): pl.pallas_call(kernel, out_shape=(shape, shape), in_specs=[smem_spec()] +...  5.64 us
  transfers between devices with their start and end apart: 29, of which 14 were waited for; matrix products, arithmetic and copies ran while one was open for 2% of the time, Pallas kernels for 26%

profile of v3, /device:TPU:0, one launch (start us, length us, event | category | flops | bytes accessed | tf_op | source)
XLA Modules:
  0.0 143.5 jit_solution(9700899224083090709)
XLA Ops:
  0.0 1.4 constant_dynamic-slice_fusion.5
  2.7 3.0 %collective-permute-start = (bf16[256,1024]{1,0:T(8,128)(2,1)S(1)}, bf16[256,1024]{1,0:T(8,128)(2,1)S(1)}, u32[]{:S(2)}, u32[]{:S(2)}) collective-permute-start(bf16[256,1024]{1,0:T(8,128)(2,1)S(1)} %copy-done.13), channel_id=1, source_target_pairs={{0,1},{1,0},{2,3},{3,2},{4,5},{5,4},{6,7},{7,6},{8,9},{9,8},{10,11... | collective-permute-start | bytes 1572872 | tf_op jit(solution)/shard_map/ppermute | solution.py:89
  5.8 1.7 %collective-permute-start.8 = (bf16[1024,512]{1,0:T(8,128)(2,1)S(1)}, bf16[1024,512]{1,0:T(8,128)(2,1)S(1)}, u32[]{:S(2)}, u32[]{:S(2)}) collective-permute-start(bf16[1024,512]{1,0:T(8,128)(2,1)S(1)} %pad_maximum_fusion.1.refs_8_), channel_id=1, source_target_pairs={{0,8},{4,20},{8,0},{12,28},{16,24},{20,4},{24,16},{28,12},{1,9},{5... | collective-permute-start | bytes 3145736 | tf_op jit(solution)/shard_map/ppermute | solution.py:81
  7.6 1.5 %collective-permute-start.9 = (bf16[1024,512]{1,0:T(8,128)(2,1)S(1)}, bf16[1024,512]{1,0:T(8,128)(2,1)S(1)}, u32[]{:S(2)}, u32[]{:S(2)}) collective-permute-start(bf16[1024,512]{1,0:T(8,128)(2,1)S(1)} %pad_maximum_fusion.1.refs_8_), channel_id=1, source_target_pairs={{0,16},{4,12},{8,24},{12,4},{16,0},{20,28},{24,8},{28,20},{1,17},{... | collective-permute-start | bytes 3145736 | tf_op jit(solution)/shard_map/ppermute | solution.py:85
  9.1 2.6 %collective-permute-start.1 = (bf16[256,1024]{1,0:T(8,128)(2,1)S(1)}, bf16[256,1024]{1,0:T(8,128)(2,1)S(1)}, u32[]{:S(2)}, u32[]{:S(2)}) collective-permute-start(bf16[256,1024]{1,0:T(8,128)(2,1)S(1)} %copy-done.13), channel_id=1, source_target_pairs={{0,2},{1,3},{2,0},{3,1},{4,6},{5,7},{6,4},{7,5},{8,10},{9,11},{10,... | collective-permute-start | bytes 1572872 | tf_op jit(solution)/shard_map/ppermute | solution.py:89
  11.7 13.4 %collective-permute-done.refs_1_ = bf16[256,1024]{1,0:T(8,128)(2,1)S(1)} collective-permute-done((bf16[256,1024]{1,0:T(8,128)(2,1)S(1)}, bf16[256,1024]{1,0:T(8,128)(2,1)S(1)}, u32[]{:S(2)}, u32[]{:S(2)}) %collective-permute-start) | collective-permute-done | bytes 524320 | tf_op jit(solution)/shard_map/ppermute | solution.py:89
  25.3 1.3 maximum_maximum_fusion.refs_2_.refs_4_
  26.5 2.7 %collective-permute-start.12 = (bf16[512,1024]{1,0:T(8,128)(2,1)}, bf16[512,1024]{1,0:T(8,128)(2,1)}, u32[]{:S(2)}, u32[]{:S(2)}) collective-permute-start(bf16[512,1024]{1,0:T(8,128)(2,1)} %maximum_maximum_fusion.refs_2_.refs_4_), channel_id=1, source_target_pairs={{0,8},{4,20},{8,0},{12,28},{16,24},{20,4},{24,16},{28,12},{1,9},{5... | collective-permute-start | bytes 3145736 | tf_op jit(solution)/shard_map/ppermute | solution.py:81
  29.2 5.7 %collective-permute-done.1.refs_2_ = bf16[256,1024]{1,0:T(8,128)(2,1)S(1)} collective-permute-done((bf16[256,1024]{1,0:T(8,128)(2,1)S(1)}, bf16[256,1024]{1,0:T(8,128)(2,1)S(1)}, u32[]{:S(2)}, u32[]{:S(2)}) %collective-permute-start.1) | collective-permute-done | bytes 524320 | tf_op jit(solution)/shard_map/ppermute | solution.py:89
  36.2 11.6 %collective-permute-done.2.refs_3_ = bf16[256,1024]{1,0:T(8,128)(2,1)} collective-permute-done((bf16[256,1024]{1,0:T(8,128)(2,1)S(1)}, bf16[256,1024]{1,0:T(8,128)(2,1)}, u32[]{:S(2)}, u32[]{:S(2)}) %collective-permute-start.2) | collective-permute-done | bytes 524320 | tf_op jit(solution)/shard_map/ppermute | solution.py:89
  47.8 0.7 copy-done.18
  49.0 2.3 %collective-permute-start.13 = (bf16[512,1024]{1,0:T(8,128)(2,1)}, bf16[512,1024]{1,0:T(8,128)(2,1)}, u32[]{:S(2)}, u32[]{:S(2)}) collective-permute-start(bf16[512,1024]{1,0:T(8,128)(2,1)} %collective-permute-done.12.refs_3_.refs_5_), channel_id=1, source_target_pairs={{0,16},{4,12},{8,24},{12,4},{16,0},{20,28},{24,8},{28,20},{1,17},{... | collective-permute-start | bytes 3145736 | tf_op jit(solution)/shard_map/ppermute | solution.py:85
  51.3 0.7 pad_add_fusion.place_ref
  52.0 1.9 %collective-permute-done.10.refs_11_ = bf16[1024,512]{1,0:T(8,128)(2,1)S(1)} collective-permute-done((bf16[1024,512]{1,0:T(8,128)(2,1)S(1)}, bf16[1024,512]{1,0:T(8,128)(2,1)S(1)}, u32[]{:S(2)}, u32[]{:S(2)}) %collective-permute-start.10) | collective-permute-done | bytes 1048608 | tf_op jit(solution)/shard_map/ppermute | solution.py:85
  53.9 1.1 copy-done.7
  55.0 5.6 %project_queries.1 = (bf16[256,512]{1,0:T(8,128)(2,1)}, bf16[256,512]{1,0:T(8,128)(2,1)}) custom-call(s32[3]{0:T(128)} %pad_add_fusion.place_ref, bf16[256,1024]{1,0:T(8,128)(2,1)} %refs_0_.1, bf16[256,1024]{1,0:T(8,128)(2,1)} %copy-done.14, bf16[256,1024]{1,0:T(8,128)(2,1)} %copy-done.16, bf16[256,1024]{1,0:T(8,128)(2,1)} %collective-permute-done.2.refs_3_, ...), custom_call_target="tpu_custom_call" | custom-call | flops 2147483648 | bytes 8388608 | tf_op jit(solution)/shard_map/project_queries/pallas_call | solution.py:166
  60.6 8.3 %attend_first.1 = (f32[256,512]{1,0:T(8,128)}, f32[256,512]{1,0:T(8,128)}, f32[256,512]{1,0:T(8,128)}, f32[256,512]{1,0:T(8,128)}, f32[256,512]{1,0:T(8,128)}, /*index=5*/f32[256,512]{1,0:T(8,128)}) custom-call(bf16[256,512]{1,0:T(8,128)(2,1)} %get-tuple-element.42.refs_0_, bf16[256,512]{1,0:T(8,128)(2,1)} %get-tuple-element.43.refs_1_, ...), custom_call_target="tpu_custom_call" | custom-call | flops 4294967296 | bytes 4718592 | tf_op jit(solution)/shard_map/attend_first/pallas_call | solution.py:261
  68.9 2.5 %collective-permute-start.17 = (bf16[512,1024]{1,0:T(8,128)(2,1)S(1)}, bf16[512,1024]{1,0:T(8,128)(2,1)S(1)}, u32[]{:S(2)}, u32[]{:S(2)}) collective-permute-start(bf16[512,1024]{1,0:T(8,128)(2,1)S(1)} %copy-done.8), channel_id=1, source_target_pairs={{0,16},{4,12},{8,24},{12,4},{16,0},{20,28},{24,8},{28,20},{1,17},{... | collective-permute-start | bytes 3145736 | tf_op jit(solution)/shard_map/ppermute | solution.py:85
  71.4 5.1 %collective-permute-done.13.refs_3_.refs_5_ = bf16[512,1024]{1,0:T(8,128)(2,1)} collective-permute-done((bf16[512,1024]{1,0:T(8,128)(2,1)}, bf16[512,1024]{1,0:T(8,128)(2,1)}, u32[]{:S(2)}, u32[]{:S(2)}) %collective-permute-start.13) | collective-permute-done | bytes 1048608 | tf_op jit(solution)/shard_map/ppermute | solution.py:85
  76.5 8.5 %attend_last.1.mine_ref = bf16[2,256,512]{2,1,0:T(8,128)(2,1)} custom-call(bf16[256,512]{1,0:T(8,128)(2,1)} %get-tuple-element.42.refs_0_, bf16[256,512]{1,0:T(8,128)(2,1)} %get-tuple-element.43.refs_1_, bf16[512,1024]{1,0:T(8,128)(2,1)} %collective-permute-done.11.refs_2_.refs_4_, bf16[512,1024]{1,0:T(8,128)(2,1)} %collective-permute-done.13.refs_3_.refs_5_, ...), custom_call_target="tpu_custom_call" | custom-call | flops 4294967296 | bytes 7864320 | tf_op jit(solution)/shard_map/attend_last/pallas_call | solution.py:261
  85.0 1.8 %collective-permute-start.16 = (bf16[512,1024]{1,0:T(8,128)(2,1)S(1)}, bf16[512,1024]{1,0:T(8,128)(2,1)}, u32[]{:S(2)}, u32[]{:S(2)}) collective-permute-start(bf16[512,1024]{1,0:T(8,128)(2,1)S(1)} %copy-done.8), channel_id=1, source_target_pairs={{0,8},{4,20},{8,0},{12,28},{16,24},{20,4},{24,16},{28,12},{1,9},{5... | collective-permute-start | bytes 3145736 | tf_op jit(solution)/shard_map/ppermute | solution.py:81
  86.8 0.8 collective-permute-done.17.weight_ref
  87.6 1.7 %collective-permute-start.22 = (bf16[512,1024]{1,0:T(8,128)(2,1)S(1)}, bf16[512,1024]{1,0:T(8,128)(2,1)}, u32[]{:S(2)}, u32[]{:S(2)}) collective-permute-start(bf16[512,1024]{1,0:T(8,128)(2,1)S(1)} %collective-permute-done.17.weight_ref), channel_id=1, source_target_pairs={{0,8},{4,20},{8,0},{12,28},{16,24},{20,4},{24,16},{28,12},{1,9},{5... | collective-permute-start | bytes 3145736 | tf_op jit(solution)/shard_map/ppermute | solution.py:81
  89.4 0.8 copy-done
  90.2 3.2 %project_out.4 = (f32[256,512]{1,0:T(8,128)}, bf16[256,512]{1,0:T(8,128)(2,1)}) custom-call(s32[3]{0:T(128)} %pad_add_fusion.place_ref, bf16[2,256,512]{2,1,0:T(8,128)(2,1)} %attend_last.1.mine_ref, bf16[2,256,512]{2,1,0:T(8,128)(2,1)} %copy-done, bf16[512,1024]{1,0:T(8,128)(2,1)} %weight_ref.1), custom_call_target="tpu_custom_call" | custom-call | flops 536870912 | bytes 1048576 | tf_op jit(solution)/shard_map/project_out/pallas_call | solution.py:312
  93.3 1.1 collective-permute-start.15
  94.5 3.1 %project_out.5 = (f32[256,512]{1,0:T(8,128)}, bf16[256,512]{1,0:T(8,128)(2,1)}) custom-call(s32[3]{0:T(128)} %pad_add_fusion.place_ref, bf16[2,256,512]{2,1,0:T(8,128)(2,1)} %attend_last.1.mine_ref, bf16[2,256,512]{2,1,0:T(8,128)(2,1)} %copy-done, bf16[512,1024]{1,0:T(8,128)(2,1)} %copy-done.9), custom_call_target="tpu_custom_call" | custom-call | flops 536870912 | bytes 1048576 | tf_op jit(solution)/shard_map/project_out/pallas_call | solution.py:312
  97.6 0.9 collective-permute-start.18
  98.5 1.5 %collective-permute-done.16.weight_ref = bf16[512,1024]{1,0:T(8,128)(2,1)} collective-permute-done((bf16[512,1024]{1,0:T(8,128)(2,1)S(1)}, bf16[512,1024]{1,0:T(8,128)(2,1)}, u32[]{:S(2)}, u32[]{:S(2)}) %collective-permute-start.16) | collective-permute-done | bytes 1048608 | tf_op jit(solution)/shard_map/ppermute | solution.py:81
  100.0 3.1 %project_out.6 = (f32[256,512]{1,0:T(8,128)}, bf16[256,512]{1,0:T(8,128)(2,1)}) custom-call(s32[3]{0:T(128)} %pad_add_fusion.place_ref, bf16[2,256,512]{2,1,0:T(8,128)(2,1)} %attend_last.1.mine_ref, bf16[2,256,512]{2,1,0:T(8,128)(2,1)} %copy-done, bf16[512,1024]{1,0:T(8,128)(2,1)} %collective-permute-done.16.weight_ref), custom_call_target="tpu_custom_call" | custom-call | flops 536870912 | bytes 1048576 | tf_op jit(solution)/shard_map/project_out/pallas_call | solution.py:312
  103.1 1.4 collective-permute-start.21
  104.5 3.8 %collective-permute-done.18.refs_4_ = bf16[256,512]{1,0:T(8,128)(2,1)S(1)} collective-permute-done((bf16[256,512]{1,0:T(8,128)(2,1)}, bf16[256,512]{1,0:T(8,128)(2,1)S(1)}, u32[]{:S(2)}, u32[]{:S(2)}) %collective-permute-start.18) | collective-permute-done | bytes 262176 | tf_op jit(solution)/shard_map/ppermute | solution.py:89
  108.4 2.3 %collective-permute-start.19 = (bf16[128,512]{1,0:T(8,128)(2,1)S(1)}, bf16[128,512]{1,0:T(8,128)(2,1)S(1)}, u32[]{:S(2)}, u32[]{:S(2)}) collective-permute-start(bf16[128,512]{1,0:T(8,128)(2,1)S(1)} %add_convert_fusion.2), channel_id=1, source_target_pairs={{0,2},{1,3},{2,0},{3,1},{4,6},{5,7},{6,4},{7,5},{8,10},{9,11},{10,... | collective-permute-start | bytes 393224 | tf_op jit(solution)/shard_map/ppermute | solution.py:89
  110.8 0.7 collective-permute-start.20
  111.4 3.1 %project_out.7 = (f32[256,512]{1,0:T(8,128)}, bf16[256,512]{1,0:T(8,128)(2,1)}) custom-call(s32[3]{0:T(128)} %pad_add_fusion.place_ref, bf16[2,256,512]{2,1,0:T(8,128)(2,1)} %attend_last.1.mine_ref, bf16[2,256,512]{2,1,0:T(8,128)(2,1)} %copy-done, bf16[512,1024]{1,0:T(8,128)(2,1)} %collective-permute-done.22.weight_ref), custom_call_target="tpu_custom_call" | custom-call | flops 536870912 | bytes 1048576 | tf_op jit(solution)/shard_map/project_out/pallas_call | solution.py:312
  114.6 1.2 collective-permute-start.25
  115.8 1.1 collective-permute-done.21.refs_7_
  117.0 1.6 %collective-permute-start.23 = (bf16[128,512]{1,0:T(8,128)(2,1)S(1)}, bf16[128,512]{1,0:T(8,128)(2,1)S(1)}, u32[]{:S(2)}, u32[]{:S(2)}) collective-permute-start(bf16[128,512]{1,0:T(8,128)(2,1)S(1)} %add_convert_fusion), channel_id=1, source_target_pairs={{0,2},{1,3},{2,0},{3,1},{4,6},{5,7},{6,4},{7,5},{8,10},{9,11},{10,... | collective-permute-start | bytes 393224 | tf_op jit(solution)/shard_map/ppermute | solution.py:89
  118.5 1.1 collective-permute-done.19.refs_2_
  119.7 3.7 %collective-permute-done.20.refs_5_ = bf16[128,512]{1,0:T(8,128)(2,1)S(1)} collective-permute-done((bf16[128,512]{1,0:T(8,128)(2,1)S(1)}, bf16[128,512]{1,0:T(8,128)(2,1)S(1)}, u32[]{:S(2)}, u32[]{:S(2)}) %collective-permute-start.20) | collective-permute-done | bytes 131104 | tf_op jit(solution)/shard_map/ppermute | solution.py:89
  123.4 2.2 %collective-permute-done.23.refs_8_ = bf16[128,512]{1,0:T(8,128)(2,1)S(1)} collective-permute-done((bf16[128,512]{1,0:T(8,128)(2,1)S(1)}, bf16[128,512]{1,0:T(8,128)(2,1)S(1)}, u32[]{:S(2)}, u32[]{:S(2)}) %collective-permute-start.23) | collective-permute-done | bytes 131104 | tf_op jit(solution)/shard_map/ppermute | solution.py:89
  125.6 0.6 copy-done.26
  126.3 2.3 %add_up.1 = (bf16[64,1536]{1,0:T(8,128)(2,1)}, bf16[64,1536]{1,0:T(8,128)(2,1)}) custom-call(f32[256,512]{1,0:T(8,128)} %get-tuple-element.55.refs_0_, bf16[256,512]{1,0:T(8,128)(2,1)} %copy-done.10, bf16[128,512]{1,0:T(8,128)(2,1)} %copy-done.24, f32[256,512]{1,0:T(8,128)} %get-tuple-element.60.refs_3_, bf16[256,512]{1,0:T(8,128)(2,1)} %copy-done.11, ...), custom_call_target="tpu_custom_call" | custom-call | flops 393216 | bytes 1966080 | tf_op jit(solution)/shard_map/add_up/pallas_call | solution.py:352
  128.6 0.7 fusion.2
  129.8 3.5 %collective-permute-start.26 = (bf16[64,512]{1,0:T(8,128)(2,1)S(1)}, bf16[64,512]{1,0:T(8,128)(2,1)S(1)}, u32[]{:S(2)}, u32[]{:S(2)}) collective-permute-start(bf16[64,512]{1,0:T(8,128)(2,1)S(1)} %get-tuple-element.84), channel_id=1, source_target_pairs={{0,2},{1,3},{2,0},{3,1},{4,6},{5,7},{6,4},{7,5},{8,10},{9,11},{10,... | collective-permute-start | bytes 196616 | tf_op jit(solution)/shard_map/ppermute | solution.py:89
  133.3 2.3 %collective-permute-done.26.refs_3_ = bf16[64,512]{1,0:T(8,128)(2,1)S(1)} collective-permute-done((bf16[64,512]{1,0:T(8,128)(2,1)S(1)}, bf16[64,512]{1,0:T(8,128)(2,1)S(1)}, u32[]{:S(2)}, u32[]{:S(2)}) %collective-permute-start.26) | collective-permute-done | bytes 65568 | tf_op jit(solution)/shard_map/ppermute | solution.py:89
  135.6 5.1 %collective-permute-done.28.refs_5_ = bf16[64,512]{1,0:T(8,128)(2,1)S(1)} collective-permute-done((bf16[64,512]{1,0:T(8,128)(2,1)S(1)}, bf16[64,512]{1,0:T(8,128)(2,1)S(1)}, u32[]{:S(2)}, u32[]{:S(2)}) %collective-permute-start.28) | collective-permute-done | bytes 65568 | tf_op jit(solution)/shard_map/ppermute | solution.py:94
  141.4 2.0 %put_in_place.1 = bf16[64,4096]{1,0:T(8,128)(2,1)} custom-call(s32[3]{0:T(128)} %pad_add_fusion.place_ref, bf16[64,1536]{1,0:T(8,128)(2,1)} %get-tuple-element.65.refs_0_, bf16[64,1536]{1,0:T(8,128)(2,1)} %copy-done.22, f32[64,512]{1,0:T(8,128)} %get-tuple-element.78.refs_2_, bf16[64,512]{1,0:T(8,128)(2,1)} %copy-done.27, f32[64,512]{1,0:T(8,128)} %copy-done.23, ...), custom_call_target="tpu_custom_call" | custom-call | bytes 1048576 | tf_op jit(solution)/shard_map/put_in_place/pallas_call | solution.py:386
  (91 shorter events, 4.8 us)
Async XLA Ops:
  0.0 1.5 %copy-start.21 = (bf16[256,1024]{1,0:T(8,128)(2,1)S(1)}, bf16[256,1024]{1,0:T(8,128)(2,1)}, u32[]{:S(2)}) copy-start(bf16[256,1024]{1,0:T(8,128)(2,1)} %param.8) | copy-start | bytes 1572868
  1.7 4.0 %collective-permute-start.7 = (bf16[1024,512]{1,0:T(8,128)(2,1)S(1)}, bf16[1024,512]{1,0:T(8,128)(2,1)S(1)}, u32[]{:S(2)}, u32[]{:S(2)}) collective-permute-start(bf16[1024,512]{1,0:T(8,128)(2,1)S(1)} %pad_maximum_fusion), channel_id=1, source_target_pairs={{0,4},{4,0},{8,12},{12,8},{16,20},{20,16},{24,28},{28,24},{1,5},{5... | collective-permute-start | bytes 3145736 | tf_op jit(solution)/shard_map/ppermute | solution.py:77
  2.7 22.5 %collective-permute-start = (bf16[256,1024]{1,0:T(8,128)(2,1)S(1)}, bf16[256,1024]{1,0:T(8,128)(2,1)S(1)}, u32[]{:S(2)}, u32[]{:S(2)}) collective-permute-start(bf16[256,1024]{1,0:T(8,128)(2,1)S(1)} %copy-done.13), channel_id=1, source_target_pairs={{0,1},{1,0},{2,3},{3,2},{4,5},{5,4},{6,7},{7,6},{8,9},{9,8},{10,11... | collective-permute-start | bytes 1572872 | tf_op jit(solution)/shard_map/ppermute | solution.py:89
  5.7 19.4 %collective-permute-start.3 = (bf16[256,1024]{1,0:T(8,128)(2,1)S(1)}, bf16[256,1024]{1,0:T(8,128)(2,1)S(1)}, u32[]{:S(2)}, u32[]{:S(2)}) collective-permute-start(bf16[256,1024]{1,0:T(8,128)(2,1)S(1)} %copy-done.13), channel_id=1, source_target_pairs={{0,4},{4,0},{8,12},{12,8},{16,20},{20,16},{24,28},{28,24},{1,5},{5... | collective-permute-start | bytes 1572872 | tf_op jit(solution)/shard_map/ppermute | solution.py:77
  5.8 20.7 %copy-start.1 = (bf16[1024,512]{1,0:T(8,128)(2,1)}, bf16[1024,512]{1,0:T(8,128)(2,1)S(1)}, u32[]{:S(2)}) copy-start(bf16[1024,512]{1,0:T(8,128)(2,1)S(1)} %pad_maximum_fusion.1.refs_8_) | copy-start | bytes 3145732
  5.8 29.7 %collective-permute-start.8 = (bf16[1024,512]{1,0:T(8,128)(2,1)S(1)}, bf16[1024,512]{1,0:T(8,128)(2,1)S(1)}, u32[]{:S(2)}, u32[]{:S(2)}) collective-permute-start(bf16[1024,512]{1,0:T(8,128)(2,1)S(1)} %pad_maximum_fusion.1.refs_8_), channel_id=1, source_target_pairs={{0,8},{4,20},{8,0},{12,28},{16,24},{20,4},{24,16},{28,12},{1,9},{5... | collective-permute-start | bytes 3145736 | tf_op jit(solution)/shard_map/ppermute | solution.py:81
  7.6 27.9 %collective-permute-start.9 = (bf16[1024,512]{1,0:T(8,128)(2,1)S(1)}, bf16[1024,512]{1,0:T(8,128)(2,1)S(1)}, u32[]{:S(2)}, u32[]{:S(2)}) collective-permute-start(bf16[1024,512]{1,0:T(8,128)(2,1)S(1)} %pad_maximum_fusion.1.refs_8_), channel_id=1, source_target_pairs={{0,16},{4,12},{8,24},{12,4},{16,0},{20,28},{24,8},{28,20},{1,17},{... | collective-permute-start | bytes 3145736 | tf_op jit(solution)/shard_map/ppermute | solution.py:85
  9.1 25.8 %collective-permute-start.1 = (bf16[256,1024]{1,0:T(8,128)(2,1)S(1)}, bf16[256,1024]{1,0:T(8,128)(2,1)S(1)}, u32[]{:S(2)}, u32[]{:S(2)}) collective-permute-start(bf16[256,1024]{1,0:T(8,128)(2,1)S(1)} %copy-done.13), channel_id=1, source_target_pairs={{0,2},{1,3},{2,0},{3,1},{4,6},{5,7},{6,4},{7,5},{8,10},{9,11},{10,... | collective-permute-start | bytes 1572872 | tf_op jit(solution)/shard_map/ppermute | solution.py:89
  25.1 1.4 copy-start.14
  25.1 10.3 %collective-permute-start.4 = (bf16[256,1024]{1,0:T(8,128)(2,1)S(1)}, bf16[256,1024]{1,0:T(8,128)(2,1)S(1)}, u32[]{:S(2)}, u32[]{:S(2)}) collective-permute-start(bf16[256,1024]{1,0:T(8,128)(2,1)S(1)} %collective-permute-done.refs_1_), channel_id=1, source_target_pairs={{0,4},{4,0},{8,12},{12,8},{16,20},{20,16},{24,28},{28,24},{1,5},{5... | collective-permute-start | bytes 1572872 | tf_op jit(solution)/shard_map/ppermute | solution.py:77
  26.5 22.5 %collective-permute-start.12 = (bf16[512,1024]{1,0:T(8,128)(2,1)}, bf16[512,1024]{1,0:T(8,128)(2,1)}, u32[]{:S(2)}, u32[]{:S(2)}) collective-permute-start(bf16[512,1024]{1,0:T(8,128)(2,1)} %maximum_maximum_fusion.refs_2_.refs_4_), channel_id=1, source_target_pairs={{0,8},{4,20},{8,0},{12,28},{16,24},{20,4},{24,16},{28,12},{1,9},{5... | collective-permute-start | bytes 3145736 | tf_op jit(solution)/shard_map/ppermute | solution.py:81
  34.9 12.9 %collective-permute-start.2 = (bf16[256,1024]{1,0:T(8,128)(2,1)S(1)}, bf16[256,1024]{1,0:T(8,128)(2,1)}, u32[]{:S(2)}, u32[]{:S(2)}) collective-permute-start(bf16[256,1024]{1,0:T(8,128)(2,1)S(1)} %collective-permute-done.1.refs_2_), channel_id=1, source_target_pairs={{0,1},{1,0},{2,3},{3,2},{4,5},{5,4},{6,7},{7,6},{8,9},{9,8},{10,11... | collective-permute-start | bytes 1572872 | tf_op jit(solution)/shard_map/ppermute | solution.py:89
  35.5 12.3 %copy-start.17 = (bf16[256,1024]{1,0:T(8,128)(2,1)}, bf16[256,1024]{1,0:T(8,128)(2,1)S(1)}, u32[]{:S(2)}) copy-start(bf16[256,1024]{1,0:T(8,128)(2,1)S(1)} %collective-permute-done.4.refs_5_) | copy-start | bytes 1572868
  35.5 12.2 %collective-permute-start.5 = (bf16[256,1024]{1,0:T(8,128)(2,1)S(1)}, bf16[256,1024]{1,0:T(8,128)(2,1)S(1)}, u32[]{:S(2)}, u32[]{:S(2)}) collective-permute-start(bf16[256,1024]{1,0:T(8,128)(2,1)S(1)} %collective-permute-done.1.refs_2_), channel_id=1, source_target_pairs={{0,4},{4,0},{8,12},{12,8},{16,20},{20,16},{24,28},{28,24},{1,5},{5... | collective-permute-start | bytes 1572872 | tf_op jit(solution)/shard_map/ppermute | solution.py:77
  35.5 18.4 %copy-start.5 = (bf16[1024,512]{1,0:T(8,128)(2,1)}, bf16[1024,512]{1,0:T(8,128)(2,1)S(1)}, u32[]{:S(2)}) copy-start(bf16[1024,512]{1,0:T(8,128)(2,1)S(1)} %collective-permute-done.8.refs_9_) | copy-start | bytes 3145732
  35.6 18.3 %copy-start.6 = (bf16[1024,512]{1,0:T(8,128)(2,1)}, bf16[1024,512]{1,0:T(8,128)(2,1)S(1)}, u32[]{:S(2)}) copy-start(bf16[1024,512]{1,0:T(8,128)(2,1)S(1)} %collective-permute-done.9.refs_10_) | copy-start | bytes 3145732
  35.6 18.3 %collective-permute-start.10 = (bf16[1024,512]{1,0:T(8,128)(2,1)S(1)}, bf16[1024,512]{1,0:T(8,128)(2,1)S(1)}, u32[]{:S(2)}, u32[]{:S(2)}) collective-permute-start(bf16[1024,512]{1,0:T(8,128)(2,1)S(1)} %collective-permute-done.8.refs_9_), channel_id=1, source_target_pairs={{0,16},{4,12},{8,24},{12,4},{16,0},{20,28},{24,8},{28,20},{1,17},{... | collective-permute-start | bytes 3145736 | tf_op jit(solution)/shard_map/ppermute | solution.py:85
  47.7 4.3 %collective-permute-start.6 = (bf16[256,1024]{1,0:T(8,128)(2,1)}, bf16[256,1024]{1,0:T(8,128)(2,1)}, u32[]{:S(2)}, u32[]{:S(2)}) collective-permute-start(bf16[256,1024]{1,0:T(8,128)(2,1)} %collective-permute-done.2.refs_3_), channel_id=1, source_target_pairs={{0,4},{4,0},{8,12},{12,8},{16,20},{20,16},{24,28},{28,24},{1,5},{5... | collective-permute-start | bytes 1572872 | tf_op jit(solution)/shard_map/ppermute | solution.py:77
  48.5 22.9 %collective-permute-start.11 = (bf16[512,1024]{1,0:T(8,128)(2,1)}, bf16[512,1024]{1,0:T(8,128)(2,1)}, u32[]{:S(2)}, u32[]{:S(2)}) collective-permute-start(bf16[512,1024]{1,0:T(8,128)(2,1)} %maximum_maximum_fusion.refs_2_.refs_4_), channel_id=1, source_target_pairs={{0,16},{4,12},{8,24},{12,4},{16,0},{20,28},{24,8},{28,20},{1,17},{... | collective-permute-start | bytes 3145736 | tf_op jit(solution)/shard_map/ppermute | solution.py:85
  49.0 27.5 %collective-permute-start.13 = (bf16[512,1024]{1,0:T(8,128)(2,1)}, bf16[512,1024]{1,0:T(8,128)(2,1)}, u32[]{:S(2)}, u32[]{:S(2)}) collective-permute-start(bf16[512,1024]{1,0:T(8,128)(2,1)} %collective-permute-done.12.refs_3_.refs_5_), channel_id=1, source_target_pairs={{0,16},{4,12},{8,24},{12,4},{16,0},{20,28},{24,8},{28,20},{1,17},{... | collective-permute-start | bytes 3145736 | tf_op jit(solution)/shard_map/ppermute | solution.py:85
  60.6 8.3 %copy-start.8 = (bf16[512,1024]{1,0:T(8,128)(2,1)S(1)}, bf16[512,1024]{1,0:T(8,128)(2,1)}, u32[]{:S(2)}) copy-start(bf16[512,1024]{1,0:T(8,128)(2,1)} %weight_ref.1) | copy-start | bytes 3145732
  68.9 18.7 %collective-permute-start.17 = (bf16[512,1024]{1,0:T(8,128)(2,1)S(1)}, bf16[512,1024]{1,0:T(8,128)(2,1)S(1)}, u32[]{:S(2)}, u32[]{:S(2)}) collective-permute-start(bf16[512,1024]{1,0:T(8,128)(2,1)S(1)} %copy-done.8), channel_id=1, source_target_pairs={{0,16},{4,12},{8,24},{12,4},{16,0},{20,28},{24,8},{28,20},{1,17},{... | collective-permute-start | bytes 3145736 | tf_op jit(solution)/shard_map/ppermute | solution.py:85
  85.0 15.0 %collective-permute-start.16 = (bf16[512,1024]{1,0:T(8,128)(2,1)S(1)}, bf16[512,1024]{1,0:T(8,128)(2,1)}, u32[]{:S(2)}, u32[]{:S(2)}) collective-permute-start(bf16[512,1024]{1,0:T(8,128)(2,1)S(1)} %copy-done.8), channel_id=1, source_target_pairs={{0,8},{4,20},{8,0},{12,28},{16,24},{20,4},{24,16},{28,12},{1,9},{5... | collective-permute-start | bytes 3145736 | tf_op jit(solution)/shard_map/ppermute | solution.py:81
  86.8 2.6 %collective-permute-start.14 = (bf16[2,256,512]{2,1,0:T(8,128)(2,1)}, bf16[2,256,512]{2,1,0:T(8,128)(2,1)S(1)}, u32[]{:S(2)}, u32[]{:S(2)}) collective-permute-start(bf16[2,256,512]{2,1,0:T(8,128)(2,1)} %attend_last.1.mine_ref), channel_id=1, source_target_pairs={{0,4},{4,0},{8,12},{12,8},{16,20},{20,16},{24,28},{28,24},{1,5},{5... | collective-permute-start | bytes 1572872 | tf_op jit(solution)/shard_map/ppermute | solution.py:77
  87.6 6.9 %copy-start.9 = (bf16[512,1024]{1,0:T(8,128)(2,1)}, bf16[512,1024]{1,0:T(8,128)(2,1)S(1)}, u32[]{:S(2)}) copy-start(bf16[512,1024]{1,0:T(8,128)(2,1)S(1)} %collective-permute-done.17.weight_ref) | copy-start | bytes 3145732
  87.6 23.8 %collective-permute-start.22 = (bf16[512,1024]{1,0:T(8,128)(2,1)S(1)}, bf16[512,1024]{1,0:T(8,128)(2,1)}, u32[]{:S(2)}, u32[]{:S(2)}) collective-permute-start(bf16[512,1024]{1,0:T(8,128)(2,1)S(1)} %collective-permute-done.17.weight_ref), channel_id=1, source_target_pairs={{0,8},{4,20},{8,0},{12,28},{16,24},{20,4},{24,16},{28,12},{1,9},{5... | collective-permute-start | bytes 3145736 | tf_op jit(solution)/shard_map/ppermute | solution.py:81
  93.3 11.2 %collective-permute-start.15 = (bf16[256,512]{1,0:T(8,128)(2,1)}, bf16[256,512]{1,0:T(8,128)(2,1)S(1)}, u32[]{:S(2)}, u32[]{:S(2)}) collective-permute-start(bf16[256,512]{1,0:T(8,128)(2,1)} %get-tuple-element.53), channel_id=1, source_target_pairs={{0,1},{1,0},{2,3},{3,2},{4,5},{5,4},{6,7},{7,6},{8,9},{9,8},{10,11... | collective-permute-start | bytes 786440 | tf_op jit(solution)/shard_map/ppermute | solution.py:89
  97.6 10.8 %collective-permute-start.18 = (bf16[256,512]{1,0:T(8,128)(2,1)}, bf16[256,512]{1,0:T(8,128)(2,1)S(1)}, u32[]{:S(2)}, u32[]{:S(2)}) collective-permute-start(bf16[256,512]{1,0:T(8,128)(2,1)} %get-tuple-element.58), channel_id=1, source_target_pairs={{0,1},{1,0},{2,3},{3,2},{4,5},{5,4},{6,7},{7,6},{8,9},{9,8},{10,11... | collective-permute-start | bytes 786440 | tf_op jit(solution)/shard_map/ppermute | solution.py:89
  98.5 6.0 %copy-start.2 = (f32[256,512]{1,0:T(8,128)S(1)}, f32[256,512]{1,0:T(8,128)}, u32[]{:S(2)}) copy-start(f32[256,512]{1,0:T(8,128)} %get-tuple-element.55.refs_0_) | copy-start | bytes 1572868
  98.5 12.2 %copy-start.3 = (f32[256,512]{1,0:T(8,128)S(1)}, f32[256,512]{1,0:T(8,128)}, u32[]{:S(2)}) copy-start(f32[256,512]{1,0:T(8,128)} %get-tuple-element.60.refs_3_) | copy-start | bytes 1572868
  103.1 13.8 %collective-permute-start.21 = (bf16[256,512]{1,0:T(8,128)(2,1)}, bf16[256,512]{1,0:T(8,128)(2,1)S(1)}, u32[]{:S(2)}, u32[]{:S(2)}) collective-permute-start(bf16[256,512]{1,0:T(8,128)(2,1)} %get-tuple-element.63), channel_id=1, source_target_pairs={{0,1},{1,0},{2,3},{3,2},{4,5},{5,4},{6,7},{7,6},{8,9},{9,8},{10,11... | collective-permute-start | bytes 786440 | tf_op jit(solution)/shard_map/ppermute | solution.py:89
  104.5 10.0 %copy-start.10 = (bf16[256,512]{1,0:T(8,128)(2,1)}, bf16[256,512]{1,0:T(8,128)(2,1)S(1)}, u32[]{:S(2)}) copy-start(bf16[256,512]{1,0:T(8,128)(2,1)S(1)} %collective-permute-done.15.refs_1_) | copy-start | bytes 786436
  108.4 6.2 %copy-start.11 = (bf16[256,512]{1,0:T(8,128)(2,1)}, bf16[256,512]{1,0:T(8,128)(2,1)S(1)}, u32[]{:S(2)}) copy-start(bf16[256,512]{1,0:T(8,128)(2,1)S(1)} %collective-permute-done.18.refs_4_) | copy-start | bytes 786436
  108.4 11.3 %collective-permute-start.19 = (bf16[128,512]{1,0:T(8,128)(2,1)S(1)}, bf16[128,512]{1,0:T(8,128)(2,1)S(1)}, u32[]{:S(2)}, u32[]{:S(2)}) collective-permute-start(bf16[128,512]{1,0:T(8,128)(2,1)S(1)} %add_convert_fusion.2), channel_id=1, source_target_pairs={{0,2},{1,3},{2,0},{3,1},{4,6},{5,7},{6,4},{7,5},{8,10},{9,11},{10,... | collective-permute-start | bytes 393224 | tf_op jit(solution)/shard_map/ppermute | solution.py:89
  110.7 6.2 %copy-start.4 = (f32[256,512]{1,0:T(8,128)S(1)}, f32[256,512]{1,0:T(8,128)}, u32[]{:S(2)}) copy-start(f32[256,512]{1,0:T(8,128)} %get-tuple-element.64.refs_6_) | copy-start | bytes 1572868
  110.8 12.6 %collective-permute-start.20 = (bf16[128,512]{1,0:T(8,128)(2,1)S(1)}, bf16[128,512]{1,0:T(8,128)(2,1)S(1)}, u32[]{:S(2)}, u32[]{:S(2)}) collective-permute-start(bf16[128,512]{1,0:T(8,128)(2,1)S(1)} %add_convert_fusion.1), channel_id=1, source_target_pairs={{0,2},{1,3},{2,0},{3,1},{4,6},{5,7},{6,4},{7,5},{8,10},{9,11},{10,... | collective-permute-start | bytes 393224 | tf_op jit(solution)/shard_map/ppermute | solution.py:89
  114.6 14.0 %collective-permute-start.25 = (bf16[256,512]{1,0:T(8,128)(2,1)}, bf16[256,512]{1,0:T(8,128)(2,1)S(1)}, u32[]{:S(2)}, u32[]{:S(2)}) collective-permute-start(bf16[256,512]{1,0:T(8,128)(2,1)} %get-tuple-element.69), channel_id=1, source_target_pairs={{0,1},{1,0},{2,3},{3,2},{4,5},{5,4},{6,7},{7,6},{8,9},{9,8},{10,11... | collective-permute-start | bytes 786440 | tf_op jit(solution)/shard_map/ppermute | solution.py:89
  116.9 8.7 %copy-start.12 = (bf16[256,512]{1,0:T(8,128)(2,1)}, bf16[256,512]{1,0:T(8,128)(2,1)S(1)}, u32[]{:S(2)}) copy-start(bf16[256,512]{1,0:T(8,128)(2,1)S(1)} %collective-permute-done.21.refs_7_) | copy-start | bytes 786436
  116.9 11.6 %copy-start.19 = (f32[256,512]{1,0:T(8,128)S(1)}, f32[256,512]{1,0:T(8,128)}, u32[]{:S(2)}) copy-start(f32[256,512]{1,0:T(8,128)} %get-tuple-element.68) | copy-start | bytes 1572868
  117.0 8.7 %collective-permute-start.23 = (bf16[128,512]{1,0:T(8,128)(2,1)S(1)}, bf16[128,512]{1,0:T(8,128)(2,1)S(1)}, u32[]{:S(2)}, u32[]{:S(2)}) collective-permute-start(bf16[128,512]{1,0:T(8,128)(2,1)S(1)} %add_convert_fusion), channel_id=1, source_target_pairs={{0,2},{1,3},{2,0},{3,1},{4,6},{5,7},{6,4},{7,5},{8,10},{9,11},{10,... | collective-permute-start | bytes 393224 | tf_op jit(solution)/shard_map/ppermute | solution.py:89
  119.6 6.0 %copy-start.24 = (bf16[128,512]{1,0:T(8,128)(2,1)}, bf16[128,512]{1,0:T(8,128)(2,1)S(1)}, u32[]{:S(2)}) copy-start(bf16[128,512]{1,0:T(8,128)(2,1)S(1)} %collective-permute-done.19.refs_2_) | copy-start | bytes 393220
  123.4 2.2 %copy-start.25 = (bf16[128,512]{1,0:T(8,128)(2,1)}, bf16[128,512]{1,0:T(8,128)(2,1)S(1)}, u32[]{:S(2)}) copy-start(bf16[128,512]{1,0:T(8,128)(2,1)S(1)} %collective-permute-done.20.refs_5_) | copy-start | bytes 393220
  128.5 4.8 %collective-permute-start.24 = (bf16[64,1536]{1,0:T(8,128)(2,1)}, bf16[64,1536]{1,0:T(8,128)(2,1)S(1)}, u32[]{:S(2)}, u32[]{:S(2)}) collective-permute-start(bf16[64,1536]{1,0:T(8,128)(2,1)} %get-tuple-element.66), channel_id=1, source_target_pairs={{0,4},{4,0},{8,12},{12,8},{16,20},{20,16},{24,28},{28,24},{1,5},{5... | collective-permute-start | bytes 589832 | tf_op jit(solution)/shard_map/ppermute | solution.py:77
  129.3 11.4 %collective-permute-start.27 = (f32[64,512]{1,0:T(8,128)S(1)}, f32[64,512]{1,0:T(8,128)S(1)}, u32[]{:S(2)}, u32[]{:S(2)}) collective-permute-start(f32[64,512]{1,0:T(8,128)S(1)} %get-tuple-element.77), channel_id=1, source_target_pairs={{0,4},{4,0},{8,12},{12,8},{16,20},{20,16},{24,28},{28,24},{1,5},{5... | collective-permute-start | bytes 393224 | tf_op jit(solution)/shard_map/ppermute | solution.py:77
  129.8 5.8 %collective-permute-start.26 = (bf16[64,512]{1,0:T(8,128)(2,1)S(1)}, bf16[64,512]{1,0:T(8,128)(2,1)S(1)}, u32[]{:S(2)}, u32[]{:S(2)}) collective-permute-start(bf16[64,512]{1,0:T(8,128)(2,1)S(1)} %get-tuple-element.84), channel_id=1, source_target_pairs={{0,2},{1,3},{2,0},{3,1},{4,6},{5,7},{6,4},{7,5},{8,10},{9,11},{10,... | collective-permute-start | bytes 196616 | tf_op jit(solution)/shard_map/ppermute | solution.py:89
  133.3 7.4 %collective-permute-start.28 = (bf16[64,512]{1,0:T(8,128)(2,1)S(1)}, bf16[64,512]{1,0:T(8,128)(2,1)S(1)}, u32[]{:S(2)}, u32[]{:S(2)}) collective-permute-start(bf16[64,512]{1,0:T(8,128)(2,1)S(1)} %get-tuple-element.70), channel_id=1, source_target_pairs={{0,6},{1,7},{2,4},{3,5},{4,2},{5,3},{6,0},{7,1},{8,14},{9,15},{10,... | collective-permute-start | bytes 196616 | tf_op jit(solution)/shard_map/ppermute | solution.py:94
  133.3 7.4 %copy-start.22 = (bf16[64,1536]{1,0:T(8,128)(2,1)}, bf16[64,1536]{1,0:T(8,128)(2,1)S(1)}, u32[]{:S(2)}) copy-start(bf16[64,1536]{1,0:T(8,128)(2,1)S(1)} %collective-permute-done.24.refs_1_) | copy-start | bytes 589828
  135.6 5.1 %copy-start.27 = (bf16[64,512]{1,0:T(8,128)(2,1)}, bf16[64,512]{1,0:T(8,128)(2,1)S(1)}, u32[]{:S(2)}) copy-start(bf16[64,512]{1,0:T(8,128)(2,1)S(1)} %collective-permute-done.26.refs_3_) | copy-start | bytes 196612
  (10 other events, 9.1 us)

commit v4 on v3

--- a/solution.py
+++ b/solution.py
@@ -87,11 +87,6 @@
 
 def over_z(a, step):
     return lax.ppermute(a, "fsdp", [(z, z ^ step) for z in range(4)])
-
-
-def over_core_and_z(a, step):
-    pairs = [(b * 4 + z, (b ^ 1) * 4 + (z ^ step)) for b in range(8) for z in range(4)]
-    return lax.ppermute(a, ("blk", "fsdp"), pairs)
 
 
 def after(value, *earlier):
@@ -208,12 +203,12 @@
     return [jnp.where(first, a, b) for a, b in zip(*found)]
 
 
-def attend(query_blocks, pieces, before=None):
+def attend(query_blocks, pieces, before=None, last=True):
     rows, columns = query_blocks[0].shape
     width = PAIRS_AT_ONCE * PAIR
     steps = columns // width
     blocks = len(query_blocks)
-    last = before is not None
+    last = last and before is not None
     held = [] if before is None else [a for block in before for a in block]
     outs = 1 if last else 3 * blocks
 
@@ -231,12 +226,14 @@
             vs = [jnp.concatenate([r[:, at], one], axis=1) for r, one in zip(v_refs, ones)]
             for n in range(blocks):
                 weighted, sums, tops = pair_part(q_refs[n][:, at], ks, vs)
-                if last:
+                if held:
                     weighted_0, sums_0, tops_0 = (r[:, at] for r in held_refs[3 * n : 3 * n + 3])
                     top = jnp.maximum(tops, tops_0)
                     now, then = jnp.exp(tops - top), jnp.exp(tops_0 - top)
                     weighted = weighted * now + weighted_0 * then
                     sums = sums * now + sums_0 * then
+                    tops = top
+                if last:
                     out_refs[0][n, :, at] = (weighted / sums).astype(jnp.bfloat16)
                 else:
                     for ref, a in zip(out_refs[3 * n : 3 * n + 3], (weighted, sums, tops)):
@@ -270,7 +267,7 @@
             bytes_accessed=sum(a.size * a.dtype.itemsize for a in args),
             transcendentals=blocks * rows * total_keys * (columns // HEAD_DIM),
         ),
-        name="attend_last" if last else "attend_first",
+        name=f"attend_{'last' if last else 'next' if held else 'first'}_{len(pieces)}",
     )(*args)
     if last:
         return found[0]
@@ -365,24 +362,26 @@
     )(*args)
 
 
-def put_in_place(place, chips, mine, got, last):
+def put_in_place(place, chips, mine, got, lasts):
     rows = mine.shape[0]
-    shard = mine.shape[1] // (len(chips) - 1)
+    early = len(chips) - len(lasts)
+    shard = mine.shape[1] // early
 
     def kernel(place_ref, *refs):
         out_ref = refs[-1]
         for n, whose in enumerate(chips):
             for core_step in range(2):
-                if n < len(chips) - 1:
+                if n < early:
                     value = refs[core_step][:, n * shard : (n + 1) * shard]
                 else:
-                    near_ref, away_ref = refs[2 + 2 * core_step : 4 + 2 * core_step]
-                    value = near_ref[...] + away_ref[...].astype(jnp.float32)
+                    first = 2 + 4 * (n - early) + 2 * core_step
+                    near_ref, away_ref = refs[first : first + 2]
+                    value = near_ref[...] + away_ref[:rows].astype(jnp.float32)
                 at = chip_of(place_ref, whose, core_step) * 2 + (place_ref[1] ^ core_step)
                 begin = pl.multiple_of(at * shard, shard)
                 out_ref[:, pl.ds(begin, shard)] = value.astype(jnp.bfloat16)
 
-    args = [mine, got, *last]
+    args = [mine, got] + [a for last in lasts for a in last]
     return pl.pallas_call(
         kernel,
         out_shape=jax.ShapeDtypeStruct((rows, 8 * shard), jnp.bfloat16),
@@ -414,8 +413,9 @@
         return (sums[0][begin:] + first[begin:].astype(jnp.float32)).astype(jnp.bfloat16)
 
     def totals(sums, first):
-        own, other, same, crossed = jnp.split(sums[0] + first.astype(jnp.float32), 4)
-        return own, other, same.astype(jnp.bfloat16), crossed.astype(jnp.bfloat16)
+        held, passed = jnp.split(sums[0] + first.astype(jnp.float32), 2)
+        own, other = jnp.split(held, 2)
+        return own, other, passed.astype(jnp.bfloat16)
 
     states_1 = over_z(decoder_states, 1)
     states_2 = over_z(decoder_states, 2)
@@ -433,8 +433,8 @@
     queries = project_queries(place, [decoder_states, states_1, states_2, states_3, others, others_1, others_2, others_3], [(OWN, weights), (NEAR, near_weights), (SIDE, side_weights), (FAR, far_weights)])
     encoded = jnp.concatenate([whole_rows(enc_keys, swapped[shard:-rows]), whole_rows(enc_values, swapped[-rows:])], axis=1)
     near_encoded = cross(after(encoded, states_1))
-    before = attend(queries, [encoded, near_encoded])
-    side_encoded = cross_back(after(encoded, states_1, states_2, others_1))
+    before = attend(after(queries, side_weights), [encoded, near_encoded])
+    side_encoded = cross_back(after(encoded, states_2, others_1))
     far_encoded = cross_back(near_encoded)
     context = attend(queries, [side_encoded, far_encoded], before)
     context_got = over_core(context)
@@ -448,20 +448,22 @@
     second_0 = over_z(after(passed_0, first_1), 2)
     passed_1 = add_passed(sums_1, first_1)
     second_1 = over_z(passed_1, 2)
+    far_out = cross(side_out)
     sums_2 = project_out(place, after(context, sums_1), context_got, near_out)
-    first_2 = over_z(sums_2[1], 1)
-    far_out = cross(side_out)
-    passed_2 = add_passed(after(sums_2, far_out), first_2)
-    second_2 = over_z(passed_2, 2)
-    most_added = add_up([(sums_0[0], first_0, second_0), (sums_1[0], first_1, second_1), (sums_2[0], first_2, second_2)])
+    sums_3 = project_out(place, after(context, sums_2), context_got, far_out)
+    most_added = add_up([(after(sums_0, sums_3)[0], first_0, second_0), (sums_1[0], first_1, second_1)])
     most_got = over_core(most_added[1])
-    sums_3 = project_out(place, after(context, sums_2), context_got, far_out)
+    first_2 = over_z(after(sums_2, context_got, context)[1], 1)
+    passed_2 = totals(after(sums_2, far_out), first_2)
+    second_2 = over_z(passed_2[2], 2)
+    got_2 = over_core(passed_2[1])
+    third_2 = over_core(second_2[second_2.shape[0] // 2 :])
     first_3 = over_z(sums_3[1], 1)
     passed_3 = totals(sums_3, first_3)
     second_3 = over_z(passed_3[2], 2)
-    last_got = over_core(passed_3[1])
-    third_3 = over_core_and_z(after(passed_3, first_2)[3], 2)
-    return put_in_place(place, (OWN, SIDE, NEAR, FAR), most_added[0], most_got, (passed_3[0], second_3, last_got, third_3))
+    got_3 = over_core(passed_3[1])
+    third_3 = over_core(second_3[second_3.shape[0] // 2 :])
+    return put_in_place(place, (OWN, SIDE, NEAR, FAR), most_added[0], most_got, [(passed_2[0], second_2, got_2, third_2), (passed_3[0], second_3, got_3, third_3)])
 
 
 def solution(mesh):

time: 144 us -> 141 us (0.979)
  waiting for transfers between devices: 59.5 us -> 55.8 us
    ppermute x1 -> x0, waiting for transfers between devices: 5.13 us -> none  [over_core_and_z(): return lax.ppermute(a, ('blk', 'fsdp'), pairs)]
    unnamed x58 -> x60, local copies, waits for them, and re-layouts: 4.64 us -> 4.63 us
  transfers between devices with their start and end apart: 29 -> 31, of which waited for: 14 -> 14; matrix products, arithmetic and copies ran while one was open for 2% -> 3% of each run, Pallas kernels for 26% -> 26%
where the time goes in v4:
time: 141 us
  waiting for transfers between devices  55.8 us (40%)
  Pallas kernels  39.3 us (28%)
  starting transfers between devices  35.4 us (25%)
  local copies, waits for them, and re-layouts  7.55 us (5%)
  other arithmetic  2.19 us (2%)
    ppermute x11, waiting for transfers between devices, over_z(): return lax.ppermute(a, 'fsdp', [(z, z ^ step) for z in range(4)])  45.3 us
    ppermute x11, starting transfers between devices, over_z(): return lax.ppermute(a, 'fsdp', [(z, z ^ step) for z in range(4)])  18.9 us
    pallas_call x2, Pallas kernels, attend(): pl.pallas_call(kernel, grid=(steps,), out_shape=out_shape, in_specs=in_sp...  16.8 us
    pallas_call x4, Pallas kernels, project_out(): pl.pallas_call(kernel, grid=(tiles,), out_shape=[jax.ShapeDtypeStruct((he...  12.7 us
    ppermute x4, starting transfers between devices, cross(): return lax.ppermute(a, 'blk', CROSS)  7.92 us
    ppermute x5, waiting for transfers between devices, cross_back(): return lax.ppermute(a, 'blk', CROSS_BACK)  7.89 us
    ppermute x5, starting transfers between devices, cross_back(): return lax.ppermute(a, 'blk', CROSS_BACK)  7.29 us
    pallas_call x1, Pallas kernels, project_queries(): pl.pallas_call(kernel, out_shape=(shape, shape), in_specs=[smem_spec()] +...  5.65 us
  transfers between devices with their start and end apart: 31, of which 14 were waited for; matrix products, arithmetic and copies ran while one was open for 3% of the time, Pallas kernels for 26%

profile of v4, /device:TPU:0, one launch (start us, length us, event | category | flops | bytes accessed | tf_op | source)
XLA Modules:
  0.0 140.6 jit_solution(3753576771887384698)
XLA Ops:
  0.0 1.4 constant_dynamic-slice_fusion.5
  2.7 3.0 %collective-permute-start = (bf16[256,1024]{1,0:T(8,128)(2,1)S(1)}, bf16[256,1024]{1,0:T(8,128)(2,1)S(1)}, u32[]{:S(2)}, u32[]{:S(2)}) collective-permute-start(bf16[256,1024]{1,0:T(8,128)(2,1)S(1)} %copy-done.11), channel_id=1, source_target_pairs={{0,1},{1,0},{2,3},{3,2},{4,5},{5,4},{6,7},{7,6},{8,9},{9,8},{10,11... | collective-permute-start | bytes 1572872 | tf_op jit(solution)/shard_map/ppermute | solution.py:89
  5.8 1.7 %collective-permute-start.8 = (bf16[1024,512]{1,0:T(8,128)(2,1)S(1)}, bf16[1024,512]{1,0:T(8,128)(2,1)S(1)}, u32[]{:S(2)}, u32[]{:S(2)}) collective-permute-start(bf16[1024,512]{1,0:T(8,128)(2,1)S(1)} %pad_maximum_fusion.1.refs_8_), channel_id=1, source_target_pairs={{0,8},{4,20},{8,0},{12,28},{16,24},{20,4},{24,16},{28,12},{1,9},{5... | collective-permute-start | bytes 3145736 | tf_op jit(solution)/shard_map/ppermute | solution.py:81
  7.6 1.5 %collective-permute-start.9 = (bf16[1024,512]{1,0:T(8,128)(2,1)S(1)}, bf16[1024,512]{1,0:T(8,128)(2,1)S(1)}, u32[]{:S(2)}, u32[]{:S(2)}) collective-permute-start(bf16[1024,512]{1,0:T(8,128)(2,1)S(1)} %pad_maximum_fusion.1.refs_8_), channel_id=1, source_target_pairs={{0,16},{4,12},{8,24},{12,4},{16,0},{20,28},{24,8},{28,20},{1,17},{... | collective-permute-start | bytes 3145736 | tf_op jit(solution)/shard_map/ppermute | solution.py:85
  9.1 2.6 %collective-permute-start.1 = (bf16[256,1024]{1,0:T(8,128)(2,1)S(1)}, bf16[256,1024]{1,0:T(8,128)(2,1)S(1)}, u32[]{:S(2)}, u32[]{:S(2)}) collective-permute-start(bf16[256,1024]{1,0:T(8,128)(2,1)S(1)} %copy-done.11), channel_id=1, source_target_pairs={{0,2},{1,3},{2,0},{3,1},{4,6},{5,7},{6,4},{7,5},{8,10},{9,11},{10,... | collective-permute-start | bytes 1572872 | tf_op jit(solution)/shard_map/ppermute | solution.py:89
  11.7 13.4 %collective-permute-done.refs_1_ = bf16[256,1024]{1,0:T(8,128)(2,1)S(1)} collective-permute-done((bf16[256,1024]{1,0:T(8,128)(2,1)S(1)}, bf16[256,1024]{1,0:T(8,128)(2,1)S(1)}, u32[]{:S(2)}, u32[]{:S(2)}) %collective-permute-start) | collective-permute-done | bytes 524320 | tf_op jit(solution)/shard_map/ppermute | solution.py:89
  25.3 1.2 maximum_maximum_fusion.refs_2_.refs_4_
  26.5 2.7 %collective-permute-start.12 = (bf16[512,1024]{1,0:T(8,128)(2,1)}, bf16[512,1024]{1,0:T(8,128)(2,1)}, u32[]{:S(2)}, u32[]{:S(2)}) collective-permute-start(bf16[512,1024]{1,0:T(8,128)(2,1)} %maximum_maximum_fusion.refs_2_.refs_4_), channel_id=1, source_target_pairs={{0,8},{4,20},{8,0},{12,28},{16,24},{20,4},{24,16},{28,12},{1,9},{5... | collective-permute-start | bytes 3145736 | tf_op jit(solution)/shard_map/ppermute | solution.py:81
  29.2 5.7 %collective-permute-done.1.refs_2_ = bf16[256,1024]{1,0:T(8,128)(2,1)S(1)} collective-permute-done((bf16[256,1024]{1,0:T(8,128)(2,1)S(1)}, bf16[256,1024]{1,0:T(8,128)(2,1)S(1)}, u32[]{:S(2)}, u32[]{:S(2)}) %collective-permute-start.1) | collective-permute-done | bytes 524320 | tf_op jit(solution)/shard_map/ppermute | solution.py:89
  34.9 0.6 collective-permute-start.2
  36.2 11.6 %collective-permute-done.2.refs_3_ = bf16[256,1024]{1,0:T(8,128)(2,1)} collective-permute-done((bf16[256,1024]{1,0:T(8,128)(2,1)S(1)}, bf16[256,1024]{1,0:T(8,128)(2,1)}, u32[]{:S(2)}, u32[]{:S(2)}) %collective-permute-start.2) | collective-permute-done | bytes 524320 | tf_op jit(solution)/shard_map/ppermute | solution.py:89
  47.8 0.7 copy-done.16
  49.0 2.3 %collective-permute-start.13 = (bf16[512,1024]{1,0:T(8,128)(2,1)}, bf16[512,1024]{1,0:T(8,128)(2,1)}, u32[]{:S(2)}, u32[]{:S(2)}) collective-permute-start(bf16[512,1024]{1,0:T(8,128)(2,1)} %collective-permute-done.12.refs_3_.refs_5_), channel_id=1, source_target_pairs={{0,16},{4,12},{8,24},{12,4},{16,0},{20,28},{24,8},{28,20},{1,17},{... | collective-permute-start | bytes 3145736 | tf_op jit(solution)/shard_map/ppermute | solution.py:85
  51.3 0.6 pad_add_fusion.place_ref
  51.9 2.0 %collective-permute-done.10.refs_11_ = bf16[1024,512]{1,0:T(8,128)(2,1)S(1)} collective-permute-done((bf16[1024,512]{1,0:T(8,128)(2,1)S(1)}, bf16[1024,512]{1,0:T(8,128)(2,1)S(1)}, u32[]{:S(2)}, u32[]{:S(2)}) %collective-permute-start.10) | collective-permute-done | bytes 1048608 | tf_op jit(solution)/shard_map/ppermute | solution.py:85
  53.9 1.1 copy-done.6
  55.0 5.6 %project_queries.1 = (bf16[256,512]{1,0:T(8,128)(2,1)}, bf16[256,512]{1,0:T(8,128)(2,1)}) custom-call(s32[3]{0:T(128)} %pad_add_fusion.place_ref, bf16[256,1024]{1,0:T(8,128)(2,1)} %refs_0_.1, bf16[256,1024]{1,0:T(8,128)(2,1)} %copy-done.12, bf16[256,1024]{1,0:T(8,128)(2,1)} %copy-done.14, bf16[256,1024]{1,0:T(8,128)(2,1)} %collective-permute-done.2.refs_3_, ...), custom_call_target="tpu_custom_call" | custom-call | flops 2147483648 | bytes 8388608 | tf_op jit(solution)/shard_map/project_queries/pallas_call | solution.py:161
  60.7 8.3 %attend_first_2.1 = (f32[256,512]{1,0:T(8,128)}, f32[256,512]{1,0:T(8,128)}, f32[256,512]{1,0:T(8,128)}, f32[256,512]{1,0:T(8,128)}, f32[256,512]{1,0:T(8,128)}, /*index=5*/f32[256,512]{1,0:T(8,128)}) custom-call(bf16[256,512]{1,0:T(8,128)(2,1)} %get-tuple-element.49.refs_0_, bf16[256,512]{1,0:T(8,128)(2,1)} %get-tuple-element.50.refs_1_, ...), custom_call_target="tpu_custom_call" | custom-call | flops 4294967296 | bytes 4718592 | tf_op jit(solution)/shard_map/attend_first_2/pallas_call | solution.py:258
  69.0 2.5 %collective-permute-start.15 = (bf16[512,1024]{1,0:T(8,128)(2,1)S(1)}, bf16[512,1024]{1,0:T(8,128)(2,1)S(1)}, u32[]{:S(2)}, u32[]{:S(2)}) collective-permute-start(bf16[512,1024]{1,0:T(8,128)(2,1)S(1)} %copy-done.7), channel_id=1, source_target_pairs={{0,16},{4,12},{8,24},{12,4},{16,0},{20,28},{24,8},{28,20},{1,17},{... | collective-permute-start | bytes 3145736 | tf_op jit(solution)/shard_map/ppermute | solution.py:85
  71.4 5.1 %collective-permute-done.13.refs_3_.refs_5_ = bf16[512,1024]{1,0:T(8,128)(2,1)} collective-permute-done((bf16[512,1024]{1,0:T(8,128)(2,1)}, bf16[512,1024]{1,0:T(8,128)(2,1)}, u32[]{:S(2)}, u32[]{:S(2)}) %collective-permute-start.13) | collective-permute-done | bytes 1048608 | tf_op jit(solution)/shard_map/ppermute | solution.py:85
  76.5 8.5 %attend_last_2.1.mine_ref = bf16[2,256,512]{2,1,0:T(8,128)(2,1)} custom-call(bf16[256,512]{1,0:T(8,128)(2,1)} %get-tuple-element.49.refs_0_, bf16[256,512]{1,0:T(8,128)(2,1)} %get-tuple-element.50.refs_1_, bf16[512,1024]{1,0:T(8,128)(2,1)} %collective-permute-done.11.refs_2_.refs_4_, bf16[512,1024]{1,0:T(8,128)(2,1)} %collective-permute-done.13.refs_3_.refs_5_, ...), custom_call_target="tpu_custom_call" | custom-call | flops 4294967296 | bytes 7864320 | tf_op jit(solution)/shard_map/attend_last_2/pallas_call | solution.py:258
  85.0 1.8 %collective-permute-start.16 = (bf16[512,1024]{1,0:T(8,128)(2,1)S(1)}, bf16[512,1024]{1,0:T(8,128)(2,1)}, u32[]{:S(2)}, u32[]{:S(2)}) collective-permute-start(bf16[512,1024]{1,0:T(8,128)(2,1)S(1)} %copy-done.7), channel_id=1, source_target_pairs={{0,8},{4,20},{8,0},{12,28},{16,24},{20,4},{24,16},{28,12},{1,9},{5... | collective-permute-start | bytes 3145736 | tf_op jit(solution)/shard_map/ppermute | solution.py:81
  86.8 0.8 collective-permute-done.15.weight_ref
  87.6 1.7 %collective-permute-start.17 = (bf16[512,1024]{1,0:T(8,128)(2,1)S(1)}, bf16[512,1024]{1,0:T(8,128)(2,1)}, u32[]{:S(2)}, u32[]{:S(2)}) collective-permute-start(bf16[512,1024]{1,0:T(8,128)(2,1)S(1)} %collective-permute-done.15.weight_ref), channel_id=1, source_target_pairs={{0,8},{4,20},{8,0},{12,28},{16,24},{20,4},{24,16},{28,12},{1,9},{5... | collective-permute-start | bytes 3145736 | tf_op jit(solution)/shard_map/ppermute | solution.py:81
  89.4 0.8 copy-done
  90.2 3.2 %project_out.4 = (f32[256,512]{1,0:T(8,128)}, bf16[256,512]{1,0:T(8,128)(2,1)}) custom-call(s32[3]{0:T(128)} %pad_add_fusion.place_ref, bf16[2,256,512]{2,1,0:T(8,128)(2,1)} %attend_last_2.1.mine_ref, bf16[2,256,512]{2,1,0:T(8,128)(2,1)} %copy-done, bf16[512,1024]{1,0:T(8,128)(2,1)} %weight_ref.1), custom_call_target="tpu_custom_call" | custom-call | flops 536870912 | bytes 1048576 | tf_op jit(solution)/shard_map/project_out/pallas_call | solution.py:309
  93.3 1.2 collective-permute-start.18
  94.5 3.2 %project_out.5 = (f32[256,512]{1,0:T(8,128)}, bf16[256,512]{1,0:T(8,128)(2,1)}) custom-call(s32[3]{0:T(128)} %pad_add_fusion.place_ref, bf16[2,256,512]{2,1,0:T(8,128)(2,1)} %attend_last_2.1.mine_ref, bf16[2,256,512]{2,1,0:T(8,128)(2,1)} %copy-done, bf16[512,1024]{1,0:T(8,128)(2,1)} %copy-done.8), custom_call_target="tpu_custom_call" | custom-call | flops 536870912 | bytes 1048576 | tf_op jit(solution)/shard_map/project_out/pallas_call | solution.py:309
  97.7 0.9 collective-permute-start.19
  98.6 1.4 %collective-permute-done.16.weight_ref = bf16[512,1024]{1,0:T(8,128)(2,1)} collective-permute-done((bf16[512,1024]{1,0:T(8,128)(2,1)S(1)}, bf16[512,1024]{1,0:T(8,128)(2,1)}, u32[]{:S(2)}, u32[]{:S(2)}) %collective-permute-start.16) | collective-permute-done | bytes 1048608 | tf_op jit(solution)/shard_map/ppermute | solution.py:81
  100.0 3.1 %project_out.6 = (f32[256,512]{1,0:T(8,128)}, bf16[256,512]{1,0:T(8,128)(2,1)}) custom-call(s32[3]{0:T(128)} %pad_add_fusion.place_ref, bf16[2,256,512]{2,1,0:T(8,128)(2,1)} %attend_last_2.1.mine_ref, bf16[2,256,512]{2,1,0:T(8,128)(2,1)} %copy-done, bf16[512,1024]{1,0:T(8,128)(2,1)} %collective-permute-done.16.weight_ref), custom_call_target="tpu_custom_call" | custom-call | flops 536870912 | bytes 1048576 | tf_op jit(solution)/shard_map/project_out/pallas_call | solution.py:309
  103.1 1.4 collective-permute-start.23
  104.6 3.8 %collective-permute-done.19.refs_4_ = bf16[256,512]{1,0:T(8,128)(2,1)S(1)} collective-permute-done((bf16[256,512]{1,0:T(8,128)(2,1)}, bf16[256,512]{1,0:T(8,128)(2,1)S(1)}, u32[]{:S(2)}, u32[]{:S(2)}) %collective-permute-start.19) | collective-permute-done | bytes 262176 | tf_op jit(solution)/shard_map/ppermute | solution.py:89
  108.4 2.4 %collective-permute-start.21 = (bf16[128,512]{1,0:T(8,128)(2,1)S(1)}, bf16[128,512]{1,0:T(8,128)(2,1)S(1)}, u32[]{:S(2)}, u32[]{:S(2)}) collective-permute-start(bf16[128,512]{1,0:T(8,128)(2,1)S(1)} %add_convert_fusion), channel_id=1, source_target_pairs={{0,2},{1,3},{2,0},{3,1},{4,6},{5,7},{6,4},{7,5},{8,10},{9,11},{10,... | collective-permute-start | bytes 393224 | tf_op jit(solution)/shard_map/ppermute | solution.py:89
  111.4 3.2 %project_out.7 = (f32[256,512]{1,0:T(8,128)}, bf16[256,512]{1,0:T(8,128)(2,1)}) custom-call(s32[3]{0:T(128)} %pad_add_fusion.place_ref, bf16[2,256,512]{2,1,0:T(8,128)(2,1)} %attend_last_2.1.mine_ref, bf16[2,256,512]{2,1,0:T(8,128)(2,1)} %copy-done, bf16[512,1024]{1,0:T(8,128)(2,1)} %collective-permute-done.17.weight_ref), custom_call_target="tpu_custom_call" | custom-call | flops 536870912 | bytes 1048576 | tf_op jit(solution)/shard_map/project_out/pallas_call | solution.py:309
  114.6 1.3 collective-permute-start.27
  115.9 1.0 collective-permute-done.23
  117.0 1.6 %collective-permute-start.24 = (bf16[128,512]{1,0:T(8,128)(2,1)S(1)}, bf16[128,512]{1,0:T(8,128)(2,1)S(1)}, u32[]{:S(2)}, u32[]{:S(2)}) collective-permute-start(bf16[128,512]{1,0:T(8,128)(2,1)S(1)} %split.37), channel_id=1, source_target_pairs={{0,2},{1,3},{2,0},{3,1},{4,6},{5,7},{6,4},{7,5},{8,10},{9,11},{10,... | collective-permute-start | bytes 393224 | tf_op jit(solution)/shard_map/ppermute | solution.py:89
  118.6 0.7 fusion.2
  119.6 3.8 %collective-permute-done.20.refs_2_ = bf16[128,512]{1,0:T(8,128)(2,1)S(1)} collective-permute-done((bf16[128,512]{1,0:T(8,128)(2,1)S(1)}, bf16[128,512]{1,0:T(8,128)(2,1)S(1)}, u32[]{:S(2)}, u32[]{:S(2)}) %collective-permute-start.20) | collective-permute-done | bytes 131104 | tf_op jit(solution)/shard_map/ppermute | solution.py:89
  123.4 0.7 copy-done.24
  124.0 2.0 %add_up.1 = (bf16[64,1024]{1,0:T(8,128)(2,1)}, bf16[64,1024]{1,0:T(8,128)(2,1)}) custom-call(f32[256,512]{1,0:T(8,128)} %get-tuple-element.71.refs_0_, bf16[256,512]{1,0:T(8,128)(2,1)} %copy-done.9, bf16[128,512]{1,0:T(8,128)(2,1)} %copy-done.24, f32[256,512]{1,0:T(8,128)} %get-tuple-element.61.refs_3_, bf16[256,512]{1,0:T(8,128)(2,1)} %copy-done.10, ...), custom_call_target="tpu_custom_call" | custom-call | flops 262144 | bytes 1310720 | tf_op jit(solution)/shard_map/add_up/pallas_call | solution.py:349
  126.0 0.9 collective-permute-done.27
  127.0 3.3 %collective-permute-start.28 = (bf16[128,512]{1,0:T(8,128)(2,1)S(1)}, bf16[128,512]{1,0:T(8,128)(2,1)S(1)}, u32[]{:S(2)}, u32[]{:S(2)}) collective-permute-start(bf16[128,512]{1,0:T(8,128)(2,1)S(1)} %split.36), channel_id=1, source_target_pairs={{0,2},{1,3},{2,0},{3,1},{4,6},{5,7},{6,4},{7,5},{8,10},{9,11},{10,... | collective-permute-start | bytes 393224 | tf_op jit(solution)/shard_map/ppermute | solution.py:89
  130.3 0.7 fusion.1
  131.6 4.8 %collective-permute-done.28.refs_7_ = bf16[128,512]{1,0:T(8,128)(2,1)S(1)} collective-permute-done((bf16[128,512]{1,0:T(8,128)(2,1)S(1)}, bf16[128,512]{1,0:T(8,128)(2,1)S(1)}, u32[]{:S(2)}, u32[]{:S(2)}) %collective-permute-start.28) | collective-permute-done | bytes 131104 | tf_op jit(solution)/shard_map/ppermute | solution.py:89
  136.6 1.2 collective-permute-done.30.refs_9_
  138.4 2.2 %put_in_place.1 = bf16[64,4096]{1,0:T(8,128)(2,1)} custom-call(s32[3]{0:T(128)} %pad_add_fusion.place_ref, bf16[64,1024]{1,0:T(8,128)(2,1)} %get-tuple-element.73.refs_0_, bf16[64,1024]{1,0:T(8,128)(2,1)} %copy-done.26, f32[64,512]{1,0:T(8,128)} %get-tuple-element.84.refs_2_, bf16[128,512]{1,0:T(8,128)(2,1)} %copy-done.21, f32[64,512]{1,0:T(8,128)} %copy-done.25, ...), custom_call_target="tpu_custom_call" | custom-call | bytes 1048576 | tf_op jit(solution)/shard_map/put_in_place/pallas_call | solution.py:385
  (101 shorter events, 5.2 us)
Async XLA Ops:
  0.0 1.5 %copy-start.20 = (bf16[256,1024]{1,0:T(8,128)(2,1)S(1)}, bf16[256,1024]{1,0:T(8,128)(2,1)}, u32[]{:S(2)}) copy-start(bf16[256,1024]{1,0:T(8,128)(2,1)} %param.8) | copy-start | bytes 1572868
  1.7 4.0 %collective-permute-start.7 = (bf16[1024,512]{1,0:T(8,128)(2,1)S(1)}, bf16[1024,512]{1,0:T(8,128)(2,1)S(1)}, u32[]{:S(2)}, u32[]{:S(2)}) collective-permute-start(bf16[1024,512]{1,0:T(8,128)(2,1)S(1)} %pad_maximum_fusion), channel_id=1, source_target_pairs={{0,4},{4,0},{8,12},{12,8},{16,20},{20,16},{24,28},{28,24},{1,5},{5... | collective-permute-start | bytes 3145736 | tf_op jit(solution)/shard_map/ppermute | solution.py:77
  2.7 22.5 %collective-permute-start = (bf16[256,1024]{1,0:T(8,128)(2,1)S(1)}, bf16[256,1024]{1,0:T(8,128)(2,1)S(1)}, u32[]{:S(2)}, u32[]{:S(2)}) collective-permute-start(bf16[256,1024]{1,0:T(8,128)(2,1)S(1)} %copy-done.11), channel_id=1, source_target_pairs={{0,1},{1,0},{2,3},{3,2},{4,5},{5,4},{6,7},{7,6},{8,9},{9,8},{10,11... | collective-permute-start | bytes 1572872 | tf_op jit(solution)/shard_map/ppermute | solution.py:89
  5.7 19.4 %collective-permute-start.3 = (bf16[256,1024]{1,0:T(8,128)(2,1)S(1)}, bf16[256,1024]{1,0:T(8,128)(2,1)S(1)}, u32[]{:S(2)}, u32[]{:S(2)}) collective-permute-start(bf16[256,1024]{1,0:T(8,128)(2,1)S(1)} %copy-done.11), channel_id=1, source_target_pairs={{0,4},{4,0},{8,12},{12,8},{16,20},{20,16},{24,28},{28,24},{1,5},{5... | collective-permute-start | bytes 1572872 | tf_op jit(solution)/shard_map/ppermute | solution.py:77
  5.8 20.7 %copy-start.1 = (bf16[1024,512]{1,0:T(8,128)(2,1)}, bf16[1024,512]{1,0:T(8,128)(2,1)S(1)}, u32[]{:S(2)}) copy-start(bf16[1024,512]{1,0:T(8,128)(2,1)S(1)} %pad_maximum_fusion.1.refs_8_) | copy-start | bytes 3145732
  5.8 29.7 %collective-permute-start.8 = (bf16[1024,512]{1,0:T(8,128)(2,1)S(1)}, bf16[1024,512]{1,0:T(8,128)(2,1)S(1)}, u32[]{:S(2)}, u32[]{:S(2)}) collective-permute-start(bf16[1024,512]{1,0:T(8,128)(2,1)S(1)} %pad_maximum_fusion.1.refs_8_), channel_id=1, source_target_pairs={{0,8},{4,20},{8,0},{12,28},{16,24},{20,4},{24,16},{28,12},{1,9},{5... | collective-permute-start | bytes 3145736 | tf_op jit(solution)/shard_map/ppermute | solution.py:81
  7.6 27.9 %collective-permute-start.9 = (bf16[1024,512]{1,0:T(8,128)(2,1)S(1)}, bf16[1024,512]{1,0:T(8,128)(2,1)S(1)}, u32[]{:S(2)}, u32[]{:S(2)}) collective-permute-start(bf16[1024,512]{1,0:T(8,128)(2,1)S(1)} %pad_maximum_fusion.1.refs_8_), channel_id=1, source_target_pairs={{0,16},{4,12},{8,24},{12,4},{16,0},{20,28},{24,8},{28,20},{1,17},{... | collective-permute-start | bytes 3145736 | tf_op jit(solution)/shard_map/ppermute | solution.py:85
  9.1 25.8 %collective-permute-start.1 = (bf16[256,1024]{1,0:T(8,128)(2,1)S(1)}, bf16[256,1024]{1,0:T(8,128)(2,1)S(1)}, u32[]{:S(2)}, u32[]{:S(2)}) collective-permute-start(bf16[256,1024]{1,0:T(8,128)(2,1)S(1)} %copy-done.11), channel_id=1, source_target_pairs={{0,2},{1,3},{2,0},{3,1},{4,6},{5,7},{6,4},{7,5},{8,10},{9,11},{10,... | collective-permute-start | bytes 1572872 | tf_op jit(solution)/shard_map/ppermute | solution.py:89
  25.1 1.4 copy-start.12
  25.1 1.4 copy-start.13
  25.1 10.3 %collective-permute-start.4 = (bf16[256,1024]{1,0:T(8,128)(2,1)S(1)}, bf16[256,1024]{1,0:T(8,128)(2,1)S(1)}, u32[]{:S(2)}, u32[]{:S(2)}) collective-permute-start(bf16[256,1024]{1,0:T(8,128)(2,1)S(1)} %collective-permute-done.refs_1_), channel_id=1, source_target_pairs={{0,4},{4,0},{8,12},{12,8},{16,20},{20,16},{24,28},{28,24},{1,5},{5... | collective-permute-start | bytes 1572872 | tf_op jit(solution)/shard_map/ppermute | solution.py:77
  26.5 22.5 %collective-permute-start.12 = (bf16[512,1024]{1,0:T(8,128)(2,1)}, bf16[512,1024]{1,0:T(8,128)(2,1)}, u32[]{:S(2)}, u32[]{:S(2)}) collective-permute-start(bf16[512,1024]{1,0:T(8,128)(2,1)} %maximum_maximum_fusion.refs_2_.refs_4_), channel_id=1, source_target_pairs={{0,8},{4,20},{8,0},{12,28},{16,24},{20,4},{24,16},{28,12},{1,9},{5... | collective-permute-start | bytes 3145736 | tf_op jit(solution)/shard_map/ppermute | solution.py:81
  34.9 12.9 %collective-permute-start.2 = (bf16[256,1024]{1,0:T(8,128)(2,1)S(1)}, bf16[256,1024]{1,0:T(8,128)(2,1)}, u32[]{:S(2)}, u32[]{:S(2)}) collective-permute-start(bf16[256,1024]{1,0:T(8,128)(2,1)S(1)} %collective-permute-done.1.refs_2_), channel_id=1, source_target_pairs={{0,1},{1,0},{2,3},{3,2},{4,5},{5,4},{6,7},{7,6},{8,9},{9,8},{10,11... | collective-permute-start | bytes 1572872 | tf_op jit(solution)/shard_map/ppermute | solution.py:89
  35.5 12.3 %copy-start.15 = (bf16[256,1024]{1,0:T(8,128)(2,1)}, bf16[256,1024]{1,0:T(8,128)(2,1)S(1)}, u32[]{:S(2)}) copy-start(bf16[256,1024]{1,0:T(8,128)(2,1)S(1)} %collective-permute-done.4.refs_5_) | copy-start | bytes 1572868
  35.5 12.2 %collective-permute-start.5 = (bf16[256,1024]{1,0:T(8,128)(2,1)S(1)}, bf16[256,1024]{1,0:T(8,128)(2,1)S(1)}, u32[]{:S(2)}, u32[]{:S(2)}) collective-permute-start(bf16[256,1024]{1,0:T(8,128)(2,1)S(1)} %collective-permute-done.1.refs_2_), channel_id=1, source_target_pairs={{0,4},{4,0},{8,12},{12,8},{16,20},{20,16},{24,28},{28,24},{1,5},{5... | collective-permute-start | bytes 1572872 | tf_op jit(solution)/shard_map/ppermute | solution.py:77
  35.5 18.4 %copy-start.4 = (bf16[1024,512]{1,0:T(8,128)(2,1)}, bf16[1024,512]{1,0:T(8,128)(2,1)S(1)}, u32[]{:S(2)}) copy-start(bf16[1024,512]{1,0:T(8,128)(2,1)S(1)} %collective-permute-done.8.refs_9_) | copy-start | bytes 3145732
  35.6 18.3 %copy-start.5 = (bf16[1024,512]{1,0:T(8,128)(2,1)}, bf16[1024,512]{1,0:T(8,128)(2,1)S(1)}, u32[]{:S(2)}) copy-start(bf16[1024,512]{1,0:T(8,128)(2,1)S(1)} %collective-permute-done.9.refs_10_) | copy-start | bytes 3145732
  35.7 18.3 %collective-permute-start.10 = (bf16[1024,512]{1,0:T(8,128)(2,1)S(1)}, bf16[1024,512]{1,0:T(8,128)(2,1)S(1)}, u32[]{:S(2)}, u32[]{:S(2)}) collective-permute-start(bf16[1024,512]{1,0:T(8,128)(2,1)S(1)} %collective-permute-done.8.refs_9_), channel_id=1, source_target_pairs={{0,16},{4,12},{8,24},{12,4},{16,0},{20,28},{24,8},{28,20},{1,17},{... | collective-permute-start | bytes 3145736 | tf_op jit(solution)/shard_map/ppermute | solution.py:85
  47.7 4.2 %collective-permute-start.6 = (bf16[256,1024]{1,0:T(8,128)(2,1)}, bf16[256,1024]{1,0:T(8,128)(2,1)}, u32[]{:S(2)}, u32[]{:S(2)}) collective-permute-start(bf16[256,1024]{1,0:T(8,128)(2,1)} %collective-permute-done.2.refs_3_), channel_id=1, source_target_pairs={{0,4},{4,0},{8,12},{12,8},{16,20},{20,16},{24,28},{28,24},{1,5},{5... | collective-permute-start | bytes 1572872 | tf_op jit(solution)/shard_map/ppermute | solution.py:77
  48.5 22.9 %collective-permute-start.11 = (bf16[512,1024]{1,0:T(8,128)(2,1)}, bf16[512,1024]{1,0:T(8,128)(2,1)}, u32[]{:S(2)}, u32[]{:S(2)}) collective-permute-start(bf16[512,1024]{1,0:T(8,128)(2,1)} %maximum_maximum_fusion.refs_2_.refs_4_), channel_id=1, source_target_pairs={{0,16},{4,12},{8,24},{12,4},{16,0},{20,28},{24,8},{28,20},{1,17},{... | collective-permute-start | bytes 3145736 | tf_op jit(solution)/shard_map/ppermute | solution.py:85
  49.0 27.5 %collective-permute-start.13 = (bf16[512,1024]{1,0:T(8,128)(2,1)}, bf16[512,1024]{1,0:T(8,128)(2,1)}, u32[]{:S(2)}, u32[]{:S(2)}) collective-permute-start(bf16[512,1024]{1,0:T(8,128)(2,1)} %collective-permute-done.12.refs_3_.refs_5_), channel_id=1, source_target_pairs={{0,16},{4,12},{8,24},{12,4},{16,0},{20,28},{24,8},{28,20},{1,17},{... | collective-permute-start | bytes 3145736 | tf_op jit(solution)/shard_map/ppermute | solution.py:85
  60.7 8.3 %copy-start.7 = (bf16[512,1024]{1,0:T(8,128)(2,1)S(1)}, bf16[512,1024]{1,0:T(8,128)(2,1)}, u32[]{:S(2)}) copy-start(bf16[512,1024]{1,0:T(8,128)(2,1)} %weight_ref.1) | copy-start | bytes 3145732
  69.0 18.7 %collective-permute-start.15 = (bf16[512,1024]{1,0:T(8,128)(2,1)S(1)}, bf16[512,1024]{1,0:T(8,128)(2,1)S(1)}, u32[]{:S(2)}, u32[]{:S(2)}) collective-permute-start(bf16[512,1024]{1,0:T(8,128)(2,1)S(1)} %copy-done.7), channel_id=1, source_target_pairs={{0,16},{4,12},{8,24},{12,4},{16,0},{20,28},{24,8},{28,20},{1,17},{... | collective-permute-start | bytes 3145736 | tf_op jit(solution)/shard_map/ppermute | solution.py:85
  85.0 15.0 %collective-permute-start.16 = (bf16[512,1024]{1,0:T(8,128)(2,1)S(1)}, bf16[512,1024]{1,0:T(8,128)(2,1)}, u32[]{:S(2)}, u32[]{:S(2)}) collective-permute-start(bf16[512,1024]{1,0:T(8,128)(2,1)S(1)} %copy-done.7), channel_id=1, source_target_pairs={{0,8},{4,20},{8,0},{12,28},{16,24},{20,4},{24,16},{28,12},{1,9},{5... | collective-permute-start | bytes 3145736 | tf_op jit(solution)/shard_map/ppermute | solution.py:81
  86.8 2.6 %collective-permute-start.14 = (bf16[2,256,512]{2,1,0:T(8,128)(2,1)}, bf16[2,256,512]{2,1,0:T(8,128)(2,1)S(1)}, u32[]{:S(2)}, u32[]{:S(2)}) collective-permute-start(bf16[2,256,512]{2,1,0:T(8,128)(2,1)} %attend_last_2.1.mine_ref), channel_id=1, source_target_pairs={{0,4},{4,0},{8,12},{12,8},{16,20},{20,16},{24,28},{28,24},{1,5},{5... | collective-permute-start | bytes 1572872 | tf_op jit(solution)/shard_map/ppermute | solution.py:77
  87.6 6.8 %copy-start.8 = (bf16[512,1024]{1,0:T(8,128)(2,1)}, bf16[512,1024]{1,0:T(8,128)(2,1)S(1)}, u32[]{:S(2)}) copy-start(bf16[512,1024]{1,0:T(8,128)(2,1)S(1)} %collective-permute-done.15.weight_ref) | copy-start | bytes 3145732
  87.6 23.7 %collective-permute-start.17 = (bf16[512,1024]{1,0:T(8,128)(2,1)S(1)}, bf16[512,1024]{1,0:T(8,128)(2,1)}, u32[]{:S(2)}, u32[]{:S(2)}) collective-permute-start(bf16[512,1024]{1,0:T(8,128)(2,1)S(1)} %collective-permute-done.15.weight_ref), channel_id=1, source_target_pairs={{0,8},{4,20},{8,0},{12,28},{16,24},{20,4},{24,16},{28,12},{1,9},{5... | collective-permute-start | bytes 3145736 | tf_op jit(solution)/shard_map/ppermute | solution.py:81
  93.3 11.2 %collective-permute-start.18 = (bf16[256,512]{1,0:T(8,128)(2,1)}, bf16[256,512]{1,0:T(8,128)(2,1)S(1)}, u32[]{:S(2)}, u32[]{:S(2)}) collective-permute-start(bf16[256,512]{1,0:T(8,128)(2,1)} %get-tuple-element.58), channel_id=1, source_target_pairs={{0,1},{1,0},{2,3},{3,2},{4,5},{5,4},{6,7},{7,6},{8,9},{9,8},{10,11... | collective-permute-start | bytes 786440 | tf_op jit(solution)/shard_map/ppermute | solution.py:89
  97.7 10.7 %collective-permute-start.19 = (bf16[256,512]{1,0:T(8,128)(2,1)}, bf16[256,512]{1,0:T(8,128)(2,1)S(1)}, u32[]{:S(2)}, u32[]{:S(2)}) collective-permute-start(bf16[256,512]{1,0:T(8,128)(2,1)} %get-tuple-element.62), channel_id=1, source_target_pairs={{0,1},{1,0},{2,3},{3,2},{4,5},{5,4},{6,7},{7,6},{8,9},{9,8},{10,11... | collective-permute-start | bytes 786440 | tf_op jit(solution)/shard_map/ppermute | solution.py:89
  98.5 6.0 %copy-start.2 = (f32[256,512]{1,0:T(8,128)S(1)}, f32[256,512]{1,0:T(8,128)}, u32[]{:S(2)}) copy-start(f32[256,512]{1,0:T(8,128)} %get-tuple-element.71.refs_0_) | copy-start | bytes 1572868
  98.6 9.8 %copy-start.3 = (f32[256,512]{1,0:T(8,128)S(1)}, f32[256,512]{1,0:T(8,128)}, u32[]{:S(2)}) copy-start(f32[256,512]{1,0:T(8,128)} %get-tuple-element.61.refs_3_) | copy-start | bytes 1572868
  103.1 13.8 %collective-permute-start.23 = (bf16[256,512]{1,0:T(8,128)(2,1)}, bf16[256,512]{1,0:T(8,128)(2,1)S(1)}, u32[]{:S(2)}, u32[]{:S(2)}) collective-permute-start(bf16[256,512]{1,0:T(8,128)(2,1)} %get-tuple-element.76), channel_id=1, source_target_pairs={{0,1},{1,0},{2,3},{3,2},{4,5},{5,4},{6,7},{7,6},{8,9},{9,8},{10,11... | collective-permute-start | bytes 786440 | tf_op jit(solution)/shard_map/ppermute | solution.py:89
  104.5 10.0 %copy-start.9 = (bf16[256,512]{1,0:T(8,128)(2,1)}, bf16[256,512]{1,0:T(8,128)(2,1)S(1)}, u32[]{:S(2)}) copy-start(bf16[256,512]{1,0:T(8,128)(2,1)S(1)} %collective-permute-done.18.refs_1_) | copy-start | bytes 786436
  108.3 6.2 %copy-start.10 = (bf16[256,512]{1,0:T(8,128)(2,1)}, bf16[256,512]{1,0:T(8,128)(2,1)S(1)}, u32[]{:S(2)}) copy-start(bf16[256,512]{1,0:T(8,128)(2,1)S(1)} %collective-permute-done.19.refs_4_) | copy-start | bytes 786436
  108.4 8.5 %copy-start.18 = (f32[256,512]{1,0:T(8,128)S(1)}, f32[256,512]{1,0:T(8,128)}, u32[]{:S(2)}) copy-start(f32[256,512]{1,0:T(8,128)} %get-tuple-element.75) | copy-start | bytes 1572868
  108.4 11.2 %collective-permute-start.21 = (bf16[128,512]{1,0:T(8,128)(2,1)S(1)}, bf16[128,512]{1,0:T(8,128)(2,1)S(1)}, u32[]{:S(2)}, u32[]{:S(2)}) collective-permute-start(bf16[128,512]{1,0:T(8,128)(2,1)S(1)} %add_convert_fusion), channel_id=1, source_target_pairs={{0,2},{1,3},{2,0},{3,1},{4,6},{5,7},{6,4},{7,5},{8,10},{9,11},{10,... | collective-permute-start | bytes 393224 | tf_op jit(solution)/shard_map/ppermute | solution.py:89
  110.8 12.6 %collective-permute-start.20 = (bf16[128,512]{1,0:T(8,128)(2,1)S(1)}, bf16[128,512]{1,0:T(8,128)(2,1)S(1)}, u32[]{:S(2)}, u32[]{:S(2)}) collective-permute-start(bf16[128,512]{1,0:T(8,128)(2,1)S(1)} %add_convert_fusion.1), channel_id=1, source_target_pairs={{0,2},{1,3},{2,0},{3,1},{4,6},{5,7},{6,4},{7,5},{8,10},{9,11},{10,... | collective-permute-start | bytes 393224 | tf_op jit(solution)/shard_map/ppermute | solution.py:89
  114.6 12.3 %collective-permute-start.27 = (bf16[256,512]{1,0:T(8,128)(2,1)}, bf16[256,512]{1,0:T(8,128)(2,1)S(1)}, u32[]{:S(2)}, u32[]{:S(2)}) collective-permute-start(bf16[256,512]{1,0:T(8,128)(2,1)} %get-tuple-element.69), channel_id=1, source_target_pairs={{0,1},{1,0},{2,3},{3,2},{4,5},{5,4},{6,7},{7,6},{8,9},{9,8},{10,11... | collective-permute-start | bytes 786440 | tf_op jit(solution)/shard_map/ppermute | solution.py:89
  117.0 14.0 %collective-permute-start.24 = (bf16[128,512]{1,0:T(8,128)(2,1)S(1)}, bf16[128,512]{1,0:T(8,128)(2,1)S(1)}, u32[]{:S(2)}, u32[]{:S(2)}) collective-permute-start(bf16[128,512]{1,0:T(8,128)(2,1)S(1)} %split.37), channel_id=1, source_target_pairs={{0,2},{1,3},{2,0},{3,1},{4,6},{5,7},{6,4},{7,5},{8,10},{9,11},{10,... | collective-permute-start | bytes 393224 | tf_op jit(solution)/shard_map/ppermute | solution.py:89
  119.3 7.6 %copy-start.17 = (f32[256,512]{1,0:T(8,128)S(1)}, f32[256,512]{1,0:T(8,128)}, u32[]{:S(2)}) copy-start(f32[256,512]{1,0:T(8,128)} %get-tuple-element.68) | copy-start | bytes 1572868
  119.3 17.2 %collective-permute-start.25 = (f32[64,512]{1,0:T(8,128)S(1)}, f32[64,512]{1,0:T(8,128)S(1)}, u32[]{:S(2)}, u32[]{:S(2)}) collective-permute-start(f32[64,512]{1,0:T(8,128)S(1)} %get-tuple-element.83), channel_id=1, source_target_pairs={{0,4},{4,0},{8,12},{12,8},{16,20},{20,16},{24,28},{28,24},{1,5},{5... | collective-permute-start | bytes 393224 | tf_op jit(solution)/shard_map/ppermute | solution.py:77
  119.6 3.8 %copy-start.23 = (bf16[128,512]{1,0:T(8,128)(2,1)}, bf16[128,512]{1,0:T(8,128)(2,1)S(1)}, u32[]{:S(2)}) copy-start(bf16[128,512]{1,0:T(8,128)(2,1)S(1)} %collective-permute-done.21.refs_5_) | copy-start | bytes 393220
  126.0 10.5 %collective-permute-start.22 = (bf16[64,1024]{1,0:T(8,128)(2,1)}, bf16[64,1024]{1,0:T(8,128)(2,1)S(1)}, u32[]{:S(2)}, u32[]{:S(2)}) collective-permute-start(bf16[64,1024]{1,0:T(8,128)(2,1)} %get-tuple-element.74), channel_id=1, source_target_pairs={{0,4},{4,0},{8,12},{12,8},{16,20},{20,16},{24,28},{28,24},{1,5},{5... | collective-permute-start | bytes 393224 | tf_op jit(solution)/shard_map/ppermute | solution.py:77
  127.0 9.4 %collective-permute-start.28 = (bf16[128,512]{1,0:T(8,128)(2,1)S(1)}, bf16[128,512]{1,0:T(8,128)(2,1)S(1)}, u32[]{:S(2)}, u32[]{:S(2)}) collective-permute-start(bf16[128,512]{1,0:T(8,128)(2,1)S(1)} %split.36), channel_id=1, source_target_pairs={{0,2},{1,3},{2,0},{3,1},{4,6},{5,7},{6,4},{7,5},{8,10},{9,11},{10,... | collective-permute-start | bytes 393224 | tf_op jit(solution)/shard_map/ppermute | solution.py:89
  131.0 5.6 %collective-permute-start.29 = (f32[64,512]{1,0:T(8,128)S(1)}, f32[64,512]{1,0:T(8,128)S(1)}, u32[]{:S(2)}, u32[]{:S(2)}) collective-permute-start(f32[64,512]{1,0:T(8,128)S(1)} %get-tuple-element.81), channel_id=1, source_target_pairs={{0,4},{4,0},{8,12},{12,8},{16,20},{20,16},{24,28},{28,24},{1,5},{5... | collective-permute-start | bytes 393224 | tf_op jit(solution)/shard_map/ppermute | solution.py:77
  131.0 6.8 %copy-start.21 = (bf16[128,512]{1,0:T(8,128)(2,1)}, bf16[128,512]{1,0:T(8,128)(2,1)S(1)}, u32[]{:S(2)}) copy-start(bf16[128,512]{1,0:T(8,128)(2,1)S(1)} %collective-permute-done.24.refs_3_) | copy-start | bytes 393220
  131.0 5.5 %collective-permute-start.26 = (bf16[64,512]{1,0:T(8,128)(2,1)S(1)}, bf16[64,512]{1,0:T(8,128)(2,1)S(1)}, u32[]{:S(2)}, u32[]{:S(2)}) collective-permute-start(bf16[64,512]{1,0:T(8,128)(2,1)S(1)} %slice.45), channel_id=1, source_target_pairs={{0,4},{4,0},{8,12},{12,8},{16,20},{20,16},{24,28},{28,24},{1,5},{5... | collective-permute-start | bytes 196616 | tf_op jit(solution)/shard_map/ppermute | solution.py:77
  136.4 1.3 collective-permute-start.30
  (13 other events, 13.4 us)

commit v5 on v4

--- a/solution.py
+++ b/solution.py
@@ -179,28 +179,23 @@
     )(place, *states, *[w[1] for w in weights])
 
 
-def pair_part(queries, keys, values):
-    rows = queries.shape[0]
-    first = lax.broadcasted_iota(jnp.int32, (rows, PAIR), 1) < HEAD_DIM
+def pair_part(queries, keys, values, tile=64):
+    keys, values = jnp.concatenate(keys, axis=0), jnp.concatenate(values, axis=0)
+    first = lax.broadcasted_iota(jnp.int32, (tile, PAIR), 1) < HEAD_DIM
     found = []
-    for head in range(2):
-        masked = jnp.where(first if head == 0 else jnp.logical_not(first), queries, 0)
-        scores = [
-            lax.dot_general(
-                masked, k, (((1,), (1,)), ((), ())), preferred_element_type=jnp.float32
-            )
-            for k in keys
-        ]
-        top = scores[0].max(axis=1, keepdims=True)
-        for s in scores[1:]:
-            top = jnp.maximum(top, s.max(axis=1, keepdims=True))
-        both = None
-        for s, v in zip(scores, values):
-            probability = jnp.exp(s - top).astype(jnp.bfloat16)
-            part = jnp.dot(probability, v, preferred_element_type=jnp.float32)
-            both = part if both is None else both + part
-        found.append((both[:, :PAIR], both[:, PAIR:], jnp.broadcast_to(top, (rows, PAIR))))
-    return [jnp.where(first, a, b) for a, b in zip(*found)]
+    for begin in range(0, queries.shape[0], tile):
+        rows = queries[begin : begin + tile]
+        masked = jnp.concatenate([jnp.where(first, rows, 0), jnp.where(first, 0, rows)], axis=0)
+        scores = lax.dot_general(
+            masked, keys, (((1,), (1,)), ((), ())), preferred_element_type=jnp.float32
+        )
+        top = scores.max(axis=1, keepdims=True)
+        probability = jnp.exp(scores - top).astype(jnp.bfloat16)
+        both = jnp.dot(probability, values, preferred_element_type=jnp.float32)
+        top = jnp.broadcast_to(top, (2 * tile, PAIR))
+        parts = both[:, :PAIR], both[:, PAIR:], top
+        found.append([jnp.where(first, a[:tile], a[tile:]) for a in parts])
+    return [jnp.concatenate(a, axis=0) for a in zip(*found)]
 
 
 def attend(query_blocks, pieces, before=None, last=True):

time: 141 us -> 140 us (level)
  no operation moved by 1% of the time
where the time goes in v5:
time: 140 us
  waiting for transfers between devices  56.2 us (40%)
  Pallas kernels  38.8 us (28%)
  starting transfers between devices  35 us (25%)
  local copies, waits for them, and re-layouts  7.55 us (5%)
  other arithmetic  2.19 us (2%)
    ppermute x11, waiting for transfers between devices, over_z(): return lax.ppermute(a, 'fsdp', [(z, z ^ step) for z in range(4)])  45.5 us
    ppermute x11, starting transfers between devices, over_z(): return lax.ppermute(a, 'fsdp', [(z, z ^ step) for z in range(4)])  18.4 us
    pallas_call x2, Pallas kernels, attend(): pl.pallas_call(kernel, grid=(steps,), out_shape=out_shape, in_specs=in_sp...  16.3 us
    pallas_call x4, Pallas kernels, project_out(): pl.pallas_call(kernel, grid=(tiles,), out_shape=[jax.ShapeDtypeStruct((he...  12.7 us
    ppermute x5, waiting for transfers between devices, cross_back(): return lax.ppermute(a, 'blk', CROSS_BACK)  8.38 us
    ppermute x4, starting transfers between devices, cross(): return lax.ppermute(a, 'blk', CROSS)  7.93 us
    ppermute x5, starting transfers between devices, cross_back(): return lax.ppermute(a, 'blk', CROSS_BACK)  7.29 us
    pallas_call x1, Pallas kernels, project_queries(): pl.pallas_call(kernel, out_shape=(shape, shape), in_specs=[smem_spec()] +...  5.65 us
  transfers between devices with their start and end apart: 31, of which 14 were waited for; matrix products, arithmetic and copies ran while one was open for 3% of the time, Pallas kernels for 26%

profile of v5, /device:TPU:0, one launch (start us, length us, event | category | flops | bytes accessed | tf_op | source)
XLA Modules:
  0.0 140.0 jit_solution(13650109904190964660)
XLA Ops:
  0.0 1.4 constant_dynamic-slice_fusion.5
  2.7 3.0 %collective-permute-start = (bf16[256,1024]{1,0:T(8,128)(2,1)S(1)}, bf16[256,1024]{1,0:T(8,128)(2,1)S(1)}, u32[]{:S(2)}, u32[]{:S(2)}) collective-permute-start(bf16[256,1024]{1,0:T(8,128)(2,1)S(1)} %copy-done.11), channel_id=1, source_target_pairs={{0,1},{1,0},{2,3},{3,2},{4,5},{5,4},{6,7},{7,6},{8,9},{9,8},{10,11... | collective-permute-start | bytes 1572872 | tf_op jit(solution)/shard_map/ppermute | solution.py:89
  5.8 1.7 %collective-permute-start.8 = (bf16[1024,512]{1,0:T(8,128)(2,1)S(1)}, bf16[1024,512]{1,0:T(8,128)(2,1)S(1)}, u32[]{:S(2)}, u32[]{:S(2)}) collective-permute-start(bf16[1024,512]{1,0:T(8,128)(2,1)S(1)} %pad_maximum_fusion.1.refs_8_), channel_id=1, source_target_pairs={{0,8},{4,20},{8,0},{12,28},{16,24},{20,4},{24,16},{28,12},{1,9},{5... | collective-permute-start | bytes 3145736 | tf_op jit(solution)/shard_map/ppermute | solution.py:81
  7.6 1.5 %collective-permute-start.9 = (bf16[1024,512]{1,0:T(8,128)(2,1)S(1)}, bf16[1024,512]{1,0:T(8,128)(2,1)S(1)}, u32[]{:S(2)}, u32[]{:S(2)}) collective-permute-start(bf16[1024,512]{1,0:T(8,128)(2,1)S(1)} %pad_maximum_fusion.1.refs_8_), channel_id=1, source_target_pairs={{0,16},{4,12},{8,24},{12,4},{16,0},{20,28},{24,8},{28,20},{1,17},{... | collective-permute-start | bytes 3145736 | tf_op jit(solution)/shard_map/ppermute | solution.py:85
  9.1 2.6 %collective-permute-start.1 = (bf16[256,1024]{1,0:T(8,128)(2,1)S(1)}, bf16[256,1024]{1,0:T(8,128)(2,1)S(1)}, u32[]{:S(2)}, u32[]{:S(2)}) collective-permute-start(bf16[256,1024]{1,0:T(8,128)(2,1)S(1)} %copy-done.11), channel_id=1, source_target_pairs={{0,2},{1,3},{2,0},{3,1},{4,6},{5,7},{6,4},{7,5},{8,10},{9,11},{10,... | collective-permute-start | bytes 1572872 | tf_op jit(solution)/shard_map/ppermute | solution.py:89
  11.7 13.4 %collective-permute-done.refs_1_ = bf16[256,1024]{1,0:T(8,128)(2,1)S(1)} collective-permute-done((bf16[256,1024]{1,0:T(8,128)(2,1)S(1)}, bf16[256,1024]{1,0:T(8,128)(2,1)S(1)}, u32[]{:S(2)}, u32[]{:S(2)}) %collective-permute-start) | collective-permute-done | bytes 524320 | tf_op jit(solution)/shard_map/ppermute | solution.py:89
  25.3 1.2 maximum_maximum_fusion.refs_2_.refs_4_
  26.5 2.7 %collective-permute-start.12 = (bf16[512,1024]{1,0:T(8,128)(2,1)}, bf16[512,1024]{1,0:T(8,128)(2,1)}, u32[]{:S(2)}, u32[]{:S(2)}) collective-permute-start(bf16[512,1024]{1,0:T(8,128)(2,1)} %maximum_maximum_fusion.refs_2_.refs_4_), channel_id=1, source_target_pairs={{0,8},{4,20},{8,0},{12,28},{16,24},{20,4},{24,16},{28,12},{1,9},{5... | collective-permute-start | bytes 3145736 | tf_op jit(solution)/shard_map/ppermute | solution.py:81
  29.2 5.7 %collective-permute-done.1.refs_2_ = bf16[256,1024]{1,0:T(8,128)(2,1)S(1)} collective-permute-done((bf16[256,1024]{1,0:T(8,128)(2,1)S(1)}, bf16[256,1024]{1,0:T(8,128)(2,1)S(1)}, u32[]{:S(2)}, u32[]{:S(2)}) %collective-permute-start.1) | collective-permute-done | bytes 524320 | tf_op jit(solution)/shard_map/ppermute | solution.py:89
  34.9 0.6 collective-permute-start.2
  36.2 11.6 %collective-permute-done.2.refs_3_ = bf16[256,1024]{1,0:T(8,128)(2,1)} collective-permute-done((bf16[256,1024]{1,0:T(8,128)(2,1)S(1)}, bf16[256,1024]{1,0:T(8,128)(2,1)}, u32[]{:S(2)}, u32[]{:S(2)}) %collective-permute-start.2) | collective-permute-done | bytes 524320 | tf_op jit(solution)/shard_map/ppermute | solution.py:89
  47.8 0.7 copy-done.16
  49.0 2.3 %collective-permute-start.13 = (bf16[512,1024]{1,0:T(8,128)(2,1)}, bf16[512,1024]{1,0:T(8,128)(2,1)}, u32[]{:S(2)}, u32[]{:S(2)}) collective-permute-start(bf16[512,1024]{1,0:T(8,128)(2,1)} %collective-permute-done.12.refs_3_.refs_5_), channel_id=1, source_target_pairs={{0,16},{4,12},{8,24},{12,4},{16,0},{20,28},{24,8},{28,20},{1,17},{... | collective-permute-start | bytes 3145736 | tf_op jit(solution)/shard_map/ppermute | solution.py:85
  51.3 0.6 pad_add_fusion.place_ref
  51.9 2.0 %collective-permute-done.10.refs_11_ = bf16[1024,512]{1,0:T(8,128)(2,1)S(1)} collective-permute-done((bf16[1024,512]{1,0:T(8,128)(2,1)S(1)}, bf16[1024,512]{1,0:T(8,128)(2,1)S(1)}, u32[]{:S(2)}, u32[]{:S(2)}) %collective-permute-start.10) | collective-permute-done | bytes 1048608 | tf_op jit(solution)/shard_map/ppermute | solution.py:85
  53.9 1.1 copy-done.6
  55.0 5.6 %project_queries.1 = (bf16[256,512]{1,0:T(8,128)(2,1)}, bf16[256,512]{1,0:T(8,128)(2,1)}) custom-call(s32[3]{0:T(128)} %pad_add_fusion.place_ref, bf16[256,1024]{1,0:T(8,128)(2,1)} %refs_0_.1, bf16[256,1024]{1,0:T(8,128)(2,1)} %copy-done.12, bf16[256,1024]{1,0:T(8,128)(2,1)} %copy-done.14, bf16[256,1024]{1,0:T(8,128)(2,1)} %collective-permute-done.2.refs_3_, ...), custom_call_target="tpu_custom_call" | custom-call | flops 2147483648 | bytes 8388608 | tf_op jit(solution)/shard_map/project_queries/pallas_call | solution.py:161
  60.7 8.1 %attend_first_2.1 = (f32[256,512]{1,0:T(8,128)}, f32[256,512]{1,0:T(8,128)}, f32[256,512]{1,0:T(8,128)}, f32[256,512]{1,0:T(8,128)}, f32[256,512]{1,0:T(8,128)}, /*index=5*/f32[256,512]{1,0:T(8,128)}) custom-call(bf16[256,512]{1,0:T(8,128)(2,1)} %get-tuple-element.49.refs_0_, bf16[256,512]{1,0:T(8,128)(2,1)} %get-tuple-element.50.refs_1_, ...), custom_call_target="tpu_custom_call" | custom-call | flops 4294967296 | bytes 4718592 | tf_op jit(solution)/shard_map/attend_first_2/pallas_call | solution.py:253
  68.8 2.5 %collective-permute-start.15 = (bf16[512,1024]{1,0:T(8,128)(2,1)S(1)}, bf16[512,1024]{1,0:T(8,128)(2,1)S(1)}, u32[]{:S(2)}, u32[]{:S(2)}) collective-permute-start(bf16[512,1024]{1,0:T(8,128)(2,1)S(1)} %copy-done.7), channel_id=1, source_target_pairs={{0,16},{4,12},{8,24},{12,4},{16,0},{20,28},{24,8},{28,20},{1,17},{... | collective-permute-start | bytes 3145736 | tf_op jit(solution)/shard_map/ppermute | solution.py:85
  71.2 5.3 %collective-permute-done.13.refs_3_.refs_5_ = bf16[512,1024]{1,0:T(8,128)(2,1)} collective-permute-done((bf16[512,1024]{1,0:T(8,128)(2,1)}, bf16[512,1024]{1,0:T(8,128)(2,1)}, u32[]{:S(2)}, u32[]{:S(2)}) %collective-permute-start.13) | collective-permute-done | bytes 1048608 | tf_op jit(solution)/shard_map/ppermute | solution.py:85
  76.5 8.2 %attend_last_2.1.mine_ref = bf16[2,256,512]{2,1,0:T(8,128)(2,1)} custom-call(bf16[256,512]{1,0:T(8,128)(2,1)} %get-tuple-element.49.refs_0_, bf16[256,512]{1,0:T(8,128)(2,1)} %get-tuple-element.50.refs_1_, bf16[512,1024]{1,0:T(8,128)(2,1)} %collective-permute-done.11.refs_2_.refs_4_, bf16[512,1024]{1,0:T(8,128)(2,1)} %collective-permute-done.13.refs_3_.refs_5_, ...), custom_call_target="tpu_custom_call" | custom-call | flops 4294967296 | bytes 7864320 | tf_op jit(solution)/shard_map/attend_last_2/pallas_call | solution.py:253
  84.7 1.8 %collective-permute-start.16 = (bf16[512,1024]{1,0:T(8,128)(2,1)S(1)}, bf16[512,1024]{1,0:T(8,128)(2,1)}, u32[]{:S(2)}, u32[]{:S(2)}) collective-permute-start(bf16[512,1024]{1,0:T(8,128)(2,1)S(1)} %copy-done.7), channel_id=1, source_target_pairs={{0,8},{4,20},{8,0},{12,28},{16,24},{20,4},{24,16},{28,12},{1,9},{5... | collective-permute-start | bytes 3145736 | tf_op jit(solution)/shard_map/ppermute | solution.py:81
  86.5 1.1 collective-permute-done.15.weight_ref
  87.6 1.7 %collective-permute-start.17 = (bf16[512,1024]{1,0:T(8,128)(2,1)S(1)}, bf16[512,1024]{1,0:T(8,128)(2,1)}, u32[]{:S(2)}, u32[]{:S(2)}) collective-permute-start(bf16[512,1024]{1,0:T(8,128)(2,1)S(1)} %collective-permute-done.15.weight_ref), channel_id=1, source_target_pairs={{0,8},{4,20},{8,0},{12,28},{16,24},{20,4},{24,16},{28,12},{1,9},{5... | collective-permute-start | bytes 3145736 | tf_op jit(solution)/shard_map/ppermute | solution.py:81
  89.4 0.8 copy-done
  90.2 3.2 %project_out.4 = (f32[256,512]{1,0:T(8,128)}, bf16[256,512]{1,0:T(8,128)(2,1)}) custom-call(s32[3]{0:T(128)} %pad_add_fusion.place_ref, bf16[2,256,512]{2,1,0:T(8,128)(2,1)} %attend_last_2.1.mine_ref, bf16[2,256,512]{2,1,0:T(8,128)(2,1)} %copy-done, bf16[512,1024]{1,0:T(8,128)(2,1)} %weight_ref.1), custom_call_target="tpu_custom_call" | custom-call | flops 536870912 | bytes 1048576 | tf_op jit(solution)/shard_map/project_out/pallas_call | solution.py:304
  93.3 1.2 collective-permute-start.18
  94.5 3.2 %project_out.5 = (f32[256,512]{1,0:T(8,128)}, bf16[256,512]{1,0:T(8,128)(2,1)}) custom-call(s32[3]{0:T(128)} %pad_add_fusion.place_ref, bf16[2,256,512]{2,1,0:T(8,128)(2,1)} %attend_last_2.1.mine_ref, bf16[2,256,512]{2,1,0:T(8,128)(2,1)} %copy-done, bf16[512,1024]{1,0:T(8,128)(2,1)} %copy-done.8), custom_call_target="tpu_custom_call" | custom-call | flops 536870912 | bytes 1048576 | tf_op jit(solution)/shard_map/project_out/pallas_call | solution.py:304
  97.7 0.9 collective-permute-start.19
  98.6 1.1 collective-permute-done.16.weight_ref
  99.7 3.1 %project_out.6 = (f32[256,512]{1,0:T(8,128)}, bf16[256,512]{1,0:T(8,128)(2,1)}) custom-call(s32[3]{0:T(128)} %pad_add_fusion.place_ref, bf16[2,256,512]{2,1,0:T(8,128)(2,1)} %attend_last_2.1.mine_ref, bf16[2,256,512]{2,1,0:T(8,128)(2,1)} %copy-done, bf16[512,1024]{1,0:T(8,128)(2,1)} %collective-permute-done.16.weight_ref), custom_call_target="tpu_custom_call" | custom-call | flops 536870912 | bytes 1048576 | tf_op jit(solution)/shard_map/project_out/pallas_call | solution.py:304
  102.8 1.5 %collective-permute-start.23 = (bf16[256,512]{1,0:T(8,128)(2,1)}, bf16[256,512]{1,0:T(8,128)(2,1)S(1)}, u32[]{:S(2)}, u32[]{:S(2)}) collective-permute-start(bf16[256,512]{1,0:T(8,128)(2,1)} %get-tuple-element.76), channel_id=1, source_target_pairs={{0,1},{1,0},{2,3},{3,2},{4,5},{5,4},{6,7},{7,6},{8,9},{9,8},{10,11... | collective-permute-start | bytes 786440 | tf_op jit(solution)/shard_map/ppermute | solution.py:89
  104.4 4.0 %collective-permute-done.19.refs_4_ = bf16[256,512]{1,0:T(8,128)(2,1)S(1)} collective-permute-done((bf16[256,512]{1,0:T(8,128)(2,1)}, bf16[256,512]{1,0:T(8,128)(2,1)S(1)}, u32[]{:S(2)}, u32[]{:S(2)}) %collective-permute-start.19) | collective-permute-done | bytes 262176 | tf_op jit(solution)/shard_map/ppermute | solution.py:89
  108.4 2.4 %collective-permute-start.21 = (bf16[128,512]{1,0:T(8,128)(2,1)S(1)}, bf16[128,512]{1,0:T(8,128)(2,1)S(1)}, u32[]{:S(2)}, u32[]{:S(2)}) collective-permute-start(bf16[128,512]{1,0:T(8,128)(2,1)S(1)} %add_convert_fusion), channel_id=1, source_target_pairs={{0,2},{1,3},{2,0},{3,1},{4,6},{5,7},{6,4},{7,5},{8,10},{9,11},{10,... | collective-permute-start | bytes 393224 | tf_op jit(solution)/shard_map/ppermute | solution.py:89
  111.4 3.2 %project_out.7 = (f32[256,512]{1,0:T(8,128)}, bf16[256,512]{1,0:T(8,128)(2,1)}) custom-call(s32[3]{0:T(128)} %pad_add_fusion.place_ref, bf16[2,256,512]{2,1,0:T(8,128)(2,1)} %attend_last_2.1.mine_ref, bf16[2,256,512]{2,1,0:T(8,128)(2,1)} %copy-done, bf16[512,1024]{1,0:T(8,128)(2,1)} %collective-permute-done.17.weight_ref), custom_call_target="tpu_custom_call" | custom-call | flops 536870912 | bytes 1048576 | tf_op jit(solution)/shard_map/project_out/pallas_call | solution.py:304
  114.6 1.2 collective-permute-start.27
  115.8 1.4 collective-permute-done.23
  117.2 1.3 collective-permute-start.24
  118.6 0.7 fusion.2
  119.6 3.8 %collective-permute-done.20.refs_2_ = bf16[128,512]{1,0:T(8,128)(2,1)S(1)} collective-permute-done((bf16[128,512]{1,0:T(8,128)(2,1)S(1)}, bf16[128,512]{1,0:T(8,128)(2,1)S(1)}, u32[]{:S(2)}, u32[]{:S(2)}) %collective-permute-start.20) | collective-permute-done | bytes 131104 | tf_op jit(solution)/shard_map/ppermute | solution.py:89
  123.4 0.7 copy-done.24
  124.0 2.0 %add_up.1 = (bf16[64,1024]{1,0:T(8,128)(2,1)}, bf16[64,1024]{1,0:T(8,128)(2,1)}) custom-call(f32[256,512]{1,0:T(8,128)} %get-tuple-element.71.refs_0_, bf16[256,512]{1,0:T(8,128)(2,1)} %copy-done.9, bf16[128,512]{1,0:T(8,128)(2,1)} %copy-done.24, f32[256,512]{1,0:T(8,128)} %get-tuple-element.61.refs_3_, bf16[256,512]{1,0:T(8,128)(2,1)} %copy-done.10, ...), custom_call_target="tpu_custom_call" | custom-call | flops 262144 | bytes 1310720 | tf_op jit(solution)/shard_map/add_up/pallas_call | solution.py:344
  126.0 0.8 collective-permute-done.27
  127.0 3.2 %collective-permute-start.28 = (bf16[128,512]{1,0:T(8,128)(2,1)S(1)}, bf16[128,512]{1,0:T(8,128)(2,1)S(1)}, u32[]{:S(2)}, u32[]{:S(2)}) collective-permute-start(bf16[128,512]{1,0:T(8,128)(2,1)S(1)} %split.36), channel_id=1, source_target_pairs={{0,2},{1,3},{2,0},{3,1},{4,6},{5,7},{6,4},{7,5},{8,10},{9,11},{10,... | collective-permute-start | bytes 393224 | tf_op jit(solution)/shard_map/ppermute | solution.py:89
  130.1 0.7 fusion.1
  131.4 4.5 %collective-permute-done.28.refs_7_ = bf16[128,512]{1,0:T(8,128)(2,1)S(1)} collective-permute-done((bf16[128,512]{1,0:T(8,128)(2,1)S(1)}, bf16[128,512]{1,0:T(8,128)(2,1)S(1)}, u32[]{:S(2)}, u32[]{:S(2)}) %collective-permute-start.28) | collective-permute-done | bytes 131104 | tf_op jit(solution)/shard_map/ppermute | solution.py:89
  136.1 1.2 collective-permute-done.30.refs_9_
  137.8 2.2 %put_in_place.1 = bf16[64,4096]{1,0:T(8,128)(2,1)} custom-call(s32[3]{0:T(128)} %pad_add_fusion.place_ref, bf16[64,1024]{1,0:T(8,128)(2,1)} %get-tuple-element.73.refs_0_, bf16[64,1024]{1,0:T(8,128)(2,1)} %copy-done.26, f32[64,512]{1,0:T(8,128)} %get-tuple-element.84.refs_2_, bf16[128,512]{1,0:T(8,128)(2,1)} %copy-done.21, f32[64,512]{1,0:T(8,128)} %copy-done.25, ...), custom_call_target="tpu_custom_call" | custom-call | bytes 1048576 | tf_op jit(solution)/shard_map/put_in_place/pallas_call | solution.py:380
  (101 shorter events, 5.3 us)
Async XLA Ops:
  0.0 1.5 %copy-start.20 = (bf16[256,1024]{1,0:T(8,128)(2,1)S(1)}, bf16[256,1024]{1,0:T(8,128)(2,1)}, u32[]{:S(2)}) copy-start(bf16[256,1024]{1,0:T(8,128)(2,1)} %param.8) | copy-start | bytes 1572868
  1.7 4.0 %collective-permute-start.7 = (bf16[1024,512]{1,0:T(8,128)(2,1)S(1)}, bf16[1024,512]{1,0:T(8,128)(2,1)S(1)}, u32[]{:S(2)}, u32[]{:S(2)}) collective-permute-start(bf16[1024,512]{1,0:T(8,128)(2,1)S(1)} %pad_maximum_fusion), channel_id=1, source_target_pairs={{0,4},{4,0},{8,12},{12,8},{16,20},{20,16},{24,28},{28,24},{1,5},{5... | collective-permute-start | bytes 3145736 | tf_op jit(solution)/shard_map/ppermute | solution.py:77
  2.7 22.5 %collective-permute-start = (bf16[256,1024]{1,0:T(8,128)(2,1)S(1)}, bf16[256,1024]{1,0:T(8,128)(2,1)S(1)}, u32[]{:S(2)}, u32[]{:S(2)}) collective-permute-start(bf16[256,1024]{1,0:T(8,128)(2,1)S(1)} %copy-done.11), channel_id=1, source_target_pairs={{0,1},{1,0},{2,3},{3,2},{4,5},{5,4},{6,7},{7,6},{8,9},{9,8},{10,11... | collective-permute-start | bytes 1572872 | tf_op jit(solution)/shard_map/ppermute | solution.py:89
  5.7 19.4 %collective-permute-start.3 = (bf16[256,1024]{1,0:T(8,128)(2,1)S(1)}, bf16[256,1024]{1,0:T(8,128)(2,1)S(1)}, u32[]{:S(2)}, u32[]{:S(2)}) collective-permute-start(bf16[256,1024]{1,0:T(8,128)(2,1)S(1)} %copy-done.11), channel_id=1, source_target_pairs={{0,4},{4,0},{8,12},{12,8},{16,20},{20,16},{24,28},{28,24},{1,5},{5... | collective-permute-start | bytes 1572872 | tf_op jit(solution)/shard_map/ppermute | solution.py:77
  5.8 20.7 %copy-start.1 = (bf16[1024,512]{1,0:T(8,128)(2,1)}, bf16[1024,512]{1,0:T(8,128)(2,1)S(1)}, u32[]{:S(2)}) copy-start(bf16[1024,512]{1,0:T(8,128)(2,1)S(1)} %pad_maximum_fusion.1.refs_8_) | copy-start | bytes 3145732
  5.8 29.7 %collective-permute-start.8 = (bf16[1024,512]{1,0:T(8,128)(2,1)S(1)}, bf16[1024,512]{1,0:T(8,128)(2,1)S(1)}, u32[]{:S(2)}, u32[]{:S(2)}) collective-permute-start(bf16[1024,512]{1,0:T(8,128)(2,1)S(1)} %pad_maximum_fusion.1.refs_8_), channel_id=1, source_target_pairs={{0,8},{4,20},{8,0},{12,28},{16,24},{20,4},{24,16},{28,12},{1,9},{5... | collective-permute-start | bytes 3145736 | tf_op jit(solution)/shard_map/ppermute | solution.py:81
  7.6 27.9 %collective-permute-start.9 = (bf16[1024,512]{1,0:T(8,128)(2,1)S(1)}, bf16[1024,512]{1,0:T(8,128)(2,1)S(1)}, u32[]{:S(2)}, u32[]{:S(2)}) collective-permute-start(bf16[1024,512]{1,0:T(8,128)(2,1)S(1)} %pad_maximum_fusion.1.refs_8_), channel_id=1, source_target_pairs={{0,16},{4,12},{8,24},{12,4},{16,0},{20,28},{24,8},{28,20},{1,17},{... | collective-permute-start | bytes 3145736 | tf_op jit(solution)/shard_map/ppermute | solution.py:85
  9.1 25.8 %collective-permute-start.1 = (bf16[256,1024]{1,0:T(8,128)(2,1)S(1)}, bf16[256,1024]{1,0:T(8,128)(2,1)S(1)}, u32[]{:S(2)}, u32[]{:S(2)}) collective-permute-start(bf16[256,1024]{1,0:T(8,128)(2,1)S(1)} %copy-done.11), channel_id=1, source_target_pairs={{0,2},{1,3},{2,0},{3,1},{4,6},{5,7},{6,4},{7,5},{8,10},{9,11},{10,... | collective-permute-start | bytes 1572872 | tf_op jit(solution)/shard_map/ppermute | solution.py:89
  25.1 1.4 copy-start.12
  25.1 1.4 copy-start.13
  25.1 10.3 %collective-permute-start.4 = (bf16[256,1024]{1,0:T(8,128)(2,1)S(1)}, bf16[256,1024]{1,0:T(8,128)(2,1)S(1)}, u32[]{:S(2)}, u32[]{:S(2)}) collective-permute-start(bf16[256,1024]{1,0:T(8,128)(2,1)S(1)} %collective-permute-done.refs_1_), channel_id=1, source_target_pairs={{0,4},{4,0},{8,12},{12,8},{16,20},{20,16},{24,28},{28,24},{1,5},{5... | collective-permute-start | bytes 1572872 | tf_op jit(solution)/shard_map/ppermute | solution.py:77
  26.5 22.5 %collective-permute-start.12 = (bf16[512,1024]{1,0:T(8,128)(2,1)}, bf16[512,1024]{1,0:T(8,128)(2,1)}, u32[]{:S(2)}, u32[]{:S(2)}) collective-permute-start(bf16[512,1024]{1,0:T(8,128)(2,1)} %maximum_maximum_fusion.refs_2_.refs_4_), channel_id=1, source_target_pairs={{0,8},{4,20},{8,0},{12,28},{16,24},{20,4},{24,16},{28,12},{1,9},{5... | collective-permute-start | bytes 3145736 | tf_op jit(solution)/shard_map/ppermute | solution.py:81
  34.9 12.9 %collective-permute-start.2 = (bf16[256,1024]{1,0:T(8,128)(2,1)S(1)}, bf16[256,1024]{1,0:T(8,128)(2,1)}, u32[]{:S(2)}, u32[]{:S(2)}) collective-permute-start(bf16[256,1024]{1,0:T(8,128)(2,1)S(1)} %collective-permute-done.1.refs_2_), channel_id=1, source_target_pairs={{0,1},{1,0},{2,3},{3,2},{4,5},{5,4},{6,7},{7,6},{8,9},{9,8},{10,11... | collective-permute-start | bytes 1572872 | tf_op jit(solution)/shard_map/ppermute | solution.py:89
  35.5 12.3 %copy-start.15 = (bf16[256,1024]{1,0:T(8,128)(2,1)}, bf16[256,1024]{1,0:T(8,128)(2,1)S(1)}, u32[]{:S(2)}) copy-start(bf16[256,1024]{1,0:T(8,128)(2,1)S(1)} %collective-permute-done.4.refs_5_) | copy-start | bytes 1572868
  35.5 12.2 %collective-permute-start.5 = (bf16[256,1024]{1,0:T(8,128)(2,1)S(1)}, bf16[256,1024]{1,0:T(8,128)(2,1)S(1)}, u32[]{:S(2)}, u32[]{:S(2)}) collective-permute-start(bf16[256,1024]{1,0:T(8,128)(2,1)S(1)} %collective-permute-done.1.refs_2_), channel_id=1, source_target_pairs={{0,4},{4,0},{8,12},{12,8},{16,20},{20,16},{24,28},{28,24},{1,5},{5... | collective-permute-start | bytes 1572872 | tf_op jit(solution)/shard_map/ppermute | solution.py:77
  35.5 18.4 %copy-start.4 = (bf16[1024,512]{1,0:T(8,128)(2,1)}, bf16[1024,512]{1,0:T(8,128)(2,1)S(1)}, u32[]{:S(2)}) copy-start(bf16[1024,512]{1,0:T(8,128)(2,1)S(1)} %collective-permute-done.8.refs_9_) | copy-start | bytes 3145732
  35.6 18.3 %copy-start.5 = (bf16[1024,512]{1,0:T(8,128)(2,1)}, bf16[1024,512]{1,0:T(8,128)(2,1)S(1)}, u32[]{:S(2)}) copy-start(bf16[1024,512]{1,0:T(8,128)(2,1)S(1)} %collective-permute-done.9.refs_10_) | copy-start | bytes 3145732
  35.7 18.3 %collective-permute-start.10 = (bf16[1024,512]{1,0:T(8,128)(2,1)S(1)}, bf16[1024,512]{1,0:T(8,128)(2,1)S(1)}, u32[]{:S(2)}, u32[]{:S(2)}) collective-permute-start(bf16[1024,512]{1,0:T(8,128)(2,1)S(1)} %collective-permute-done.8.refs_9_), channel_id=1, source_target_pairs={{0,16},{4,12},{8,24},{12,4},{16,0},{20,28},{24,8},{28,20},{1,17},{... | collective-permute-start | bytes 3145736 | tf_op jit(solution)/shard_map/ppermute | solution.py:85
  47.7 4.2 %collective-permute-start.6 = (bf16[256,1024]{1,0:T(8,128)(2,1)}, bf16[256,1024]{1,0:T(8,128)(2,1)}, u32[]{:S(2)}, u32[]{:S(2)}) collective-permute-start(bf16[256,1024]{1,0:T(8,128)(2,1)} %collective-permute-done.2.refs_3_), channel_id=1, source_target_pairs={{0,4},{4,0},{8,12},{12,8},{16,20},{20,16},{24,28},{28,24},{1,5},{5... | collective-permute-start | bytes 1572872 | tf_op jit(solution)/shard_map/ppermute | solution.py:77
  48.5 22.7 %collective-permute-start.11 = (bf16[512,1024]{1,0:T(8,128)(2,1)}, bf16[512,1024]{1,0:T(8,128)(2,1)}, u32[]{:S(2)}, u32[]{:S(2)}) collective-permute-start(bf16[512,1024]{1,0:T(8,128)(2,1)} %maximum_maximum_fusion.refs_2_.refs_4_), channel_id=1, source_target_pairs={{0,16},{4,12},{8,24},{12,4},{16,0},{20,28},{24,8},{28,20},{1,17},{... | collective-permute-start | bytes 3145736 | tf_op jit(solution)/shard_map/ppermute | solution.py:85
  49.0 27.5 %collective-permute-start.13 = (bf16[512,1024]{1,0:T(8,128)(2,1)}, bf16[512,1024]{1,0:T(8,128)(2,1)}, u32[]{:S(2)}, u32[]{:S(2)}) collective-permute-start(bf16[512,1024]{1,0:T(8,128)(2,1)} %collective-permute-done.12.refs_3_.refs_5_), channel_id=1, source_target_pairs={{0,16},{4,12},{8,24},{12,4},{16,0},{20,28},{24,8},{28,20},{1,17},{... | collective-permute-start | bytes 3145736 | tf_op jit(solution)/shard_map/ppermute | solution.py:85
  60.7 8.1 %copy-start.7 = (bf16[512,1024]{1,0:T(8,128)(2,1)S(1)}, bf16[512,1024]{1,0:T(8,128)(2,1)}, u32[]{:S(2)}) copy-start(bf16[512,1024]{1,0:T(8,128)(2,1)} %weight_ref.1) | copy-start | bytes 3145732
  68.8 18.9 %collective-permute-start.15 = (bf16[512,1024]{1,0:T(8,128)(2,1)S(1)}, bf16[512,1024]{1,0:T(8,128)(2,1)S(1)}, u32[]{:S(2)}, u32[]{:S(2)}) collective-permute-start(bf16[512,1024]{1,0:T(8,128)(2,1)S(1)} %copy-done.7), channel_id=1, source_target_pairs={{0,16},{4,12},{8,24},{12,4},{16,0},{20,28},{24,8},{28,20},{1,17},{... | collective-permute-start | bytes 3145736 | tf_op jit(solution)/shard_map/ppermute | solution.py:85
  84.7 15.0 %collective-permute-start.16 = (bf16[512,1024]{1,0:T(8,128)(2,1)S(1)}, bf16[512,1024]{1,0:T(8,128)(2,1)}, u32[]{:S(2)}, u32[]{:S(2)}) collective-permute-start(bf16[512,1024]{1,0:T(8,128)(2,1)S(1)} %copy-done.7), channel_id=1, source_target_pairs={{0,8},{4,20},{8,0},{12,28},{16,24},{20,4},{24,16},{28,12},{1,9},{5... | collective-permute-start | bytes 3145736 | tf_op jit(solution)/shard_map/ppermute | solution.py:81
  86.5 2.9 %collective-permute-start.14 = (bf16[2,256,512]{2,1,0:T(8,128)(2,1)}, bf16[2,256,512]{2,1,0:T(8,128)(2,1)S(1)}, u32[]{:S(2)}, u32[]{:S(2)}) collective-permute-start(bf16[2,256,512]{2,1,0:T(8,128)(2,1)} %attend_last_2.1.mine_ref), channel_id=1, source_target_pairs={{0,4},{4,0},{8,12},{12,8},{16,20},{20,16},{24,28},{28,24},{1,5},{5... | collective-permute-start | bytes 1572872 | tf_op jit(solution)/shard_map/ppermute | solution.py:77
  87.6 6.8 %copy-start.8 = (bf16[512,1024]{1,0:T(8,128)(2,1)}, bf16[512,1024]{1,0:T(8,128)(2,1)S(1)}, u32[]{:S(2)}) copy-start(bf16[512,1024]{1,0:T(8,128)(2,1)S(1)} %collective-permute-done.15.weight_ref) | copy-start | bytes 3145732
  87.6 23.7 %collective-permute-start.17 = (bf16[512,1024]{1,0:T(8,128)(2,1)S(1)}, bf16[512,1024]{1,0:T(8,128)(2,1)}, u32[]{:S(2)}, u32[]{:S(2)}) collective-permute-start(bf16[512,1024]{1,0:T(8,128)(2,1)S(1)} %collective-permute-done.15.weight_ref), channel_id=1, source_target_pairs={{0,8},{4,20},{8,0},{12,28},{16,24},{20,4},{24,16},{28,12},{1,9},{5... | collective-permute-start | bytes 3145736 | tf_op jit(solution)/shard_map/ppermute | solution.py:81
  93.3 11.0 %collective-permute-start.18 = (bf16[256,512]{1,0:T(8,128)(2,1)}, bf16[256,512]{1,0:T(8,128)(2,1)S(1)}, u32[]{:S(2)}, u32[]{:S(2)}) collective-permute-start(bf16[256,512]{1,0:T(8,128)(2,1)} %get-tuple-element.58), channel_id=1, source_target_pairs={{0,1},{1,0},{2,3},{3,2},{4,5},{5,4},{6,7},{7,6},{8,9},{9,8},{10,11... | collective-permute-start | bytes 786440 | tf_op jit(solution)/shard_map/ppermute | solution.py:89
  97.7 10.7 %collective-permute-start.19 = (bf16[256,512]{1,0:T(8,128)(2,1)}, bf16[256,512]{1,0:T(8,128)(2,1)S(1)}, u32[]{:S(2)}, u32[]{:S(2)}) collective-permute-start(bf16[256,512]{1,0:T(8,128)(2,1)} %get-tuple-element.62), channel_id=1, source_target_pairs={{0,1},{1,0},{2,3},{3,2},{4,5},{5,4},{6,7},{7,6},{8,9},{9,8},{10,11... | collective-permute-start | bytes 786440 | tf_op jit(solution)/shard_map/ppermute | solution.py:89
  98.5 5.8 %copy-start.2 = (f32[256,512]{1,0:T(8,128)S(1)}, f32[256,512]{1,0:T(8,128)}, u32[]{:S(2)}) copy-start(f32[256,512]{1,0:T(8,128)} %get-tuple-element.71.refs_0_) | copy-start | bytes 1572868
  98.6 9.8 %copy-start.3 = (f32[256,512]{1,0:T(8,128)S(1)}, f32[256,512]{1,0:T(8,128)}, u32[]{:S(2)}) copy-start(f32[256,512]{1,0:T(8,128)} %get-tuple-element.61.refs_3_) | copy-start | bytes 1572868
  102.8 14.3 %collective-permute-start.23 = (bf16[256,512]{1,0:T(8,128)(2,1)}, bf16[256,512]{1,0:T(8,128)(2,1)S(1)}, u32[]{:S(2)}, u32[]{:S(2)}) collective-permute-start(bf16[256,512]{1,0:T(8,128)(2,1)} %get-tuple-element.76), channel_id=1, source_target_pairs={{0,1},{1,0},{2,3},{3,2},{4,5},{5,4},{6,7},{7,6},{8,9},{9,8},{10,11... | collective-permute-start | bytes 786440 | tf_op jit(solution)/shard_map/ppermute | solution.py:89
  104.4 10.2 %copy-start.9 = (bf16[256,512]{1,0:T(8,128)(2,1)}, bf16[256,512]{1,0:T(8,128)(2,1)S(1)}, u32[]{:S(2)}) copy-start(bf16[256,512]{1,0:T(8,128)(2,1)S(1)} %collective-permute-done.18.refs_1_) | copy-start | bytes 786436
  108.3 6.2 %copy-start.10 = (bf16[256,512]{1,0:T(8,128)(2,1)}, bf16[256,512]{1,0:T(8,128)(2,1)S(1)}, u32[]{:S(2)}) copy-start(bf16[256,512]{1,0:T(8,128)(2,1)S(1)} %collective-permute-done.19.refs_4_) | copy-start | bytes 786436
  108.4 8.7 %copy-start.18 = (f32[256,512]{1,0:T(8,128)S(1)}, f32[256,512]{1,0:T(8,128)}, u32[]{:S(2)}) copy-start(f32[256,512]{1,0:T(8,128)} %get-tuple-element.75) | copy-start | bytes 1572868
  108.4 11.2 %collective-permute-start.21 = (bf16[128,512]{1,0:T(8,128)(2,1)S(1)}, bf16[128,512]{1,0:T(8,128)(2,1)S(1)}, u32[]{:S(2)}, u32[]{:S(2)}) collective-permute-start(bf16[128,512]{1,0:T(8,128)(2,1)S(1)} %add_convert_fusion), channel_id=1, source_target_pairs={{0,2},{1,3},{2,0},{3,1},{4,6},{5,7},{6,4},{7,5},{8,10},{9,11},{10,... | collective-permute-start | bytes 393224 | tf_op jit(solution)/shard_map/ppermute | solution.py:89
  110.8 12.6 %collective-permute-start.20 = (bf16[128,512]{1,0:T(8,128)(2,1)S(1)}, bf16[128,512]{1,0:T(8,128)(2,1)S(1)}, u32[]{:S(2)}, u32[]{:S(2)}) collective-permute-start(bf16[128,512]{1,0:T(8,128)(2,1)S(1)} %add_convert_fusion.1), channel_id=1, source_target_pairs={{0,2},{1,3},{2,0},{3,1},{4,6},{5,7},{6,4},{7,5},{8,10},{9,11},{10,... | collective-permute-start | bytes 393224 | tf_op jit(solution)/shard_map/ppermute | solution.py:89
  114.6 12.3 %collective-permute-start.27 = (bf16[256,512]{1,0:T(8,128)(2,1)}, bf16[256,512]{1,0:T(8,128)(2,1)S(1)}, u32[]{:S(2)}, u32[]{:S(2)}) collective-permute-start(bf16[256,512]{1,0:T(8,128)(2,1)} %get-tuple-element.69), channel_id=1, source_target_pairs={{0,1},{1,0},{2,3},{3,2},{4,5},{5,4},{6,7},{7,6},{8,9},{9,8},{10,11... | collective-permute-start | bytes 786440 | tf_op jit(solution)/shard_map/ppermute | solution.py:89
  117.2 13.6 %collective-permute-start.24 = (bf16[128,512]{1,0:T(8,128)(2,1)S(1)}, bf16[128,512]{1,0:T(8,128)(2,1)S(1)}, u32[]{:S(2)}, u32[]{:S(2)}) collective-permute-start(bf16[128,512]{1,0:T(8,128)(2,1)S(1)} %split.37), channel_id=1, source_target_pairs={{0,2},{1,3},{2,0},{3,1},{4,6},{5,7},{6,4},{7,5},{8,10},{9,11},{10,... | collective-permute-start | bytes 393224 | tf_op jit(solution)/shard_map/ppermute | solution.py:89
  119.2 7.6 %copy-start.17 = (f32[256,512]{1,0:T(8,128)S(1)}, f32[256,512]{1,0:T(8,128)}, u32[]{:S(2)}) copy-start(f32[256,512]{1,0:T(8,128)} %get-tuple-element.68) | copy-start | bytes 1572868
  119.2 16.7 %collective-permute-start.25 = (f32[64,512]{1,0:T(8,128)S(1)}, f32[64,512]{1,0:T(8,128)S(1)}, u32[]{:S(2)}, u32[]{:S(2)}) collective-permute-start(f32[64,512]{1,0:T(8,128)S(1)} %get-tuple-element.83), channel_id=1, source_target_pairs={{0,4},{4,0},{8,12},{12,8},{16,20},{20,16},{24,28},{28,24},{1,5},{5... | collective-permute-start | bytes 393224 | tf_op jit(solution)/shard_map/ppermute | solution.py:77
  119.6 3.8 %copy-start.23 = (bf16[128,512]{1,0:T(8,128)(2,1)}, bf16[128,512]{1,0:T(8,128)(2,1)S(1)}, u32[]{:S(2)}) copy-start(bf16[128,512]{1,0:T(8,128)(2,1)S(1)} %collective-permute-done.21.refs_5_) | copy-start | bytes 393220
  126.0 10.0 %collective-permute-start.22 = (bf16[64,1024]{1,0:T(8,128)(2,1)}, bf16[64,1024]{1,0:T(8,128)(2,1)S(1)}, u32[]{:S(2)}, u32[]{:S(2)}) collective-permute-start(bf16[64,1024]{1,0:T(8,128)(2,1)} %get-tuple-element.74), channel_id=1, source_target_pairs={{0,4},{4,0},{8,12},{12,8},{16,20},{20,16},{24,28},{28,24},{1,5},{5... | collective-permute-start | bytes 393224 | tf_op jit(solution)/shard_map/ppermute | solution.py:77
  127.0 8.9 %collective-permute-start.28 = (bf16[128,512]{1,0:T(8,128)(2,1)S(1)}, bf16[128,512]{1,0:T(8,128)(2,1)S(1)}, u32[]{:S(2)}, u32[]{:S(2)}) collective-permute-start(bf16[128,512]{1,0:T(8,128)(2,1)S(1)} %split.36), channel_id=1, source_target_pairs={{0,2},{1,3},{2,0},{3,1},{4,6},{5,7},{6,4},{7,5},{8,10},{9,11},{10,... | collective-permute-start | bytes 393224 | tf_op jit(solution)/shard_map/ppermute | solution.py:89
  130.8 5.2 %collective-permute-start.29 = (f32[64,512]{1,0:T(8,128)S(1)}, f32[64,512]{1,0:T(8,128)S(1)}, u32[]{:S(2)}, u32[]{:S(2)}) collective-permute-start(f32[64,512]{1,0:T(8,128)S(1)} %get-tuple-element.81), channel_id=1, source_target_pairs={{0,4},{4,0},{8,12},{12,8},{16,20},{20,16},{24,28},{28,24},{1,5},{5... | collective-permute-start | bytes 393224 | tf_op jit(solution)/shard_map/ppermute | solution.py:77
  130.8 6.4 %copy-start.21 = (bf16[128,512]{1,0:T(8,128)(2,1)}, bf16[128,512]{1,0:T(8,128)(2,1)S(1)}, u32[]{:S(2)}) copy-start(bf16[128,512]{1,0:T(8,128)(2,1)S(1)} %collective-permute-done.24.refs_3_) | copy-start | bytes 393220
  130.8 5.2 %collective-permute-start.26 = (bf16[64,512]{1,0:T(8,128)(2,1)S(1)}, bf16[64,512]{1,0:T(8,128)(2,1)S(1)}, u32[]{:S(2)}, u32[]{:S(2)}) collective-permute-start(bf16[64,512]{1,0:T(8,128)(2,1)S(1)} %slice.45), channel_id=1, source_target_pairs={{0,4},{4,0},{8,12},{12,8},{16,20},{20,16},{24,28},{28,24},{1,5},{5... | collective-permute-start | bytes 196616 | tf_op jit(solution)/shard_map/ppermute | solution.py:77
  135.9 1.3 collective-permute-start.30
  (13 other events, 13.4 us)
